TPU v7x, 32 devices: a whole 2x2x4 slice. The times are simulated.
32 devices in a mesh: grp: 2 (over y), exp: 4 (over z), dat: 2 (over x), mdl: 2 (over core).
Axes of the slice: x: 2, y: 2, z: 4, core: 2. Of those that a mesh axis runs over, the one named last changes fastest.
Arguments:
- tokens: bfloat16 [4096, 4096], P(('grp', 'exp', 'dat'), 'mdl'), parts along dimension 0, may hold values from -6 to 6
- cotangent: bfloat16 [4096, 4096], P(('grp', 'exp', 'dat'), 'mdl'), parts along dimension 0, may hold values from -6 to 6
- routes: int32 [4096, 2], P(('grp', 'exp', 'dat')), parts along dimension 0, may hold values from 0 to 3, all different within a row; in each aligned block of 256 rows (0 to 255, 256 to 511, ...) at most 256 rows name the same one
- doc_ids: int32 [16, 256], P(('grp', 'exp', 'dat')), parts along dimension 0, may hold values from 0 to 3, never falling along the last dimension, each value on 1 to 96 neighbouring positions
- gate_weight: bfloat16 [4, 4096, 768], P('exp', 'dat', 'mdl'), may hold values from -0.09375 to 0.09375
- up_weight: bfloat16 [4, 4096, 768], P('exp', 'dat', 'mdl'), may hold values from -0.09375 to 0.09375
- proj_in: bfloat16 [32, 768], P(None, 'mdl'), may hold values from -0.21875 to 0.21875
- proj_out: bfloat16 [32, 4096], P(None, 'mdl'), may hold values from -0.09375 to 0.09375
Outputs:
- grads: float32 [64, 4, 1024], P(('grp', 'exp', 'dat')), parts along dimension 0
There are 2 independent parts, one for each index of `grp`. A program takes and returns all parts, laid end to end along the dimension named above; an argument that names none is the same for every part. Nothing has to cross between parts.
Inputs may be any that keep to these rules, and one draw needn't show every extreme that they name: Each token names 2 different experts; among the tokens of one document shard (aligned blocks of 256 rows) no expert is named by more than 256 routes, and one expert is named by exactly 256. `doc_ids`: each row never falls and holds every document number; a document has at most 96 tokens, and one has exactly that many.
All inputs are finite; a program needn't handle non-finite values.
Results may differ from a plain program's by a relative error of at most 0.0029.
Values may be sent and summed in bfloat16 or wider, within the bound.
No kernel may reach another device: no remote copies, remote signals or barrier semaphores. Data moves between devices by JAX's collectives and lax.ppermute only.
A program may use at most 64 MiB of HBM per device.

v0:
```python
import jax
import jax.numpy as jnp
from jax import lax
from jax.sharding import PartitionSpec as P

DOCS_DEV = 4


def slot_tokens(routes, experts, capacity):
    pair_expert = routes.reshape(-1)
    pair_count = pair_expert.shape[0]
    topk_width = routes.shape[1]
    onehot = (pair_expert[:, None] == jnp.arange(experts, dtype=jnp.int32)[None, :]).astype(
        jnp.int32
    )
    before = jnp.cumsum(onehot, axis=0) - onehot
    position = jnp.sum(before * onehot, axis=1)
    target = pair_expert * capacity + position
    holder = jnp.full((experts * capacity,), routes.shape[0], jnp.int32)
    holder = holder.at[target].set(jnp.arange(pair_count, dtype=jnp.int32) // topk_width)
    return (onehot, target, holder)


def on_device(tokens, cotangent, routes, doc_ids, gate_weight, up_weight, proj_in, proj_out):
    experts = lax.axis_size("exp")
    tok_count, topk_width = routes.shape
    capacity = 2 * tok_count * topk_width // experts
    rank_width = proj_in.shape[0]
    grad_part = jnp.dot(cotangent, proj_out.T, preferred_element_type=jnp.float32)
    grad_codes = lax.psum(grad_part, "mdl")
    onehot, target, holder = slot_tokens(routes, experts, capacity)
    outgoing = jnp.take(tokens, holder, axis=0, mode="fill", fill_value=0)
    outgoing = outgoing.reshape(experts, capacity, tokens.shape[1])
    arrived = lax.all_to_all(outgoing, "exp", split_axis=0, concat_axis=0, tiled=True)
    arrived = lax.all_gather(arrived, "mdl", axis=2, tiled=True)
    arrived = arrived.reshape(experts * capacity, arrived.shape[2])
    gate_local = gate_weight[0]
    up_local = up_weight[0]
    gate_total = jnp.dot(
        arrived,
        lax.all_gather(gate_local, "dat", axis=0, tiled=True),
        preferred_element_type=jnp.float32,
    )
    up_total = jnp.dot(
        arrived,
        lax.all_gather(up_local, "dat", axis=0, tiled=True),
        preferred_element_type=jnp.float32,
    )
    hidden = (jax.nn.silu(gate_total) * up_total).astype(jnp.bfloat16)
    code_part = jnp.dot(hidden, proj_in.T, preferred_element_type=jnp.float32)
    code_send = lax.psum(code_part, "mdl")
    returned = lax.all_to_all(
        code_send.reshape(experts, capacity, rank_width),
        "exp",
        split_axis=0,
        concat_axis=0,
        tiled=True,
    )
    pair_codes = returned.reshape(experts * capacity, rank_width)[target]
    spread = onehot.astype(jnp.float32)[:, :, None] * pair_codes[:, None, :]
    spread = spread.reshape(tok_count, topk_width, experts * rank_width).sum(axis=1)
    docs_mask = (doc_ids[0][None, :] == jnp.arange(DOCS_DEV, dtype=jnp.int32)[:, None]).astype(
        jnp.float32
    )
    weighted = docs_mask[:, :, None] * grad_codes[None, :, :]
    blocks = jnp.einsum("dti,tf->dif", weighted, spread, precision=lax.Precision.HIGHEST)
    blocks = blocks.reshape(DOCS_DEV, rank_width, experts, rank_width).transpose(0, 2, 1, 3)
    return blocks.reshape(DOCS_DEV, experts, rank_width * rank_width)


def solution(mesh):
    placed = (
        P(("grp", "exp", "dat"), "mdl"),
        P(("grp", "exp", "dat"), "mdl"),
        P(("grp", "exp", "dat"), None),
        P(("grp", "exp", "dat"), None),
        P("exp", "dat", "mdl"),
        P("exp", "dat", "mdl"),
        P(None, "mdl"),
        P(None, "mdl"),
    )
    return jax.shard_map(
        on_device,
        mesh=mesh,
        in_specs=placed,
        out_specs=P(("grp", "exp", "dat"), None, None),
        check_vma=False,
    )
```

profile of v0, /device:TPU:0, one launch (start us, length us, event | category | flops | bytes accessed | tf_op | source)
XLA Modules:
  0.0 239.4 jit_solution(9699273386727716396)
XLA Ops:
  6.5 0.0 copy-start
  6.5 0.9 copy.23
  7.4 0.1 eq.56
  7.6 0.1 eq.52
  7.7 0.7 broadcast_multiply_fusion.1
  8.4 1.2 reduce-window.6
  9.6 0.2 slice_reduce_fusion
  9.9 0.2 reduce-window.9
  10.0 0.1 add_bitcast_fusion
  10.1 0.1 copy.25
  10.3 0.1 mul.62
  10.5 2.4 %scatter_custom_fusion = s32[1024]{0:T(1024)S(1)} fusion(s32[512]{0:T(512)S(1)} %bitcast.56, s32[512]{0:T(512)S(1)} %add_select_fusion, s32[]{:T(128)} %constant.37.clone.1), kind=kCustom, calls=%fused_computation.41 | custom fusion | bytes 4100 | tf_op jit(solution)/shard_map/scatter | solution.py:20
  13.0 0.0 copy-done
  13.0 6.0 %gather_fusion = bf16[1024,2048]{1,0:T(8,128)(2,1)} fusion(bf16[256,2048]{1,0:T(8,128)(2,1)S(1)} %copy-done, s32[1024]{0:T(1024)S(1)} %fusion.18), kind=kCustom, calls=%fused_computation | custom fusion | bytes 8392704 | tf_op jit(solution)/shard_map/jit(_take)/gather | solution.py:32
  19.0 4.5 %broadcast_select_fusion = bf16[4,256,2048]{2,1,0:T(8,128)(2,1)} fusion(bf16[4,256,2048]{2,1,0:T(8,128)(2,1)} %bitcast.50, pred[4,256]{1,0:T(4,128)(4,1)S(1)} %broadcast_in_dim.26), kind=kLoop, calls=%fused_computation.3 | loop fusion | flops 2097152 | bytes 8389632 | tf_op jit(solution)/shard_map/jit(_take)/select_n | solution.py:32
  23.5 6.3 %all-to-all-start = ((bf16[4,256,2048]{2,1,0:T(8,128)(2,1)}), bf16[4,256,2048]{2,1,0:T(8,128)(2,1)}, u32[]{:S(2)}, u32[]{:S(2)}) async-start(bf16[4,256,2048]{2,1,0:T(8,128)(2,1)} %broadcast_select_fusion), calls=%async_computation | async-start | bytes 8388608 | tf_op jit(solution)/shard_map/all_to_all | solution.py:34
  29.8 0.0 all-gather.8.cloned.1.call-start
  29.8 0.7 all-gather.8.cloned.1.call-update
  30.5 0.0 copy-start.1
  30.5 0.0 copy-start.2
  30.5 0.0 all-gather.6.cloned.1.call-start
  30.6 92.6 %all-to-all-done = bf16[4,256,2048]{2,1,0:T(8,128)(2,1)} async-done(((bf16[4,256,2048]{2,1,0:T(8,128)(2,1)}), bf16[4,256,2048]{2,1,0:T(8,128)(2,1)}, u32[]{:S(2)}, u32[]{:S(2)}) %all-to-all-start) | async-done | bytes 4194336 | tf_op jit(solution)/shard_map/all_to_all | solution.py:34
  123.2 0.0 all-gather.6.cloned.1.call-update
  123.2 0.0 all-gather.10.cloned.1.call-start
  123.3 0.7 all-gather.10.cloned.1.call-update
  124.0 0.0 all-reduce.2.cloned.1.call-start
  124.0 0.1 copy.24
  124.2 0.0 copy-done.1
  124.2 0.4 fusion.25
  124.6 0.0 all-gather.8.cloned.1.call-done
  124.6 17.8 %all-gather.6.cloned.1.call-done = bf16[4,256,4096]{2,1,0:T(8,128)(2,1)} async-done(((bf16[4,256,2048]{2,1,0:T(8,128)(2,1)}), bf16[4,256,4096]{2,1,0:T(8,128)(2,1)}) %all-gather.6.cloned.1.call-update) | async-done | bytes 8388624 | tf_op jit(solution)/shard_map/all_gather | solution.py:35
  142.5 10.0 %fusion.2 = f32[1024,384]{1,0:T(8,128)} fusion(bf16[1024,4096]{1,0:T(8,128)(2,1)} %bitcast.61, bf16[1,4096,384]{2,1,0:T(8,128)(2,1)} %all-gather.8.cloned.1.call-done), kind=kOutput, calls=%fused_computation.6 | convolution fusion | flops 3221225472 | bytes 13107200 | tf_op jit(solution)/shard_map/dot_general | solution.py:39
  152.5 37.7 %all-gather.10.cloned.1.call-done = bf16[1,4096,384]{2,1,0:T(8,128)(2,1)} async-done(((bf16[1,2048,384]{2,1,0:T(8,128)(2,1)}), bf16[1,4096,384]{2,1,0:T(8,128)(2,1)}) %all-gather.10.cloned.1.call-update) | async-done | bytes 3145744 | tf_op jit(solution)/shard_map/all_gather | solution.py:46
  190.2 8.4 %fusion.7 = f32[1024,32]{0,1:T(8,128)S(1)} fusion(bf16[32,384]{1,0:T(8,128)(2,1)S(1)} %copy-done.4, f32[1024,384]{1,0:T(8,128)} %fusion.2, bf16[1024,4096]{1,0:T(8,128)(2,1)} %bitcast.62, bf16[1,4096,384]{2,1,0:T(8,128)(2,1)} %all-gather.10.cloned.1.call-done), kind=kOutput, calls=%fused_computation.9 | convolution fusion | flops 3248750592 | bytes 13262848 | tf_op jit(solution)/shard_map/dot_general | solution.py:50
  198.5 0.7 copy.35
  199.2 0.0 all-reduce.2.cloned.1.call-update
  199.2 3.4 %psum.14 = f32[256,32]{0,1:T(8,128)S(1)} all-reduce(f32[256,32]{0,1:T(8,128)S(1)} %fusion.25), channel_id=1, replica_groups=mesh['grp'=2,'exp'=4,'dat'=2,'mdl'=2] {'mdl'}, use_global_device_ids=true, to_apply=%region_0.0 | all-reduce | flops 8192 | bytes 65536 | tf_op jit(solution)/shard_map/psum | solution.py:30
  202.7 14.6 %all-reduce.2.cloned.1.call-done = f32[4,256,32]{1,2,0:T(8,128)} async-done(((f32[4,256,32]{1,2,0:T(8,128)}), f32[4,256,32]{1,2,0:T(8,128)}) %all-reduce.2.cloned.1.call-update) | async-done | bytes 131088 | tf_op jit(solution)/shard_map/psum | solution.py:51
  217.3 4.9 %all-to-all-start.1 = ((f32[4,256,32]{1,2,0:T(8,128)}), f32[4,256,32]{1,2,0:T(8,128)S(1)}, u32[]{:S(2)}, u32[]{:S(2)}) async-start(f32[4,256,32]{1,2,0:T(8,128)} %all-reduce.2.cloned.1.call-done), calls=%async_computation.1 | async-start | bytes 262144 | tf_op jit(solution)/shard_map/all_to_all | solution.py:52
  222.2 6.4 %all-to-all-done.1 = f32[4,256,32]{1,2,0:T(8,128)S(1)} async-done(((f32[4,256,32]{1,2,0:T(8,128)}), f32[4,256,32]{1,2,0:T(8,128)S(1)}, u32[]{:S(2)}, u32[]{:S(2)}) %all-to-all-start.1) | async-done | bytes 131104 | tf_op jit(solution)/shard_map/all_to_all | solution.py:52
  228.5 0.2 copy.28
  228.7 1.0 gather_fusion.1
  229.8 0.7 broadcast_multiply_fusion
  230.5 0.7 mul.68
  231.2 0.3 reduce_sum.22
  231.5 0.1 copy.29
  231.6 0.5 convolution_bitcast_fusion
  232.1 0.8 reshape.128
  (15 shorter events, 0.1 us)
Async XLA Ops:
  6.5 6.4 %copy-start = (bf16[256,2048]{1,0:T(8,128)(2,1)S(1)}, bf16[256,2048]{1,0:T(8,128)(2,1)}, u32[]{:S(2)}) copy-start(bf16[256,2048]{1,0:T(8,128)(2,1)} %param.8) | copy-start | bytes 3145732
  23.5 99.7 %all-to-all-start = ((bf16[4,256,2048]{2,1,0:T(8,128)(2,1)}), bf16[4,256,2048]{2,1,0:T(8,128)(2,1)}, u32[]{:S(2)}, u32[]{:S(2)}) async-start(bf16[4,256,2048]{2,1,0:T(8,128)(2,1)} %broadcast_select_fusion), calls=%async_computation | async-start | bytes 8388608 | tf_op jit(solution)/shard_map/all_to_all | solution.py:34
  29.8 94.9 %all-gather.8.cloned.1.call-start = ((), (), s32[]{:S(2)}) async-start(), calls=%async_computation.4 | async-start | bytes 4718592 | tf_op jit(solution)/shard_map/all_gather | solution.py:41
  30.5 93.7 %copy-start.1 = (bf16[256,2048]{1,0:T(8,128)(2,1)S(1)}, bf16[256,2048]{1,0:T(8,128)(2,1)}, u32[]{:S(2)}) copy-start(bf16[256,2048]{1,0:T(8,128)(2,1)} %param.9) | copy-start | bytes 3145732
  30.5 93.7 %copy-start.2 = (bf16[32,2048]{1,0:T(8,128)(2,1)S(1)}, bf16[32,2048]{1,0:T(8,128)(2,1)}, u32[]{:S(2)}) copy-start(bf16[32,2048]{1,0:T(8,128)(2,1)} %param.15) | copy-start | bytes 393220
  30.5 112.0 %all-gather.6.cloned.1.call-start = ((), (), s32[]{:S(2)}) async-start(), calls=%async_computation.2 | async-start | bytes 12582912 | tf_op jit(solution)/shard_map/all_gather | solution.py:35
  123.2 66.9 %all-gather.10.cloned.1.call-start = ((), (), s32[]{:S(2)}) async-start(), calls=%async_computation.5 | async-start | bytes 4718592 | tf_op jit(solution)/shard_map/all_gather | solution.py:46
  124.0 93.4 %all-reduce.2.cloned.1.call-start = ((), (), s32[]{:S(2)}) async-start(), calls=%async_computation.3 | async-start | bytes 262144 | tf_op jit(solution)/shard_map/psum | solution.py:51
  142.5 47.7 %copy-start.4 = (bf16[32,384]{1,0:T(8,128)(2,1)S(1)}, bf16[32,384]{1,0:T(8,128)(2,1)}, u32[]{:S(2)}) copy-start(bf16[32,384]{1,0:T(8,128)(2,1)} %param.14) | copy-start | bytes 73732
  152.5 69.7 %copy-start.3 = (s32[1,256]{1,0:T(1,128)S(1)}, s32[1,256]{1,0:T(1,128)}, u32[]{:S(2)}) copy-start(s32[1,256]{1,0:T(1,128)} %param.11) | copy-start | bytes 3076
  217.3 11.2 %all-to-all-start.1 = ((f32[4,256,32]{1,2,0:T(8,128)}), f32[4,256,32]{1,2,0:T(8,128)S(1)}, u32[]{:S(2)}, u32[]{:S(2)}) async-start(f32[4,256,32]{1,2,0:T(8,128)} %all-reduce.2.cloned.1.call-done), calls=%async_computation.1 | async-start | bytes 262144 | tf_op jit(solution)/shard_map/all_to_all | solution.py:52
Sparse Core Ops, SparseCore 0:
  32.1 46.4 all-gather.7
  123.3 19.0 all-gather.5
  144.0 46.0 all-gather.9
  199.4 17.9 all-reduce.1
where the time goes:
time: 240 us; the launch traced here: 239 us
  waiting for transfers between devices  171 us (71%)
  matrix products  19.2 us (8%)
  local copies, waits for them, and re-layouts  13.8 us (6%)
  between operations  13.3 us (6%)
  starting transfers between devices  11.3 us (5%)
  other arithmetic  7.71 us (3%)
  blocking collectives  3.41 us (1%)
    all_to_all x1, waiting for transfers between devices, on_device(): lax.all_to_all(outgoing, 'exp', split_axis=0, concat_axis=0, tiled=True)  92.6 us
    all_gather x1, waiting for transfers between devices, on_device(): lax.all_gather(up_local, 'dat', axis=0, tiled=True)  37.7 us
    all_gather x1, waiting for transfers between devices, on_device(): arrived = lax.all_gather(arrived, 'mdl', axis=2, tiled=True)  17.8 us
    psum x1, waiting for transfers between devices, on_device(): code_send = lax.psum(code_part, 'mdl')  14.6 us
    dot_general x1, matrix products, on_device(): jnp.dot(arrived, lax.all_gather(gate_local, 'dat', axis=0, tiled=True), p...  10 us
    dot_general x1, matrix products, on_device(): code_part = jnp.dot(hidden, proj_in.T, preferred_element_type=jnp.float32)  8.36 us
    all_to_all x1, waiting for transfers between devices, on_device(): lax.all_to_all(code_send.reshape(experts, capacity, rank_width), 'exp', s...  6.37 us
    all_to_all x1, starting transfers between devices, on_device(): lax.all_to_all(outgoing, 'exp', split_axis=0, concat_axis=0, tiled=True)  6.32 us
  transfers between devices with their start and end apart: 6, of which 5 were waited for; matrix products, arithmetic and copies ran while one was open for 4% of the time, Pallas kernels for 0%

commit v1 on v0

v1 whole, which is shorter than its diff:
```python
import functools

import jax
import jax.numpy as jnp
from jax import lax
from jax.experimental import pallas as pl
from jax.experimental.pallas import tpu as pltpu
from jax.sharding import PartitionSpec as P

DOCS_DEV = 4
CHUNKS = 2
K_BLOCK = 512


def gate_up_kernel(first, last, *refs):
    refs = list(refs)
    mine, other, gate_mine, up_mine, gate_other, up_other = refs[:6]
    refs = refs[6:]
    if not first:
        gate_in, up_in = refs[:2]
        refs = refs[2:]
    if last:
        proj = refs.pop(0)
        out, gate_acc, up_acc = refs
    else:
        gate_acc, up_acc = refs
    step = pl.program_id(0)

    @pl.when(step == 0)
    def _():
        if first:
            gate_acc[...] = jnp.zeros_like(gate_acc)
            up_acc[...] = jnp.zeros_like(up_acc)
        else:
            gate_acc[...] = gate_in[...]
            up_acc[...] = up_in[...]

    x_mine, x_other = mine[...], other[...]
    dot = functools.partial(jnp.dot, preferred_element_type=jnp.float32)
    gate_acc[...] += dot(x_mine, gate_mine[...]) + dot(x_other, gate_other[...])
    up_acc[...] += dot(x_mine, up_mine[...]) + dot(x_other, up_other[...])

    if last:

        @pl.when(step == pl.num_programs(0) - 1)
        def _():
            gate = gate_acc[...]
            hidden = (gate / (1.0 + jnp.exp(-gate)) * up_acc[...]).astype(jnp.bfloat16)
            out[...] = lax.dot_general(
                proj[...], hidden, (((1,), (1,)), ((), ())), preferred_element_type=jnp.float32
            )


def gate_up(mine, other, weights, chunk, sums, proj):
    rows, depth = mine.shape
    cols = weights[0].shape[1]
    first, last = sums is None, proj is not None
    block = min(K_BLOCK, depth)
    steps = depth // block
    base = chunk * steps
    x_spec = pl.BlockSpec((rows, block), lambda i: (0, i))
    w_spec = pl.BlockSpec((block, cols), lambda i: (base + i, 0))
    whole = pl.BlockSpec((rows, cols), lambda i: (0, 0))
    args = [mine, other, *weights]
    in_specs = [x_spec, x_spec] + [w_spec] * 4
    if not first:
        args += list(sums)
        in_specs += [whole, whole]
    acc = jax.ShapeDtypeStruct((rows, cols), jnp.float32)
    if last:
        args.append(proj)
        in_specs.append(pl.BlockSpec(proj.shape, lambda i: (0, 0)))
        out_shape = jax.ShapeDtypeStruct((proj.shape[0], rows), jnp.float32)
        out_specs = pl.BlockSpec(out_shape.shape, lambda i: (0, 0))
        scratch = [pltpu.VMEM((rows, cols), jnp.float32)] * 2
    else:
        out_shape, out_specs, scratch = [acc, acc], [whole, whole], []
    return pl.pallas_call(
        functools.partial(gate_up_kernel, first, last),
        grid=(steps,),
        in_specs=in_specs,
        out_specs=out_specs,
        out_shape=out_shape,
        scratch_shapes=scratch,
        compiler_params=pltpu.CompilerParams(vmem_limit_bytes=24 * 2**20),
        cost_estimate=pl.CostEstimate(
            flops=8 * rows * depth * cols,
            bytes_accessed=4 * rows * depth + 8 * depth * cols,
            transcendentals=rows * cols,
        ),
        name="gate_up",
    )(*args)


def grads_kernel(experts, where, grad_mine, grad_other, docs, routes, *refs):
    same, cross, out = refs[:experts], refs[experts : 2 * experts], refs[2 * experts]
    exact = functools.partial(
        lax.dot_general, precision=lax.Precision.HIGHEST, preferred_element_type=jnp.float32
    )
    rank = grad_mine.shape[0]
    home = where[0]
    grad = grad_mine[...] + grad_other[...]
    left = jnp.concatenate(
        [jnp.where(docs[...] == d, grad, 0.0) for d in range(DOCS_DEV)], axis=0
    )
    row = lax.broadcasted_iota(jnp.int32, (rank, rank * rank), 0)
    lane = lax.broadcasted_iota(jnp.int32, (rank, rank * rank), 1)
    tile = (row == lane % rank).astype(jnp.float32)
    keep = row == lane // rank
    for k in range(experts):
        expert = lax.rem(home + k, experts)
        named = (routes[0:1, :] == expert) | (routes[1:2, :] == expert)
        codes = jnp.where(named, same[k][...] + cross[k][...], 0.0)
        block = exact(left, codes, (((1,), (1,)), ((), ())))
        spread = exact(block, tile, (((1,), (0,)), ((), ())))
        for d in range(DOCS_DEV):
            part = jnp.where(keep, spread[d * rank : (d + 1) * rank], 0.0)
            out[d, pl.ds(expert, 1), :] = jnp.sum(part, axis=0, keepdims=True)


def on_device(tokens, cotangent, routes, doc_ids, gate_weight, up_weight, proj_in, proj_out):
    experts, dats = lax.axis_size("exp"), lax.axis_size("dat")
    home, dat = lax.axis_index("exp"), lax.axis_index("dat")
    core, grp = lax.axis_index("mdl"), lax.axis_index("grp")
    rank = proj_in.shape[0]
    swap = [(0, 1), (1, 0)]
    gate, up = gate_weight[0], up_weight[0]

    width = tokens.shape[1] // CHUNKS
    mine = [[tokens[:, j * width : (j + 1) * width] for j in range(CHUNKS)]]
    ring = [(i, (i + 1) % experts) for i in range(experts)]
    for _ in range(1, experts):
        mine.append([lax.ppermute(x, "exp", ring) for x in mine[-1]])
    other = [[lax.ppermute(x, "mdl", swap) for x in xs] for xs in mine]

    half = jnp.where(grp == 0, gate, up)
    gates, ups = [gate], [up]
    for k in range(1, dats):
        direct = lax.ppermute(half, "dat", [((i + k) % dats, i) for i in range(dats)])
        swapped = lax.ppermute(direct, "grp", swap)
        gates.append(jnp.where(grp == 0, direct, swapped))
        ups.append(jnp.where(grp == 0, swapped, direct))
    per = dats // 2

    def half_of(slots, which):
        blocks = [
            lax.select_n((which * per + i - dat) % dats == 0, slots[1], slots[0])
            if dats == 2
            else lax.select_n((which * per + i - dat) % dats, *slots)
            for i in range(per)
        ]
        return blocks[0] if per == 1 else jnp.concatenate(blocks, axis=0)

    weights = (
        half_of(gates, core),
        half_of(ups, core),
        half_of(gates, 1 - core),
        half_of(ups, 1 - core),
    )

    grad_mine = lax.dot_general(
        proj_out, cotangent, (((1,), (1,)), ((), ())), preferred_element_type=jnp.float32
    )
    grad_other = lax.ppermute(grad_mine, "mdl", swap)

    same, cross = [], []
    for k in range(experts):
        sums = None
        for j in range(CHUNKS):
            last = j == CHUNKS - 1
            sums = gate_up(mine[k][j], other[k][j], weights, j, sums, proj_in if last else None)
        codes = sums
        back = [
            [
                (z * 2 + c, (z - k) % experts * 2 + (c ^ flip))
                for z in range(experts)
                for c in range(2)
            ]
            for flip in range(2)
        ]
        same.append(codes if k == 0 else lax.ppermute(codes, ("exp", "mdl"), back[0]))
        cross.append(lax.ppermute(codes, ("exp", "mdl"), back[1]))

    tok_count = tokens.shape[0]
    vmem = pl.BlockSpec(memory_space=pltpu.VMEM)
    return pl.pallas_call(
        functools.partial(grads_kernel, experts),
        in_specs=[pl.BlockSpec(memory_space=pltpu.SMEM)] + [vmem] * (4 + 2 * experts),
        out_specs=vmem,
        out_shape=jax.ShapeDtypeStruct((DOCS_DEV, experts, rank * rank), jnp.float32),
        compiler_params=pltpu.CompilerParams(vmem_limit_bytes=24 * 2**20),
        cost_estimate=pl.CostEstimate(
            flops=2 * experts * DOCS_DEV * rank * rank * tok_count,
            bytes_accessed=2**20,
            transcendentals=0,
        ),
        name="doc_grads",
    )(home.reshape(1), grad_mine, grad_other, doc_ids, routes.T, *same, *cross)


def solution(mesh):
    placed = (
        P(("grp", "exp", "dat"), "mdl"),
        P(("grp", "exp", "dat"), "mdl"),
        P(("grp", "exp", "dat"), None),
        P(("grp", "exp", "dat"), None),
        P("exp", "dat", "mdl"),
        P("exp", "dat", "mdl"),
        P(None, "mdl"),
        P(None, "mdl"),
    )
    return jax.shard_map(
        on_device,
        mesh=mesh,
        in_specs=placed,
        out_specs=P(("grp", "exp", "dat"), None, None),
        check_vma=False,
    )
```

time: 240 us -> 128 us (0.53)
  waiting for transfers between devices: 171 us -> 78.8 us
  Pallas kernels: 0 us -> 21.7 us
  matrix products: 19.2 us -> 0.41 us
  local copies, waits for them, and re-layouts: 13.8 us -> 0.1 us
  between operations: 13.3 us -> 0.23 us
  starting transfers between devices: 11.3 us -> 20.8 us
  blocking collectives: 3.41 us -> 0 us
    all_to_all x2 -> x0, waiting for transfers between devices: 99 us -> none  [the longest x1 92.6 us: on_device(): lax.all_to_all(outgoing, 'exp', split_axis=0, concat_axis=0, tiled=True)]
    ppermute x0 -> x24, waiting for transfers between devices: none -> 78.8 us  [the longest x6 43.4 us: on_device(): mine.append([lax.ppermute(x, 'exp', ring) for x in mine[-1]])]
    all_gather x3 -> x0, waiting for transfers between devices: 55.5 us -> none  [the longest x1 37.7 us: on_device(): lax.all_gather(up_local, 'dat', axis=0, tiled=True)]
    pallas_call x0 -> x9, Pallas kernels: none -> 21.7 us  [the longest x8 18.1 us: gate_up(): pl.pallas_call(functools.partial(gate_up_kernel, first, last), grid=(step...]
    ppermute x0 -> x24, starting transfers between devices: none -> 20.8 us  [the longest x6 6.36 us: on_device(): mine.append([lax.ppermute(x, 'exp', ring) for x in mine[-1]])]
    dot_general x4 -> x1, matrix products: 19.2 us -> 0.41 us  [on_device(): lax.dot_general(proj_out, cotangent, (((1,), (1,)), ((), ())), preferred_...]
    psum x1 -> x0, waiting for transfers between devices: 14.6 us -> none  [on_device(): code_send = lax.psum(code_part, 'mdl')]
    all_to_all x2 -> x0, starting transfers between devices: 11.2 us -> none  [the longest x1 6.32 us: on_device(): lax.all_to_all(outgoing, 'exp', split_axis=0, concat_axis=0, tiled=True)]
  transfers between devices with their start and end apart: 6 -> 24, of which waited for: 5 -> 7; matrix products, arithmetic and copies ran while one was open for 4% -> 3% of each run, Pallas kernels for 0% -> 14%
where the time goes in v1:
time: 128 us
  waiting for transfers between devices  78.8 us (62%)
  Pallas kernels  21.7 us (17%)
  starting transfers between devices  20.8 us (16%)
  other arithmetic  5.77 us (5%)
    ppermute x6, waiting for transfers between devices, on_device(): mine.append([lax.ppermute(x, 'exp', ring) for x in mine[-1]])  43.4 us
    ppermute x1, waiting for transfers between devices, on_device(): lax.ppermute(half, 'dat', [((i + k) % dats, i) for i in range(dats)])  31.2 us
    pallas_call x8, Pallas kernels, gate_up(): pl.pallas_call(functools.partial(gate_up_kernel, first, last), grid=(step...  18.1 us
    ppermute x6, starting transfers between devices, on_device(): mine.append([lax.ppermute(x, 'exp', ring) for x in mine[-1]])  6.36 us
    ppermute x4, waiting for transfers between devices, on_device(): cross.append(lax.ppermute(codes, ('exp', 'mdl'), back[1]))  4.15 us
    ppermute x4, starting transfers between devices, on_device(): cross.append(lax.ppermute(codes, ('exp', 'mdl'), back[1]))  4.12 us
    select_n x1, other arithmetic, half_of(): lax.select_n((which * per + i - dat) % dats == 0, slots[1], slots[0])  3.56 us
    pallas_call x1, Pallas kernels, on_device(): pl.pallas_call(functools.partial(grads_kernel, experts), in_specs=[pl.Blo...  3.55 us
  transfers between devices with their start and end apart: 24, of which 7 were waited for; matrix products, arithmetic and copies ran while one was open for 3% of the time, Pallas kernels for 14%

profile of v1, /device:TPU:0, one launch (start us, length us, event | category | flops | bytes accessed | tf_op | source)
XLA Modules:
  0.0 127.8 jit_solution(5085474582913263703)
XLA Ops:
  0.0 2.2 %bitcast_select_fusion.2 = bf16[2048,384]{1,0:T(8,128)(2,1)S(1)} fusion(bf16[1,2048,384]{2,1,0:T(8,128)(2,1)} %param.13, bf16[1,2048,384]{2,1,0:T(8,128)(2,1)} %param.12, pred[]{:T(512)S(6)} %eq.19), kind=kLoop, calls=%fused_computation.2 | loop fusion | flops 786432 | bytes 4718593 | tf_op jit(solution)/shard_map/jit(_where)/select_n | solution.py:136
  2.2 0.0 copy-start.7
  2.2 3.0 %collective-permute-start.2 = (bf16[2048,384]{1,0:T(8,128)(2,1)S(1)}, bf16[2048,384]{1,0:T(8,128)(2,1)}, u32[]{:S(2)}, u32[]{:S(2)}) collective-permute-start(bf16[2048,384]{1,0:T(8,128)(2,1)S(1)} %bitcast_select_fusion.2), channel_id=1, source_target_pairs={{2,0},{0,2},{3,1},{1,3},{6,4},{4,6},{7,5},{5,7},{10,8},{8,10},{11,... | collective-permute-start | bytes 4718600 | tf_op jit(solution)/shard_map/ppermute | solution.py:139
  5.2 0.1 fusion
  5.3 1.6 %collective-permute-start.5 = (bf16[256,1024]{1,0:T(8,128)(2,1)S(1)}, bf16[256,1024]{1,0:T(8,128)(2,1)S(1)}, u32[]{:S(2)}, u32[]{:S(2)}) collective-permute-start(bf16[256,1024]{1,0:T(8,128)(2,1)S(1)} %get-tuple-element.28.refs_0_), channel_id=1, source_target_pairs={{0,4},{4,8},{8,12},{12,0},{1,5},{5,9},{9,13},{13,1},{2,6},{6,10},{... | collective-permute-start | bytes 1572872 | tf_op jit(solution)/shard_map/ppermute | solution.py:133
  6.9 1.6 %collective-permute-start.7 = (bf16[256,1024]{1,0:T(8,128)(2,1)S(1)}, bf16[256,1024]{1,0:T(8,128)(2,1)S(1)}, u32[]{:S(2)}, u32[]{:S(2)}) collective-permute-start(bf16[256,1024]{1,0:T(8,128)(2,1)S(1)} %get-tuple-element.27.refs_0_), channel_id=1, source_target_pairs={{0,4},{4,8},{8,12},{12,0},{1,5},{5,9},{9,13},{13,1},{2,6},{6,10},{... | collective-permute-start | bytes 1572872 | tf_op jit(solution)/shard_map/ppermute | solution.py:133
  8.5 31.2 %collective-permute-done.2 = bf16[2048,384]{1,0:T(8,128)(2,1)} collective-permute-done((bf16[2048,384]{1,0:T(8,128)(2,1)S(1)}, bf16[2048,384]{1,0:T(8,128)(2,1)}, u32[]{:S(2)}, u32[]{:S(2)}) %collective-permute-start.2) | collective-permute-done | bytes 1572896 | tf_op jit(solution)/shard_map/ppermute | solution.py:139
  39.7 1.8 %collective-permute-start.3 = (bf16[2048,384]{1,0:T(8,128)(2,1)}, bf16[2048,384]{1,0:T(8,128)(2,1)}, u32[]{:S(2)}, u32[]{:S(2)}) collective-permute-start(bf16[2048,384]{1,0:T(8,128)(2,1)} %collective-permute-done.2), channel_id=1, source_target_pairs={{0,16},{16,0},{1,17},{17,1},{2,18},{18,2},{3,19},{19,3},{4,20},{20... | collective-permute-start | bytes 4718600 | tf_op jit(solution)/shard_map/ppermute | solution.py:140
  41.5 1.6 %collective-permute-start.10 = (bf16[256,1024]{1,0:T(8,128)(2,1)S(1)}, bf16[256,1024]{1,0:T(8,128)(2,1)}, u32[]{:S(2)}, u32[]{:S(2)}) collective-permute-start(bf16[256,1024]{1,0:T(8,128)(2,1)S(1)} %collective-permute-done.5.refs_0_), channel_id=1, source_target_pairs={{0,4},{4,8},{8,12},{12,0},{1,5},{5,9},{9,13},{13,1},{2,6},{6,10},{... | collective-permute-start | bytes 1572872 | tf_op jit(solution)/shard_map/ppermute | solution.py:133
  43.1 0.0 collective-permute-done.7.refs_0_
  43.1 1.6 %collective-permute-start.12 = (bf16[256,1024]{1,0:T(8,128)(2,1)S(1)}, bf16[256,1024]{1,0:T(8,128)(2,1)}, u32[]{:S(2)}, u32[]{:S(2)}) collective-permute-start(bf16[256,1024]{1,0:T(8,128)(2,1)S(1)} %collective-permute-done.7.refs_0_), channel_id=1, source_target_pairs={{0,4},{4,8},{8,12},{12,0},{1,5},{5,9},{9,13},{13,1},{2,6},{6,10},{... | collective-permute-start | bytes 1572872 | tf_op jit(solution)/shard_map/ppermute | solution.py:133
  44.7 0.0 collective-permute-start.4
  44.7 0.5 collective-permute-start.8
  45.2 13.1 %collective-permute-done.10.refs_0_ = bf16[256,1024]{1,0:T(8,128)(2,1)} collective-permute-done((bf16[256,1024]{1,0:T(8,128)(2,1)S(1)}, bf16[256,1024]{1,0:T(8,128)(2,1)}, u32[]{:S(2)}, u32[]{:S(2)}) %collective-permute-start.10) | collective-permute-done | bytes 524320 | tf_op jit(solution)/shard_map/ppermute | solution.py:133
  58.3 11.2 %collective-permute-done.12.refs_0_ = bf16[256,1024]{1,0:T(8,128)(2,1)} collective-permute-done((bf16[256,1024]{1,0:T(8,128)(2,1)S(1)}, bf16[256,1024]{1,0:T(8,128)(2,1)}, u32[]{:S(2)}, u32[]{:S(2)}) %collective-permute-start.12) | collective-permute-done | bytes 524320 | tf_op jit(solution)/shard_map/ppermute | solution.py:133
  69.5 0.4 fusion.1.grad_mine
  69.9 0.0 collective-permute-done.4.refs_1_
  70.0 0.1 collective-permute-start.6
  70.0 0.0 collective-permute-done.8.refs_1_
  70.1 0.5 collective-permute-start.11
  70.5 10.2 %collective-permute-done.15.refs_0_ = bf16[256,1024]{1,0:T(8,128)(2,1)} collective-permute-done((bf16[256,1024]{1,0:T(8,128)(2,1)}, bf16[256,1024]{1,0:T(8,128)(2,1)}, u32[]{:S(2)}, u32[]{:S(2)}) %collective-permute-start.15) | collective-permute-done | bytes 524320 | tf_op jit(solution)/shard_map/ppermute | solution.py:133
  80.7 0.0 collective-permute-start.13
  80.8 8.8 %collective-permute-done.17.refs_0_ = bf16[256,1024]{1,0:T(8,128)(2,1)S(1)} collective-permute-done((bf16[256,1024]{1,0:T(8,128)(2,1)}, bf16[256,1024]{1,0:T(8,128)(2,1)S(1)}, u32[]{:S(2)}, u32[]{:S(2)}) %collective-permute-start.17) | collective-permute-done | bytes 524320 | tf_op jit(solution)/shard_map/ppermute | solution.py:133
  89.6 0.0 collective-permute-start.16
  89.6 0.0 collective-permute-done.3
  89.6 0.5 collective-permute-start.18
  90.1 3.6 %bitcast_select_fusion = (bf16[2048,384]{1,0:T(8,128)(2,1)S(1)}, bf16[2048,384]{1,0:T(8,128)(2,1)S(1)}, bf16[2048,384]{1,0:T(8,128)(2,1)S(1)}, bf16[2048,384]{1,0:T(8,128)(2,1)S(1)}) fusion(bf16[1,2048,384]{2,1,0:T(8,128)(2,1)} %param.13, pred[]{:T(512)S(6)} %eq.20, bf16[2048,384]{1,0:T(8,128)(2,1)} %collective-permute-done.3, ...), kind=kLoop, calls=%fused_computation | loop fusion | flops 4718592 | bytes 12582915 | tf_op jit(solution)/shard_map/select_n | solution.py:147
  93.7 0.1 collective-permute-start.1
  93.8 2.5 %gate_up.8 = (f32[256,384]{1,0:T(8,128)S(1)}, f32[256,384]{1,0:T(8,128)S(1)}) custom-call(bf16[256,1024]{1,0:T(8,128)(2,1)S(1)} %get-tuple-element.27.refs_0_, bf16[256,1024]{1,0:T(8,128)(2,1)} %collective-permute-done.4.refs_1_, bf16[2048,384]{1,0:T(8,128)(2,1)S(1)} %get-tuple-element.25.refs_2_, bf16[2048,384]{1,0:T(8,128)(2,1)S(1)} %get-tuple-element.22.refs_3_, ...), custom_call_target="tpu_custom_call" | custom-call | flops 805306368 | bytes 4194304 | tf_op jit(solution)/shard_map/gate_up/pallas_call | solution.py:78
  96.3 2.5 %gate_up.10 = (f32[256,384]{1,0:T(8,128)S(1)}, f32[256,384]{1,0:T(8,128)S(1)}) custom-call(bf16[256,1024]{1,0:T(8,128)(2,1)S(1)} %collective-permute-done.7.refs_0_, bf16[256,1024]{1,0:T(8,128)(2,1)} %collective-permute-done.8.refs_1_, bf16[2048,384]{1,0:T(8,128)(2,1)S(1)} %get-tuple-element.25.refs_2_, bf16[2048,384]{1,0:T(8,128)(2,1)S(1)} %get-tuple-element.22.refs_3_, ...), custom_call_target="tpu_custom_call" | custom-call | flops 805306368 | bytes 4194304 | tf_op jit(solution)/shard_map/gate_up/pallas_call | solution.py:78
  98.8 0.0 copy-start.3
  98.8 2.5 %gate_up.12 = (f32[256,384]{1,0:T(8,128)S(1)}, f32[256,384]{1,0:T(8,128)S(1)}) custom-call(bf16[256,1024]{1,0:T(8,128)(2,1)} %collective-permute-done.12.refs_0_, bf16[256,1024]{1,0:T(8,128)(2,1)S(1)} %collective-permute-done.13.refs_1_, bf16[2048,384]{1,0:T(8,128)(2,1)S(1)} %get-tuple-element.25.refs_2_, bf16[2048,384]{1,0:T(8,128)(2,1)S(1)} %get-tuple-element.22.refs_3_, ...), custom_call_target="tpu_custom_call" | custom-call | flops 805306368 | bytes 4194304 | tf_op jit(solution)/shard_map/gate_up/pallas_call | solution.py:78
  101.3 0.6 collective-permute-start
  101.9 1.8 %gate_up.11 = f32[32,256]{1,0:T(8,128)S(1)} custom-call(bf16[256,1024]{1,0:T(8,128)(2,1)S(1)} %copy-done.2, bf16[256,1024]{1,0:T(8,128)(2,1)S(1)} %collective-permute-done.6.refs_1_, bf16[2048,384]{1,0:T(8,128)(2,1)S(1)} %get-tuple-element.25.refs_2_, bf16[2048,384]{1,0:T(8,128)(2,1)S(1)} %get-tuple-element.22.refs_3_, ...), custom_call_target="tpu_custom_call" | custom-call | flops 805306368 | bytes 4194304 | tf_op jit(solution)/shard_map/gate_up/pallas_call | solution.py:78
  103.7 1.8 %collective-permute-start.9 = (f32[32,256]{1,0:T(8,128)S(1)}, f32[32,256]{1,0:T(8,128)S(1)}, u32[]{:S(2)}, u32[]{:S(2)}) collective-permute-start(f32[32,256]{1,0:T(8,128)S(1)} %gate_up.11), channel_id=1, source_target_pairs={{0,12},{1,13},{4,0},{5,1},{8,4},{9,5},{12,8},{13,9},{2,14},{3,15},... | collective-permute-start | bytes 98312 | tf_op jit(solution)/shard_map/ppermute | solution.py:181
  105.5 1.6 %gate_up.14 = (f32[256,384]{1,0:T(8,128)S(1)}, f32[256,384]{1,0:T(8,128)S(1)}) custom-call(bf16[256,1024]{1,0:T(8,128)(2,1)S(1)} %collective-permute-done.17.refs_0_, bf16[256,1024]{1,0:T(8,128)(2,1)S(1)} %collective-permute-done.18.refs_1_, bf16[2048,384]{1,0:T(8,128)(2,1)S(1)} %get-tuple-element.25.refs_2_, ...), custom_call_target="tpu_custom_call" | custom-call | flops 805306368 | bytes 4194304 | tf_op jit(solution)/shard_map/gate_up/pallas_call | solution.py:78
  107.1 0.1 collective-permute-start.21
  107.2 2.7 %gate_up.13 = f32[32,256]{1,0:T(8,128)S(1)} custom-call(bf16[256,1024]{1,0:T(8,128)(2,1)} %collective-permute-done.10.refs_0_, bf16[256,1024]{1,0:T(8,128)(2,1)S(1)} %collective-permute-done.11.refs_1_, bf16[2048,384]{1,0:T(8,128)(2,1)S(1)} %get-tuple-element.25.refs_2_, bf16[2048,384]{1,0:T(8,128)(2,1)S(1)} %get-tuple-element.22.refs_3_, ...), custom_call_target="tpu_custom_call" | custom-call | flops 805306368 | bytes 4194304 | tf_op jit(solution)/shard_map/gate_up/pallas_call | solution.py:78
  109.9 1.2 collective-permute-start.14
  111.1 2.7 %gate_up.15 = f32[32,256]{1,0:T(8,128)S(1)} custom-call(bf16[256,1024]{1,0:T(8,128)(2,1)} %collective-permute-done.15.refs_0_, bf16[256,1024]{1,0:T(8,128)(2,1)S(1)} %collective-permute-done.16.refs_1_, bf16[2048,384]{1,0:T(8,128)(2,1)S(1)} %get-tuple-element.25.refs_2_, bf16[2048,384]{1,0:T(8,128)(2,1)S(1)} %get-tuple-element.22.refs_3_, ...), custom_call_target="tpu_custom_call" | custom-call | flops 805306368 | bytes 4194304 | tf_op jit(solution)/shard_map/gate_up/pallas_call | solution.py:78
  113.8 0.3 collective-permute-start.19
  114.2 1.8 %gate_up.9.refs_0_ = f32[32,256]{1,0:T(8,128)S(1)} custom-call(bf16[256,1024]{1,0:T(8,128)(2,1)S(1)} %get-tuple-element.28.refs_0_, bf16[256,1024]{1,0:T(8,128)(2,1)S(1)} %collective-permute-done.1.refs_1_, bf16[2048,384]{1,0:T(8,128)(2,1)S(1)} %get-tuple-element.25.refs_2_, bf16[2048,384]{1,0:T(8,128)(2,1)S(1)} %get-tuple-element.22.refs_3_, ...), custom_call_target="tpu_custom_call" | custom-call | flops 805306368 | bytes 4194304 | tf_op jit(solution)/shard_map/gate_up/pallas_call | solution.py:78
  116.0 0.5 collective-permute-start.20
  116.5 2.6 %collective-permute-start.22 = (f32[32,256]{1,0:T(8,128)S(1)}, f32[32,256]{1,0:T(8,128)S(1)}, u32[]{:S(2)}, u32[]{:S(2)}) collective-permute-start(f32[32,256]{1,0:T(8,128)S(1)} %gate_up.13), channel_id=1, source_target_pairs={{0,9},{1,8},{4,13},{5,12},{8,1},{9,0},{12,5},{13,4},{2,11},{3,10},... | collective-permute-start | bytes 98312 | tf_op jit(solution)/shard_map/ppermute | solution.py:182
  119.1 1.0 collective-permute-start.23
  120.1 0.8 collective-permute-done.22.refs_6_
  120.8 3.4 %collective-permute-done.23.refs_7_ = f32[32,256]{1,0:T(8,128)S(1)} collective-permute-done((f32[32,256]{1,0:T(8,128)S(1)}, f32[32,256]{1,0:T(8,128)S(1)}, u32[]{:S(2)}, u32[]{:S(2)}) %collective-permute-start.23) | collective-permute-done | bytes 32800 | tf_op jit(solution)/shard_map/ppermute | solution.py:182
  124.2 3.5 %doc_grads.1 = f32[4,4,1024]{2,1,0:T(4,128)} custom-call(s32[1]{0:T(128)} %bitcast.where, f32[32,256]{1,0:T(8,128)S(1)} %fusion.1.grad_mine, f32[32,256]{1,0:T(8,128)S(1)} %collective-permute-done.grad_other, s32[1,256]{1,0:T(1,128)S(1)} %copy-done.5, s32[2,256]{1,0:T(2,128)S(1)} %bitcast.12, f32[32,256]{1,0:T(8,128)S(1)} %gate_up.9.refs_0_, ...), custom_call_target="tpu_custom_call" | custom-call | flops 8388608 | bytes 1048576 | tf_op jit(solution)/shard_map/doc_grads/pallas_call | solution.py:186
  (29 shorter events, 0.1 us)
Async XLA Ops:
  0.0 69.5 %copy-start = (bf16[256,2048]{1,0:T(8,128)(2,1)S(1)}, bf16[256,2048]{1,0:T(8,128)(2,1)}, u32[]{:S(2)}) copy-start(bf16[256,2048]{1,0:T(8,128)(2,1)} %param.9) | copy-start | bytes 3145732
  0.0 5.2 %copy-start.6 = (bf16[256,2048]{1,0:T(8,128)(2,1)S(1)}, bf16[256,2048]{1,0:T(8,128)(2,1)}, u32[]{:S(2)}) copy-start(bf16[256,2048]{1,0:T(8,128)(2,1)} %param.8) | copy-start | bytes 3145732
  2.2 67.3 %copy-start.7 = (bf16[32,2048]{1,0:T(8,128)(2,1)S(1)}, bf16[32,2048]{1,0:T(8,128)(2,1)}, u32[]{:S(2)}) copy-start(bf16[32,2048]{1,0:T(8,128)(2,1)} %param.15) | copy-start | bytes 393220
  2.2 37.5 %collective-permute-start.2 = (bf16[2048,384]{1,0:T(8,128)(2,1)S(1)}, bf16[2048,384]{1,0:T(8,128)(2,1)}, u32[]{:S(2)}, u32[]{:S(2)}) collective-permute-start(bf16[2048,384]{1,0:T(8,128)(2,1)S(1)} %bitcast_select_fusion.2), channel_id=1, source_target_pairs={{2,0},{0,2},{3,1},{1,3},{6,4},{4,6},{7,5},{5,7},{10,8},{8,10},{11,... | collective-permute-start | bytes 4718600 | tf_op jit(solution)/shard_map/ppermute | solution.py:139
  5.3 36.2 %collective-permute-start.5 = (bf16[256,1024]{1,0:T(8,128)(2,1)S(1)}, bf16[256,1024]{1,0:T(8,128)(2,1)S(1)}, u32[]{:S(2)}, u32[]{:S(2)}) collective-permute-start(bf16[256,1024]{1,0:T(8,128)(2,1)S(1)} %get-tuple-element.28.refs_0_), channel_id=1, source_target_pairs={{0,4},{4,8},{8,12},{12,0},{1,5},{5,9},{9,13},{13,1},{2,6},{6,10},{... | collective-permute-start | bytes 1572872 | tf_op jit(solution)/shard_map/ppermute | solution.py:133
  6.9 36.1 %collective-permute-start.7 = (bf16[256,1024]{1,0:T(8,128)(2,1)S(1)}, bf16[256,1024]{1,0:T(8,128)(2,1)S(1)}, u32[]{:S(2)}, u32[]{:S(2)}) collective-permute-start(bf16[256,1024]{1,0:T(8,128)(2,1)S(1)} %get-tuple-element.27.refs_0_), channel_id=1, source_target_pairs={{0,4},{4,8},{8,12},{12,0},{1,5},{5,9},{9,13},{13,1},{2,6},{6,10},{... | collective-permute-start | bytes 1572872 | tf_op jit(solution)/shard_map/ppermute | solution.py:133
  39.7 49.9 %collective-permute-start.3 = (bf16[2048,384]{1,0:T(8,128)(2,1)}, bf16[2048,384]{1,0:T(8,128)(2,1)}, u32[]{:S(2)}, u32[]{:S(2)}) collective-permute-start(bf16[2048,384]{1,0:T(8,128)(2,1)} %collective-permute-done.2), channel_id=1, source_target_pairs={{0,16},{16,0},{1,17},{17,1},{2,18},{18,2},{3,19},{19,3},{4,20},{20... | collective-permute-start | bytes 4718600 | tf_op jit(solution)/shard_map/ppermute | solution.py:140
  41.5 28.0 %copy-start.1 = (bf16[256,1024]{1,0:T(8,128)(2,1)}, bf16[256,1024]{1,0:T(8,128)(2,1)S(1)}, u32[]{:S(2)}) copy-start(bf16[256,1024]{1,0:T(8,128)(2,1)S(1)} %collective-permute-done.5.refs_0_) | copy-start | bytes 1572868
  41.5 16.8 %collective-permute-start.10 = (bf16[256,1024]{1,0:T(8,128)(2,1)S(1)}, bf16[256,1024]{1,0:T(8,128)(2,1)}, u32[]{:S(2)}, u32[]{:S(2)}) collective-permute-start(bf16[256,1024]{1,0:T(8,128)(2,1)S(1)} %collective-permute-done.5.refs_0_), channel_id=1, source_target_pairs={{0,4},{4,8},{8,12},{12,0},{1,5},{5,9},{9,13},{13,1},{2,6},{6,10},{... | collective-permute-start | bytes 1572872 | tf_op jit(solution)/shard_map/ppermute | solution.py:133
  43.1 26.4 %collective-permute-start.12 = (bf16[256,1024]{1,0:T(8,128)(2,1)S(1)}, bf16[256,1024]{1,0:T(8,128)(2,1)}, u32[]{:S(2)}, u32[]{:S(2)}) collective-permute-start(bf16[256,1024]{1,0:T(8,128)(2,1)S(1)} %collective-permute-done.7.refs_0_), channel_id=1, source_target_pairs={{0,4},{4,8},{8,12},{12,0},{1,5},{5,9},{9,13},{13,1},{2,6},{6,10},{... | collective-permute-start | bytes 1572872 | tf_op jit(solution)/shard_map/ppermute | solution.py:133
  44.7 25.3 %collective-permute-start.4 = (bf16[256,1024]{1,0:T(8,128)(2,1)S(1)}, bf16[256,1024]{1,0:T(8,128)(2,1)}, u32[]{:S(2)}, u32[]{:S(2)}) collective-permute-start(bf16[256,1024]{1,0:T(8,128)(2,1)S(1)} %get-tuple-element.27.refs_0_), channel_id=1, source_target_pairs={{0,1},{1,0},{2,3},{3,2},{4,5},{5,4},{6,7},{7,6},{8,9},{9,8},{10,11... | collective-permute-start | bytes 1572872 | tf_op jit(solution)/shard_map/ppermute | solution.py:134
  44.7 25.4 %collective-permute-start.8 = (bf16[256,1024]{1,0:T(8,128)(2,1)S(1)}, bf16[256,1024]{1,0:T(8,128)(2,1)}, u32[]{:S(2)}, u32[]{:S(2)}) collective-permute-start(bf16[256,1024]{1,0:T(8,128)(2,1)S(1)} %collective-permute-done.7.refs_0_), channel_id=1, source_target_pairs={{0,1},{1,0},{2,3},{3,2},{4,5},{5,4},{6,7},{7,6},{8,9},{9,8},{10,11... | collective-permute-start | bytes 1572872 | tf_op jit(solution)/shard_map/ppermute | solution.py:134
  58.3 22.5 %collective-permute-start.15 = (bf16[256,1024]{1,0:T(8,128)(2,1)}, bf16[256,1024]{1,0:T(8,128)(2,1)}, u32[]{:S(2)}, u32[]{:S(2)}) collective-permute-start(bf16[256,1024]{1,0:T(8,128)(2,1)} %collective-permute-done.10.refs_0_), channel_id=1, source_target_pairs={{0,4},{4,8},{8,12},{12,0},{1,5},{5,9},{9,13},{13,1},{2,6},{6,10},{... | collective-permute-start | bytes 1572872 | tf_op jit(solution)/shard_map/ppermute | solution.py:133
  69.5 20.1 %collective-permute-start.17 = (bf16[256,1024]{1,0:T(8,128)(2,1)}, bf16[256,1024]{1,0:T(8,128)(2,1)S(1)}, u32[]{:S(2)}, u32[]{:S(2)}) collective-permute-start(bf16[256,1024]{1,0:T(8,128)(2,1)} %collective-permute-done.12.refs_0_), channel_id=1, source_target_pairs={{0,4},{4,8},{8,12},{12,0},{1,5},{5,9},{9,13},{13,1},{2,6},{6,10},{... | collective-permute-start | bytes 1572872 | tf_op jit(solution)/shard_map/ppermute | solution.py:133
  70.0 31.4 %collective-permute-start.6 = (bf16[256,1024]{1,0:T(8,128)(2,1)}, bf16[256,1024]{1,0:T(8,128)(2,1)S(1)}, u32[]{:S(2)}, u32[]{:S(2)}) collective-permute-start(bf16[256,1024]{1,0:T(8,128)(2,1)} %copy-done.1), channel_id=1, source_target_pairs={{0,1},{1,0},{2,3},{3,2},{4,5},{5,4},{6,7},{7,6},{8,9},{9,8},{10,11... | collective-permute-start | bytes 1572872 | tf_op jit(solution)/shard_map/ppermute | solution.py:134
  70.1 37.1 %collective-permute-start.11 = (bf16[256,1024]{1,0:T(8,128)(2,1)}, bf16[256,1024]{1,0:T(8,128)(2,1)S(1)}, u32[]{:S(2)}, u32[]{:S(2)}) collective-permute-start(bf16[256,1024]{1,0:T(8,128)(2,1)} %collective-permute-done.10.refs_0_), channel_id=1, source_target_pairs={{0,1},{1,0},{2,3},{3,2},{4,5},{5,4},{6,7},{7,6},{8,9},{9,8},{10,11... | collective-permute-start | bytes 1572872 | tf_op jit(solution)/shard_map/ppermute | solution.py:134
  80.7 12.9 %collective-permute-start.13 = (bf16[256,1024]{1,0:T(8,128)(2,1)}, bf16[256,1024]{1,0:T(8,128)(2,1)S(1)}, u32[]{:S(2)}, u32[]{:S(2)}) collective-permute-start(bf16[256,1024]{1,0:T(8,128)(2,1)} %collective-permute-done.12.refs_0_), channel_id=1, source_target_pairs={{0,1},{1,0},{2,3},{3,2},{4,5},{5,4},{6,7},{7,6},{8,9},{9,8},{10,11... | collective-permute-start | bytes 1572872 | tf_op jit(solution)/shard_map/ppermute | solution.py:134
  89.6 20.3 %collective-permute-start.16 = (bf16[256,1024]{1,0:T(8,128)(2,1)}, bf16[256,1024]{1,0:T(8,128)(2,1)S(1)}, u32[]{:S(2)}, u32[]{:S(2)}) collective-permute-start(bf16[256,1024]{1,0:T(8,128)(2,1)} %collective-permute-done.15.refs_0_), channel_id=1, source_target_pairs={{0,1},{1,0},{2,3},{3,2},{4,5},{5,4},{6,7},{7,6},{8,9},{9,8},{10,11... | collective-permute-start | bytes 1572872 | tf_op jit(solution)/shard_map/ppermute | solution.py:134
  89.6 14.1 %collective-permute-start.18 = (bf16[256,1024]{1,0:T(8,128)(2,1)S(1)}, bf16[256,1024]{1,0:T(8,128)(2,1)S(1)}, u32[]{:S(2)}, u32[]{:S(2)}) collective-permute-start(bf16[256,1024]{1,0:T(8,128)(2,1)S(1)} %collective-permute-done.17.refs_0_), channel_id=1, source_target_pairs={{0,1},{1,0},{2,3},{3,2},{4,5},{5,4},{6,7},{7,6},{8,9},{9,8},{10,11... | collective-permute-start | bytes 1572872 | tf_op jit(solution)/shard_map/ppermute | solution.py:134
  93.7 20.1 %collective-permute-start.1 = (bf16[256,1024]{1,0:T(8,128)(2,1)S(1)}, bf16[256,1024]{1,0:T(8,128)(2,1)S(1)}, u32[]{:S(2)}, u32[]{:S(2)}) collective-permute-start(bf16[256,1024]{1,0:T(8,128)(2,1)S(1)} %get-tuple-element.28.refs_0_), channel_id=1, source_target_pairs={{0,1},{1,0},{2,3},{3,2},{4,5},{5,4},{6,7},{7,6},{8,9},{9,8},{10,11... | collective-permute-start | bytes 1572872 | tf_op jit(solution)/shard_map/ppermute | solution.py:134
  98.8 3.1 %copy-start.2 = (bf16[256,1024]{1,0:T(8,128)(2,1)S(1)}, bf16[256,1024]{1,0:T(8,128)(2,1)}, u32[]{:S(2)}) copy-start(bf16[256,1024]{1,0:T(8,128)(2,1)} %copy-done.1) | copy-start | bytes 1572868
  98.8 3.1 %copy-start.3 = (bf16[32,384]{1,0:T(8,128)(2,1)S(1)}, bf16[32,384]{1,0:T(8,128)(2,1)}, u32[]{:S(2)}) copy-start(bf16[32,384]{1,0:T(8,128)(2,1)} %refs_8_.7) | copy-start | bytes 73732
  101.3 14.6 %collective-permute-start = (f32[32,256]{1,0:T(8,128)S(1)}, f32[32,256]{1,0:T(8,128)S(1)}, u32[]{:S(2)}, u32[]{:S(2)}) collective-permute-start(f32[32,256]{1,0:T(8,128)S(1)} %fusion.1.grad_mine), channel_id=1, source_target_pairs={{0,1},{1,0},{2,3},{3,2},{4,5},{5,4},{6,7},{7,6},{8,9},{9,8},{10,11... | collective-permute-start | bytes 98312 | tf_op jit(solution)/shard_map/ppermute | solution.py:164
  103.7 12.8 %collective-permute-start.9 = (f32[32,256]{1,0:T(8,128)S(1)}, f32[32,256]{1,0:T(8,128)S(1)}, u32[]{:S(2)}, u32[]{:S(2)}) collective-permute-start(f32[32,256]{1,0:T(8,128)S(1)} %gate_up.11), channel_id=1, source_target_pairs={{0,12},{1,13},{4,0},{5,1},{8,4},{9,5},{12,8},{13,9},{2,14},{3,15},... | collective-permute-start | bytes 98312 | tf_op jit(solution)/shard_map/ppermute | solution.py:181
  107.1 12.9 %collective-permute-start.21 = (f32[32,256]{1,0:T(8,128)S(1)}, f32[32,256]{1,0:T(8,128)S(1)}, u32[]{:S(2)}, u32[]{:S(2)}) collective-permute-start(f32[32,256]{1,0:T(8,128)S(1)} %gate_up.11), channel_id=1, source_target_pairs={{0,13},{1,12},{4,1},{5,0},{8,5},{9,4},{12,9},{13,8},{2,15},{3,14},... | collective-permute-start | bytes 98312 | tf_op jit(solution)/shard_map/ppermute | solution.py:182
  109.9 9.1 %collective-permute-start.14 = (f32[32,256]{1,0:T(8,128)S(1)}, f32[32,256]{1,0:T(8,128)S(1)}, u32[]{:S(2)}, u32[]{:S(2)}) collective-permute-start(f32[32,256]{1,0:T(8,128)S(1)} %gate_up.13), channel_id=1, source_target_pairs={{0,8},{1,9},{4,12},{5,13},{8,0},{9,1},{12,4},{13,5},{2,10},{3,11},... | collective-permute-start | bytes 98312 | tf_op jit(solution)/shard_map/ppermute | solution.py:181
  113.8 6.3 %collective-permute-start.19 = (f32[32,256]{1,0:T(8,128)S(1)}, f32[32,256]{1,0:T(8,128)S(1)}, u32[]{:S(2)}, u32[]{:S(2)}) collective-permute-start(f32[32,256]{1,0:T(8,128)S(1)} %gate_up.15), channel_id=1, source_target_pairs={{0,4},{1,5},{4,8},{5,9},{8,12},{9,13},{12,0},{13,1},{2,6},{3,7},{6... | collective-permute-start | bytes 98312 | tf_op jit(solution)/shard_map/ppermute | solution.py:181
  114.1 10.1 %copy-start.4 = (s32[256,2]{0,1:T(2,128)S(1)}, s32[256,2]{0,1:T(2,128)}, u32[]{:S(2)}) copy-start(s32[256,2]{0,1:T(2,128)} %param.10) | copy-start | bytes 6148
  114.1 10.1 %copy-start.5 = (s32[1,256]{1,0:T(1,128)S(1)}, s32[1,256]{1,0:T(1,128)}, u32[]{:S(2)}) copy-start(s32[1,256]{1,0:T(1,128)} %docs.1) | copy-start | bytes 3076
  116.0 4.1 %collective-permute-start.20 = (f32[32,256]{1,0:T(8,128)S(1)}, f32[32,256]{1,0:T(8,128)S(1)}, u32[]{:S(2)}, u32[]{:S(2)}) collective-permute-start(f32[32,256]{1,0:T(8,128)S(1)} %gate_up.9.refs_0_), channel_id=1, source_target_pairs={{0,1},{1,0},{4,5},{5,4},{8,9},{9,8},{12,13},{13,12},{2,3},{3,2},{6... | collective-permute-start | bytes 98312 | tf_op jit(solution)/shard_map/ppermute | solution.py:182
  116.5 4.3 %collective-permute-start.22 = (f32[32,256]{1,0:T(8,128)S(1)}, f32[32,256]{1,0:T(8,128)S(1)}, u32[]{:S(2)}, u32[]{:S(2)}) collective-permute-start(f32[32,256]{1,0:T(8,128)S(1)} %gate_up.13), channel_id=1, source_target_pairs={{0,9},{1,8},{4,13},{5,12},{8,1},{9,0},{12,5},{13,4},{2,11},{3,10},... | collective-permute-start | bytes 98312 | tf_op jit(solution)/shard_map/ppermute | solution.py:182
  119.1 5.1 %collective-permute-start.23 = (f32[32,256]{1,0:T(8,128)S(1)}, f32[32,256]{1,0:T(8,128)S(1)}, u32[]{:S(2)}, u32[]{:S(2)}) collective-permute-start(f32[32,256]{1,0:T(8,128)S(1)} %gate_up.15), channel_id=1, source_target_pairs={{0,5},{1,4},{4,9},{5,8},{8,13},{9,12},{12,1},{13,0},{2,7},{3,6},{6... | collective-permute-start | bytes 98312 | tf_op jit(solution)/shard_map/ppermute | solution.py:182

commit v2 on v1

v2 whole, which is shorter than its diff:
```python
import functools

import jax
import jax.numpy as jnp
from jax import lax
from jax.experimental import pallas as pl
from jax.experimental.pallas import tpu as pltpu
from jax.sharding import PartitionSpec as P

DOCS_DEV = 4
CHUNKS = 2
LANES = 128


def after(x, *others):
    place = pl.BlockSpec(memory_space=pl.ANY)
    return pl.pallas_call(
        lambda *refs: None,
        in_specs=[place] * (1 + len(others)),
        out_specs=place,
        out_shape=jax.ShapeDtypeStruct(x.shape, x.dtype),
        input_output_aliases={0: 0},
        name="after",
    )(x, *others)


def gate_up_kernel(first, last, mine, other, mine_weights, other_weights, *refs):
    dot = functools.partial(jnp.dot, preferred_element_type=jnp.float32)
    total = dot(mine[...], mine_weights[...]) + dot(other[...], other_weights[...])
    if not first:
        total = total + refs[0][...]
    out = refs[-1]
    if not last:
        out[...] = total
        return
    cols = total.shape[1] // 2
    gate, up = total[:, :cols], total[:, cols:]
    hidden = (gate / (1.0 + jnp.exp(-gate)) * up).astype(jnp.bfloat16)
    proj = refs[-2]
    out[...] = lax.dot_general(
        proj[...], hidden, (((1,), (1,)), ((), ())), preferred_element_type=jnp.float32
    )


def gate_up(mine, other, weights, total, proj):
    rows, depth = mine.shape
    cols = weights[0].shape[1]
    first, last = total is None, proj is not None
    args = [mine, other, *weights]
    args += [] if first else [total]
    args += [proj] if last else []
    vmem = pl.BlockSpec(memory_space=pltpu.VMEM)
    shape = (proj.shape[0], rows) if last else (rows, cols)
    return pl.pallas_call(
        functools.partial(gate_up_kernel, first, last),
        in_specs=[vmem] * len(args),
        out_specs=vmem,
        out_shape=jax.ShapeDtypeStruct(shape, jnp.float32),
        compiler_params=pltpu.CompilerParams(vmem_limit_bytes=24 * 2**20),
        cost_estimate=pl.CostEstimate(
            flops=4 * rows * depth * cols,
            bytes_accessed=4 * rows * depth + 4 * depth * cols,
            transcendentals=rows * cols // 2 if last else 0,
        ),
        name="gate_up",
    )(*args)


def grads_kernel(experts, where, grad_mine, grad_other, docs, routes, *refs):
    same, cross = refs[:experts], refs[experts : 2 * experts]
    out, by_expert = refs[2 * experts :]
    rank = grad_mine.shape[0]
    group = LANES // rank
    long = rank // group
    home = where[0]
    grad = grad_mine[...] + grad_other[...]
    masks = [docs[...] == d for d in range(DOCS_DEV)]
    left = jnp.concatenate(
        [
            jnp.where(mask, grad[q * long : (q + 1) * long], 0.0)
            for q in range(group)
            for mask in masks
        ],
        axis=0,
    )
    for k in range(experts):
        by_expert[lax.rem(home + k, experts)] = same[k][...] + cross[k][...]
    for expert in range(experts):
        named = (routes[0:1, :] == expert) | (routes[1:2, :] == expert)
        codes = jnp.where(named, by_expert[expert], 0.0)
        block = lax.dot_general(
            left,
            codes,
            (((1,), (1,)), ((), ())),
            precision=lax.Precision.HIGHEST,
            preferred_element_type=jnp.float32,
        )
        rows = DOCS_DEV * long
        wide = jnp.concatenate(
            [block[q * rows : (q + 1) * rows] for q in range(group)], axis=1
        )
        for d in range(DOCS_DEV):
            for i in range(long):
                at = d * long + i
                out[d, expert : expert + 1, i * LANES : (i + 1) * LANES] = wide[at : at + 1]


def on_device(tokens, cotangent, routes, doc_ids, gate_weight, up_weight, proj_in, proj_out):
    experts, dats = lax.axis_size("exp"), lax.axis_size("dat")
    home, dat = lax.axis_index("exp"), lax.axis_index("dat")
    core, grp = lax.axis_index("mdl"), lax.axis_index("grp")
    rank, half = proj_in.shape[0], tokens.shape[1]
    swap = [(0, 1), (1, 0)]
    gate, up = gate_weight[0], up_weight[0]

    width = half // CHUNKS
    mine = [[tokens[:, j * width : (j + 1) * width] for j in range(CHUNKS)]]
    ring = [(i, (i + 1) % experts) for i in range(experts)]
    for _ in range(1, experts):
        mine.append([lax.ppermute(x, "exp", ring) for x in mine[-1]])
    other = [[lax.ppermute(x, "mdl", swap) for x in xs] for xs in mine]

    block = gate.shape[0]
    piece = min(block, width)
    held = [[] for _ in range(block // piece)]
    for i, slots in enumerate(held):
        rows = slice(i * piece, (i + 1) * piece)
        gate_own, up_own = gate[rows], up[rows]
        slots.append(jnp.concatenate([gate_own, up_own], axis=1))
        sent = jnp.where(grp == 0, gate_own, up_own)
        for k in range(1, dats):
            direct = lax.ppermute(sent, "dat", [((z + k) % dats, z) for z in range(dats)])
            if dats == 2 and experts > 2 and i < 2:
                direct = after(direct, mine[1][1] if i == 0 else mine[2][0])
            swapped = lax.ppermute(direct, "grp", swap)
            slots.append(
                jnp.concatenate(
                    [
                        jnp.where(grp == 0, direct, swapped),
                        jnp.where(grp == 0, swapped, direct),
                    ],
                    axis=1,
                )
            )

    def rows_of(which, chunk):
        found = []
        for at in range(chunk * width, (chunk + 1) * width, piece):
            slot = (which * (half // block) + at // block - dat) % dats
            slots = held[at % block // piece]
            found.append(lax.select_n(slot == 1 if dats == 2 else slot, *slots))
        return found[0] if len(found) == 1 else jnp.concatenate(found, axis=0)

    weights = [(rows_of(core, j), rows_of(1 - core, j)) for j in range(CHUNKS)]

    group = LANES // rank
    ordered = proj_out.reshape(rank // group, group, half).transpose(1, 0, 2).reshape(rank, half)
    grad_mine = lax.dot_general(
        ordered, cotangent, (((1,), (1,)), ((), ())), preferred_element_type=jnp.float32
    )
    grad_other = lax.ppermute(grad_mine, "mdl", swap)

    same, cross = [], []
    for k in range(experts):
        total = None
        for j in range(CHUNKS):
            last = j == CHUNKS - 1
            total = gate_up(mine[k][j], other[k][j], weights[j], total, proj_in if last else None)
        back = [
            [
                (z * 2 + c, (z - k) % experts * 2 + (c ^ flip))
                for z in range(experts)
                for c in range(2)
            ]
            for flip in range(2)
        ]
        same.append(total if k == 0 else lax.ppermute(total, ("exp", "mdl"), back[0]))
        cross.append(lax.ppermute(total, ("exp", "mdl"), back[1]))

    tok_count = tokens.shape[0]
    vmem = pl.BlockSpec(memory_space=pltpu.VMEM)
    return pl.pallas_call(
        functools.partial(grads_kernel, experts),
        in_specs=[pl.BlockSpec(memory_space=pltpu.SMEM)] + [vmem] * (4 + 2 * experts),
        out_specs=vmem,
        out_shape=jax.ShapeDtypeStruct((DOCS_DEV, experts, rank * rank), jnp.float32),
        scratch_shapes=[pltpu.VMEM((experts, rank, tok_count), jnp.float32)],
        compiler_params=pltpu.CompilerParams(vmem_limit_bytes=24 * 2**20),
        cost_estimate=pl.CostEstimate(
            flops=2 * experts * DOCS_DEV * rank * rank * tok_count,
            bytes_accessed=2**20,
            transcendentals=0,
        ),
        name="doc_grads",
    )(home.reshape(1), grad_mine, grad_other, doc_ids, routes.T, *same, *cross)


def solution(mesh):
    placed = (
        P(("grp", "exp", "dat"), "mdl"),
        P(("grp", "exp", "dat"), "mdl"),
        P(("grp", "exp", "dat"), None),
        P(("grp", "exp", "dat"), None),
        P("exp", "dat", "mdl"),
        P("exp", "dat", "mdl"),
        P(None, "mdl"),
        P(None, "mdl"),
    )
    return jax.shard_map(
        on_device,
        mesh=mesh,
        in_specs=placed,
        out_specs=P(("grp", "exp", "dat"), None, None),
        check_vma=False,
    )
```

time: 128 us -> 101 us (0.79)
  waiting for transfers between devices: 78.8 us -> 52.5 us
  Pallas kernels: 21.7 us -> 13.9 us
  local copies, waits for them, and re-layouts: 0.1 us -> 6.06 us
  other arithmetic: 5.77 us -> 7.13 us
    ppermute x8 -> x9, waiting for transfers between devices: 35.4 us -> 4.08 us  [the longest x3 4.07 us: on_device(): lax.ppermute(total, ('exp', 'mdl'), back[0])]
    pallas_call x8 -> x10, Pallas kernels: 18.1 us -> 12.7 us  [the longest x8 12.7 us: gate_up(): pl.pallas_call(functools.partial(gate_up_kernel, first, last), in_specs=[...]
    ppermute x6, waiting for transfers between devices: 43.4 us -> 48.4 us  [on_device(): mine.append([lax.ppermute(x, 'exp', ring) for x in mine[-1]])]
    slice x0 -> x1, local copies, waits for them, and re-layouts: none -> 3.76 us  [on_device(): gate_own, up_own = (gate[rows], up[rows])]
    pallas_call x1, Pallas kernels: 3.55 us -> 1.28 us  [on_device(): pl.pallas_call(functools.partial(grads_kernel, experts), in_specs=[pl.Blo...]
    ppermute x1 -> x2, starting transfers between devices: 1.77 us -> 3.6 us  [on_device(): swapped = lax.ppermute(direct, 'grp', swap)]
    select_n x2 -> x5, other arithmetic: 5.77 us -> 7.13 us  [the longest x2 3.04 us: on_device(): jnp.where(grp == 0, direct, swapped)]
    slice x1, local copies, waits for them, and re-layouts: 0.07 us -> 1.36 us  [on_device(): mine = [[tokens[:, j * width:(j + 1) * width] for j in range(CHUNKS)]]]
  transfers between devices with their start and end apart: 24 -> 26, of which waited for: 7 -> 7; matrix products, arithmetic and copies ran while one was open for 3% -> 11% of each run, Pallas kernels for 14% -> 13%
where the time goes in v2:
time: 101 us
  waiting for transfers between devices  52.5 us (52%)
  starting transfers between devices  20.6 us (20%)
  Pallas kernels  13.9 us (14%)
  other arithmetic  7.13 us (7%)
  local copies, waits for them, and re-layouts  6.06 us (6%)
    ppermute x6, waiting for transfers between devices, on_device(): mine.append([lax.ppermute(x, 'exp', ring) for x in mine[-1]])  48.4 us
    pallas_call x8, Pallas kernels, gate_up(): pl.pallas_call(functools.partial(gate_up_kernel, first, last), in_specs=[...  12.7 us
    ppermute x4, starting transfers between devices, on_device(): cross.append(lax.ppermute(total, ('exp', 'mdl'), back[1]))  6.09 us
    ppermute x6, starting transfers between devices, on_device(): mine.append([lax.ppermute(x, 'exp', ring) for x in mine[-1]])  6.07 us
    ppermute x3, waiting for transfers between devices, on_device(): lax.ppermute(total, ('exp', 'mdl'), back[0])  4.07 us
    slice x1, local copies, waits for them, and re-layouts, on_device(): gate_own, up_own = (gate[rows], up[rows])  3.76 us
    ppermute x2, starting transfers between devices, on_device(): swapped = lax.ppermute(direct, 'grp', swap)  3.6 us
    ppermute x2, starting transfers between devices, on_device(): lax.ppermute(sent, 'dat', [((z + k) % dats, z) for z in range(dats)])  3.2 us
  transfers between devices with their start and end apart: 26, of which 7 were waited for; matrix products, arithmetic and copies ran while one was open for 11% of the time, Pallas kernels for 13%

profile of v2, /device:TPU:0, one launch (start us, length us, event | category | flops | bytes accessed | tf_op | source)
XLA Modules:
  0.0 100.9 jit_solution(1933706062634910989)
XLA Ops:
  0.0 1.4 %fusion.3 = (bf16[256,1024]{1,0:T(8,128)(2,1)S(1)}, bf16[256,1024]{1,0:T(8,128)(2,1)S(1)}) fusion(bf16[256,2048]{1,0:T(8,128)(2,1)} %param.8), kind=kLoop, calls=%fused_computation.21 | loop fusion | bytes 2097152 | tf_op jit(solution)/shard_map/slice | solution.py:117
  1.4 3.1 %collective-permute-start.3 = (bf16[256,1024]{1,0:T(8,128)(2,1)S(1)}, bf16[256,1024]{1,0:T(8,128)(2,1)}, u32[]{:S(2)}, u32[]{:S(2)}) collective-permute-start(bf16[256,1024]{1,0:T(8,128)(2,1)S(1)} %get-tuple-element.19.mine), channel_id=1, source_target_pairs={{0,4},{4,8},{8,12},{12,0},{1,5},{5,9},{9,13},{13,1},{2,6},{6,10},{... | collective-permute-start | bytes 1572872 | tf_op jit(solution)/shard_map/ppermute | solution.py:120
  4.4 2.9 %broadcast_select_fusion.6 = (bf16[1024,384]{1,0:T(8,128)(2,1)S(1)}, bf16[1024,384]{1,0:T(8,128)(2,1)}) fusion(pred[]{:T(512)S(6)} %eq.22, bf16[1,2048,384]{2,1,0:T(8,128)(2,1)} %param.12, bf16[1,2048,384]{2,1,0:T(8,128)(2,1)} %param.13), kind=kLoop, calls=%fused_computation.14 | loop fusion | flops 786432 | bytes 4718593 | tf_op jit(solution)/shard_map/jit(_where)/select_n | solution.py:130
  7.4 1.5 %collective-permute-start.7 = (bf16[1024,384]{1,0:T(8,128)(2,1)S(1)}, bf16[1024,384]{1,0:T(8,128)(2,1)}, u32[]{:S(2)}, u32[]{:S(2)}) collective-permute-start(bf16[1024,384]{1,0:T(8,128)(2,1)S(1)} %get-tuple-element.7), channel_id=1, source_target_pairs={{2,0},{0,2},{3,1},{1,3},{6,4},{4,6},{7,5},{5,7},{10,8},{8,10},{11,... | collective-permute-start | bytes 2359304 | tf_op jit(solution)/shard_map/ppermute | solution.py:132
  8.9 1.6 %collective-permute-start.8 = (bf16[256,1024]{1,0:T(8,128)(2,1)S(1)}, bf16[256,1024]{1,0:T(8,128)(2,1)S(1)}, u32[]{:S(2)}, u32[]{:S(2)}) collective-permute-start(bf16[256,1024]{1,0:T(8,128)(2,1)S(1)} %get-tuple-element.20.mine), channel_id=1, source_target_pairs={{0,4},{4,8},{8,12},{12,0},{1,5},{5,9},{9,13},{13,1},{2,6},{6,10},{... | collective-permute-start | bytes 1572872 | tf_op jit(solution)/shard_map/ppermute | solution.py:120
  10.4 8.9 %collective-permute-done.3.mine = bf16[256,1024]{1,0:T(8,128)(2,1)} collective-permute-done((bf16[256,1024]{1,0:T(8,128)(2,1)S(1)}, bf16[256,1024]{1,0:T(8,128)(2,1)}, u32[]{:S(2)}, u32[]{:S(2)}) %collective-permute-start.3) | collective-permute-done | bytes 524320 | tf_op jit(solution)/shard_map/ppermute | solution.py:120
  19.3 0.0 collective-permute-start.4
  19.4 1.7 %collective-permute-start.2 = (bf16[1024,384]{1,0:T(8,128)(2,1)}, bf16[1024,384]{1,0:T(8,128)(2,1)}, u32[]{:S(2)}, u32[]{:S(2)}) collective-permute-start(bf16[1024,384]{1,0:T(8,128)(2,1)} %get-tuple-element.8), channel_id=1, source_target_pairs={{2,0},{0,2},{3,1},{1,3},{6,4},{4,6},{7,5},{5,7},{10,8},{8,10},{11,... | collective-permute-start | bytes 2359304 | tf_op jit(solution)/shard_map/ppermute | solution.py:132
  21.1 9.4 %collective-permute-done.8.refs_1_.mine = bf16[256,1024]{1,0:T(8,128)(2,1)S(1)} collective-permute-done((bf16[256,1024]{1,0:T(8,128)(2,1)S(1)}, bf16[256,1024]{1,0:T(8,128)(2,1)S(1)}, u32[]{:S(2)}, u32[]{:S(2)}) %collective-permute-start.8) | collective-permute-done | bytes 524320 | tf_op jit(solution)/shard_map/ppermute | solution.py:120
  30.5 0.8 copy-done.1
  31.2 1.8 %collective-permute-start.9 = (bf16[1024,384]{1,0:T(8,128)(2,1)}, bf16[1024,384]{1,0:T(8,128)(2,1)}, u32[]{:S(2)}, u32[]{:S(2)}) collective-permute-start(bf16[1024,384]{1,0:T(8,128)(2,1)} %after.3), channel_id=1, source_target_pairs={{0,16},{16,0},{1,17},{17,1},{2,18},{18,2},{3,19},{19,3},{4,20},{20... | collective-permute-start | bytes 2359304 | tf_op jit(solution)/shard_map/ppermute | solution.py:135
  33.0 0.1 reshape.14
  33.1 0.1 collective-permute-start.13
  33.1 8.5 %collective-permute-done.4.refs_1_.mine = bf16[256,1024]{1,0:T(8,128)(2,1)S(1)} collective-permute-done((bf16[256,1024]{1,0:T(8,128)(2,1)}, bf16[256,1024]{1,0:T(8,128)(2,1)S(1)}, u32[]{:S(2)}, u32[]{:S(2)}) %collective-permute-start.4) | collective-permute-done | bytes 524320 | tf_op jit(solution)/shard_map/ppermute | solution.py:120
  41.7 3.8 %slice_bitcast_fusion = (bf16[1024,384]{1,0:T(8,128)(2,1)}, bf16[1024,384]{1,0:T(8,128)(2,1)}, bf16[1024,384]{1,0:T(8,128)(2,1)}, bf16[1024,384]{1,0:T(8,128)(2,1)}) fusion(bf16[1,2048,384]{2,1,0:T(8,128)(2,1)} %param.13, bf16[1,2048,384]{2,1,0:T(8,128)(2,1)} %param.12), kind=kLoop, calls=%fused_computation.8 | loop fusion | bytes 6291456 | tf_op jit(solution)/shard_map/slice | solution.py:128
  45.5 1.8 %collective-permute-start.5 = (bf16[1024,384]{1,0:T(8,128)(2,1)}, bf16[1024,384]{1,0:T(8,128)(2,1)}, u32[]{:S(2)}, u32[]{:S(2)}) collective-permute-start(bf16[1024,384]{1,0:T(8,128)(2,1)} %after.2), channel_id=1, source_target_pairs={{0,16},{16,0},{1,17},{17,1},{2,18},{18,2},{3,19},{19,3},{4,20},{20... | collective-permute-start | bytes 2359304 | tf_op jit(solution)/shard_map/ppermute | solution.py:135
  47.3 0.4 fusion.grad_mine
  47.8 4.4 %collective-permute-done.13.mine = bf16[256,1024]{1,0:T(8,128)(2,1)} collective-permute-done((bf16[256,1024]{1,0:T(8,128)(2,1)}, bf16[256,1024]{1,0:T(8,128)(2,1)}, u32[]{:S(2)}, u32[]{:S(2)}) %collective-permute-start.13) | collective-permute-done | bytes 524320 | tf_op jit(solution)/shard_map/ppermute | solution.py:120
  52.2 0.1 collective-permute-start.19
  52.3 1.3 %collective-permute-start.17 = (bf16[256,1024]{1,0:T(8,128)(2,1)}, bf16[256,1024]{1,0:T(8,128)(2,1)S(1)}, u32[]{:S(2)}, u32[]{:S(2)}) collective-permute-start(bf16[256,1024]{1,0:T(8,128)(2,1)} %collective-permute-done.13.mine), channel_id=1, source_target_pairs={{0,4},{4,8},{8,12},{12,0},{1,5},{5,9},{9,13},{13,1},{2,6},{6,10},{... | collective-permute-start | bytes 1572872 | tf_op jit(solution)/shard_map/ppermute | solution.py:120
  53.6 1.5 %broadcast_select_fusion.5 = (bf16[1024,384]{1,0:T(8,128)(2,1)S(1)}, bf16[1024,384]{1,0:T(8,128)(2,1)S(1)}) fusion(bf16[1024,384]{1,0:T(8,128)(2,1)} %after.3, bf16[1024,384]{1,0:T(8,128)(2,1)} %collective-permute-done.9, pred[]{:T(512)S(6)} %eq.22), kind=kLoop, calls=%fused_computation.13 | loop fusion | flops 786432 | bytes 3145729 | tf_op jit(solution)/shard_map/jit(_where)/select_n | solution.py:139
  55.1 0.6 broadcast_select_fusion
  55.7 2.0 %gate_up.12.refs_0_ = f32[256,768]{1,0:T(8,128)S(1)} custom-call(bf16[256,1024]{1,0:T(8,128)(2,1)S(1)} %copy-done.4, bf16[256,1024]{1,0:T(8,128)(2,1)} %collective-permute-done.15.other, bf16[1024,768]{1,0:T(8,128)(2,1)S(1)} %get-tuple-element.6.mine_weights, bf16[1024,768]{1,0:T(8,128)(2,1)S(1)} %get-tuple-element.5.other_weights), custom_call_target="tpu_custom_call" | custom-call | flops 805306368 | bytes 4194304 | tf_op jit(solution)/shard_map/gate_up/pallas_call | solution.py:54
  57.7 0.1 collective-permute-start.1
  57.8 2.0 %gate_up.10.refs_0_ = f32[256,768]{1,0:T(8,128)S(1)} custom-call(bf16[256,1024]{1,0:T(8,128)(2,1)} %collective-permute-done.3.mine, bf16[256,1024]{1,0:T(8,128)(2,1)S(1)} %collective-permute-done.11.other, bf16[1024,768]{1,0:T(8,128)(2,1)S(1)} %get-tuple-element.6.mine_weights, bf16[1024,768]{1,0:T(8,128)(2,1)S(1)} %get-tuple-element.5.other_weights), custom_call_target="tpu_custom_call" | custom-call | flops 805306368 | bytes 4194304 | tf_op jit(solution)/shard_map/gate_up/pallas_call | solution.py:54
  59.9 0.6 collective-permute-start.14
  60.4 2.0 %gate_up.8.refs_0_ = f32[256,768]{1,0:T(8,128)S(1)} custom-call(bf16[256,1024]{1,0:T(8,128)(2,1)S(1)} %get-tuple-element.19.mine, bf16[256,1024]{1,0:T(8,128)(2,1)} %collective-permute-done.6.other, bf16[1024,768]{1,0:T(8,128)(2,1)S(1)} %get-tuple-element.6.mine_weights, bf16[1024,768]{1,0:T(8,128)(2,1)S(1)} %get-tuple-element.5.other_weights), custom_call_target="tpu_custom_call" | custom-call | flops 805306368 | bytes 4194304 | tf_op jit(solution)/shard_map/gate_up/pallas_call | solution.py:54
  62.4 6.3 %collective-permute-done.19.mine = bf16[256,1024]{1,0:T(8,128)(2,1)S(1)} collective-permute-done((bf16[256,1024]{1,0:T(8,128)(2,1)S(1)}, bf16[256,1024]{1,0:T(8,128)(2,1)S(1)}, u32[]{:S(2)}, u32[]{:S(2)}) %collective-permute-start.19) | collective-permute-done | bytes 524320 | tf_op jit(solution)/shard_map/ppermute | solution.py:120
  68.8 10.8 %collective-permute-done.17.mine = bf16[256,1024]{1,0:T(8,128)(2,1)S(1)} collective-permute-done((bf16[256,1024]{1,0:T(8,128)(2,1)}, bf16[256,1024]{1,0:T(8,128)(2,1)S(1)}, u32[]{:S(2)}, u32[]{:S(2)}) %collective-permute-start.17) | collective-permute-done | bytes 524320 | tf_op jit(solution)/shard_map/ppermute | solution.py:120
  79.6 0.5 collective-permute-start.18
  80.1 1.5 %broadcast_select_fusion.8 = (bf16[1024,384]{1,0:T(8,128)(2,1)S(1)}, bf16[1024,384]{1,0:T(8,128)(2,1)S(1)}) fusion(bf16[1024,384]{1,0:T(8,128)(2,1)} %after.2, bf16[1024,384]{1,0:T(8,128)(2,1)} %collective-permute-done.5, pred[]{:T(512)S(6)} %eq.22), kind=kLoop, calls=%fused_computation.16 | loop fusion | flops 786432 | bytes 3145729 | tf_op jit(solution)/shard_map/jit(_where)/select_n | solution.py:139
  81.6 0.6 broadcast_select_fusion.1
  82.3 0.1 collective-permute-start
  82.3 0.0 copy-done.5
  82.4 2.2 %gate_up.13 = f32[32,256]{1,0:T(8,128)S(1)} custom-call(bf16[256,1024]{1,0:T(8,128)(2,1)} %collective-permute-done.13.mine, bf16[256,1024]{1,0:T(8,128)(2,1)S(1)} %collective-permute-done.14.other, bf16[1024,768]{1,0:T(8,128)(2,1)S(1)} %get-tuple-element.10.mine_weights, bf16[1024,768]{1,0:T(8,128)(2,1)S(1)} %get-tuple-element.9.other_weights, ...), custom_call_target="tpu_custom_call" | custom-call | flops 805306368 | bytes 4194304 | tf_op jit(solution)/shard_map/gate_up/pallas_call | solution.py:54
  84.6 0.1 collective-permute-start.16
  84.6 1.2 %gate_up.11 = f32[32,256]{1,0:T(8,128)S(1)} custom-call(bf16[256,1024]{1,0:T(8,128)(2,1)S(1)} %copy-done.2, bf16[256,1024]{1,0:T(8,128)(2,1)S(1)} %collective-permute-done.10.other, bf16[1024,768]{1,0:T(8,128)(2,1)S(1)} %get-tuple-element.10.mine_weights, bf16[1024,768]{1,0:T(8,128)(2,1)S(1)} %get-tuple-element.9.other_weights, ...), custom_call_target="tpu_custom_call" | custom-call | flops 805306368 | bytes 4194304 | tf_op jit(solution)/shard_map/gate_up/pallas_call | solution.py:54
  85.8 2.7 %collective-permute-start.24 = (f32[32,256]{1,0:T(8,128)S(1)}, f32[32,256]{1,0:T(8,128)S(1)}, u32[]{:S(2)}, u32[]{:S(2)}) collective-permute-start(f32[32,256]{1,0:T(8,128)S(1)} %gate_up.13), channel_id=1, source_target_pairs={{0,9},{1,8},{4,13},{5,12},{8,1},{9,0},{12,5},{13,4},{2,11},{3,10},... | collective-permute-start | bytes 98312 | tf_op jit(solution)/shard_map/ppermute | solution.py:178
  88.5 1.2 %gate_up.9.refs_0_ = f32[32,256]{1,0:T(8,128)S(1)} custom-call(bf16[256,1024]{1,0:T(8,128)(2,1)S(1)} %get-tuple-element.20.mine, bf16[256,1024]{1,0:T(8,128)(2,1)S(1)} %collective-permute-done.1.other, bf16[1024,768]{1,0:T(8,128)(2,1)S(1)} %get-tuple-element.10.mine_weights, bf16[1024,768]{1,0:T(8,128)(2,1)S(1)} %get-tuple-element.9.other_weights, ...), custom_call_target="tpu_custom_call" | custom-call | flops 805306368 | bytes 4194304 | tf_op jit(solution)/shard_map/gate_up/pallas_call | solution.py:54
  89.7 0.0 collective-permute-start.12
  89.7 1.0 gate_up.14.refs_0_
  90.7 1.2 %collective-permute-start.23 = (f32[32,256]{1,0:T(8,128)S(1)}, f32[32,256]{1,0:T(8,128)S(1)}, u32[]{:S(2)}, u32[]{:S(2)}) collective-permute-start(f32[32,256]{1,0:T(8,128)S(1)} %gate_up.11), channel_id=1, source_target_pairs={{0,13},{1,12},{4,1},{5,0},{8,5},{9,4},{12,9},{13,8},{2,15},{3,14},... | collective-permute-start | bytes 98312 | tf_op jit(solution)/shard_map/ppermute | solution.py:178
  92.0 1.2 %gate_up.15 = f32[32,256]{1,0:T(8,128)S(1)} custom-call(bf16[256,1024]{1,0:T(8,128)(2,1)S(1)} %collective-permute-done.17.mine, bf16[256,1024]{1,0:T(8,128)(2,1)S(1)} %collective-permute-done.18.other, bf16[1024,768]{1,0:T(8,128)(2,1)S(1)} %get-tuple-element.10.mine_weights, bf16[1024,768]{1,0:T(8,128)(2,1)S(1)} %get-tuple-element.9.other_weights, ...), custom_call_target="tpu_custom_call" | custom-call | flops 805306368 | bytes 4194304 | tf_op jit(solution)/shard_map/gate_up/pallas_call | solution.py:54
  93.1 0.7 collective-permute-start.22
  93.9 0.3 collective-permute-start.21
  94.1 1.4 %collective-permute-start.25 = (f32[32,256]{1,0:T(8,128)S(1)}, f32[32,256]{1,0:T(8,128)S(1)}, u32[]{:S(2)}, u32[]{:S(2)}) collective-permute-start(f32[32,256]{1,0:T(8,128)S(1)} %gate_up.15), channel_id=1, source_target_pairs={{0,5},{1,4},{4,9},{5,8},{8,13},{9,12},{12,1},{13,0},{2,7},{3,6},{6... | collective-permute-start | bytes 98312 | tf_op jit(solution)/shard_map/ppermute | solution.py:178
  95.6 4.1 %collective-permute-done.21.refs_3_ = f32[32,256]{1,0:T(8,128)S(1)} collective-permute-done((f32[32,256]{1,0:T(8,128)S(1)}, f32[32,256]{1,0:T(8,128)S(1)}, u32[]{:S(2)}, u32[]{:S(2)}) %collective-permute-start.21) | collective-permute-done | bytes 32800 | tf_op jit(solution)/shard_map/ppermute | solution.py:177
  99.6 1.3 %doc_grads.1 = f32[4,4,1024]{2,1,0:T(4,128)} custom-call(s32[1]{0:T(128)} %bitcast.where, f32[32,256]{1,0:T(8,128)S(1)} %fusion.grad_mine, f32[32,256]{1,0:T(8,128)S(1)} %collective-permute-done.grad_other, s32[1,256]{1,0:T(1,128)S(1)} %copy-done.7, s32[2,256]{1,0:T(2,128)S(1)} %bitcast.23, f32[32,256]{1,0:T(8,128)S(1)} %gate_up.9.refs_0_, ...), custom_call_target="tpu_custom_call" | custom-call | flops 8388608 | bytes 1048576 | tf_op jit(solution)/shard_map/doc_grads/pallas_call | solution.py:182
  (50 shorter events, 0.1 us)
Async XLA Ops:
  0.0 47.3 %copy-start = (bf16[256,2048]{1,0:T(8,128)(2,1)S(1)}, bf16[256,2048]{1,0:T(8,128)(2,1)}, u32[]{:S(2)}) copy-start(bf16[256,2048]{1,0:T(8,128)(2,1)} %param.9) | copy-start | bytes 3145732
  1.4 18.0 %collective-permute-start.3 = (bf16[256,1024]{1,0:T(8,128)(2,1)S(1)}, bf16[256,1024]{1,0:T(8,128)(2,1)}, u32[]{:S(2)}, u32[]{:S(2)}) collective-permute-start(bf16[256,1024]{1,0:T(8,128)(2,1)S(1)} %get-tuple-element.19.mine), channel_id=1, source_target_pairs={{0,4},{4,8},{8,12},{12,0},{1,5},{5,9},{9,13},{13,1},{2,6},{6,10},{... | collective-permute-start | bytes 1572872 | tf_op jit(solution)/shard_map/ppermute | solution.py:120
  7.4 25.7 %copy-start.12 = (bf16[32,2048]{1,0:T(8,128)(2,1)S(1)}, bf16[32,2048]{1,0:T(8,128)(2,1)}, u32[]{:S(2)}) copy-start(bf16[32,2048]{1,0:T(8,128)(2,1)} %param.15) | copy-start | bytes 393220
  7.4 23.1 %collective-permute-start.7 = (bf16[1024,384]{1,0:T(8,128)(2,1)S(1)}, bf16[1024,384]{1,0:T(8,128)(2,1)}, u32[]{:S(2)}, u32[]{:S(2)}) collective-permute-start(bf16[1024,384]{1,0:T(8,128)(2,1)S(1)} %get-tuple-element.7), channel_id=1, source_target_pairs={{2,0},{0,2},{3,1},{1,3},{6,4},{4,6},{7,5},{5,7},{10,8},{8,10},{11,... | collective-permute-start | bytes 2359304 | tf_op jit(solution)/shard_map/ppermute | solution.py:132
  8.9 21.6 %collective-permute-start.8 = (bf16[256,1024]{1,0:T(8,128)(2,1)S(1)}, bf16[256,1024]{1,0:T(8,128)(2,1)S(1)}, u32[]{:S(2)}, u32[]{:S(2)}) collective-permute-start(bf16[256,1024]{1,0:T(8,128)(2,1)S(1)} %get-tuple-element.20.mine), channel_id=1, source_target_pairs={{0,4},{4,8},{8,12},{12,0},{1,5},{5,9},{9,13},{13,1},{2,6},{6,10},{... | collective-permute-start | bytes 1572872 | tf_op jit(solution)/shard_map/ppermute | solution.py:120
  19.3 22.4 %collective-permute-start.4 = (bf16[256,1024]{1,0:T(8,128)(2,1)}, bf16[256,1024]{1,0:T(8,128)(2,1)S(1)}, u32[]{:S(2)}, u32[]{:S(2)}) collective-permute-start(bf16[256,1024]{1,0:T(8,128)(2,1)} %collective-permute-done.3.mine), channel_id=1, source_target_pairs={{0,4},{4,8},{8,12},{12,0},{1,5},{5,9},{9,13},{13,1},{2,6},{6,10},{... | collective-permute-start | bytes 1572872 | tf_op jit(solution)/shard_map/ppermute | solution.py:120
  19.4 26.1 %collective-permute-start.2 = (bf16[1024,384]{1,0:T(8,128)(2,1)}, bf16[1024,384]{1,0:T(8,128)(2,1)}, u32[]{:S(2)}, u32[]{:S(2)}) collective-permute-start(bf16[1024,384]{1,0:T(8,128)(2,1)} %get-tuple-element.8), channel_id=1, source_target_pairs={{2,0},{0,2},{3,1},{1,3},{6,4},{4,6},{7,5},{5,7},{10,8},{8,10},{11,... | collective-permute-start | bytes 2359304 | tf_op jit(solution)/shard_map/ppermute | solution.py:132
  30.5 0.8 copy-start.1
  31.2 21.0 %collective-permute-start.9 = (bf16[1024,384]{1,0:T(8,128)(2,1)}, bf16[1024,384]{1,0:T(8,128)(2,1)}, u32[]{:S(2)}, u32[]{:S(2)}) collective-permute-start(bf16[1024,384]{1,0:T(8,128)(2,1)} %after.3), channel_id=1, source_target_pairs={{0,16},{16,0},{1,17},{17,1},{2,18},{18,2},{3,19},{19,3},{4,20},{20... | collective-permute-start | bytes 2359304 | tf_op jit(solution)/shard_map/ppermute | solution.py:135
  33.0 26.8 %collective-permute-start.6 = (bf16[256,1024]{1,0:T(8,128)(2,1)S(1)}, bf16[256,1024]{1,0:T(8,128)(2,1)}, u32[]{:S(2)}, u32[]{:S(2)}) collective-permute-start(bf16[256,1024]{1,0:T(8,128)(2,1)S(1)} %get-tuple-element.19.mine), channel_id=1, source_target_pairs={{0,1},{1,0},{2,3},{3,2},{4,5},{5,4},{6,7},{7,6},{8,9},{9,8},{10,11... | collective-permute-start | bytes 1572872 | tf_op jit(solution)/shard_map/ppermute | solution.py:121
  33.1 19.1 %collective-permute-start.13 = (bf16[256,1024]{1,0:T(8,128)(2,1)}, bf16[256,1024]{1,0:T(8,128)(2,1)}, u32[]{:S(2)}, u32[]{:S(2)}) collective-permute-start(bf16[256,1024]{1,0:T(8,128)(2,1)} %copy-done.1), channel_id=1, source_target_pairs={{0,4},{4,8},{8,12},{12,0},{1,5},{5,9},{9,13},{13,1},{2,6},{6,10},{... | collective-permute-start | bytes 1572872 | tf_op jit(solution)/shard_map/ppermute | solution.py:120
  41.7 3.8 %copy-start.3 = (bf16[256,1024]{1,0:T(8,128)(2,1)}, bf16[256,1024]{1,0:T(8,128)(2,1)S(1)}, u32[]{:S(2)}) copy-start(bf16[256,1024]{1,0:T(8,128)(2,1)S(1)} %collective-permute-done.4.refs_1_.mine) | copy-start | bytes 1572868
  41.7 10.5 %collective-permute-start.15 = (bf16[256,1024]{1,0:T(8,128)(2,1)S(1)}, bf16[256,1024]{1,0:T(8,128)(2,1)}, u32[]{:S(2)}, u32[]{:S(2)}) collective-permute-start(bf16[256,1024]{1,0:T(8,128)(2,1)S(1)} %collective-permute-done.4.refs_1_.mine), channel_id=1, source_target_pairs={{0,1},{1,0},{2,3},{3,2},{4,5},{5,4},{6,7},{7,6},{8,9},{9,8},{10,11... | collective-permute-start | bytes 1572872 | tf_op jit(solution)/shard_map/ppermute | solution.py:121
  45.5 6.7 %copy-start.4 = (bf16[256,1024]{1,0:T(8,128)(2,1)S(1)}, bf16[256,1024]{1,0:T(8,128)(2,1)}, u32[]{:S(2)}) copy-start(bf16[256,1024]{1,0:T(8,128)(2,1)} %copy-done.3) | copy-start | bytes 1572868
  45.5 34.1 %collective-permute-start.5 = (bf16[1024,384]{1,0:T(8,128)(2,1)}, bf16[1024,384]{1,0:T(8,128)(2,1)}, u32[]{:S(2)}, u32[]{:S(2)}) collective-permute-start(bf16[1024,384]{1,0:T(8,128)(2,1)} %after.2), channel_id=1, source_target_pairs={{0,16},{16,0},{1,17},{17,1},{2,18},{18,2},{3,19},{19,3},{4,20},{20... | collective-permute-start | bytes 2359304 | tf_op jit(solution)/shard_map/ppermute | solution.py:135
  47.7 7.4 %copy-start.10 = (bf16[1024,384]{1,0:T(8,128)(2,1)S(1)}, bf16[1024,384]{1,0:T(8,128)(2,1)}, u32[]{:S(2)}) copy-start(bf16[1024,384]{1,0:T(8,128)(2,1)} %get-tuple-element.15) | copy-start | bytes 2359300
  47.7 7.3 %copy-start.11 = (bf16[1024,384]{1,0:T(8,128)(2,1)S(1)}, bf16[1024,384]{1,0:T(8,128)(2,1)}, u32[]{:S(2)}) copy-start(bf16[1024,384]{1,0:T(8,128)(2,1)} %get-tuple-element.22) | copy-start | bytes 2359300
  52.2 5.5 %collective-permute-start.11 = (bf16[256,1024]{1,0:T(8,128)(2,1)}, bf16[256,1024]{1,0:T(8,128)(2,1)S(1)}, u32[]{:S(2)}, u32[]{:S(2)}) collective-permute-start(bf16[256,1024]{1,0:T(8,128)(2,1)} %collective-permute-done.3.mine), channel_id=1, source_target_pairs={{0,1},{1,0},{2,3},{3,2},{4,5},{5,4},{6,7},{7,6},{8,9},{9,8},{10,11... | collective-permute-start | bytes 1572872 | tf_op jit(solution)/shard_map/ppermute | solution.py:121
  52.2 16.6 %collective-permute-start.19 = (bf16[256,1024]{1,0:T(8,128)(2,1)S(1)}, bf16[256,1024]{1,0:T(8,128)(2,1)S(1)}, u32[]{:S(2)}, u32[]{:S(2)}) collective-permute-start(bf16[256,1024]{1,0:T(8,128)(2,1)S(1)} %copy-done.4), channel_id=1, source_target_pairs={{0,4},{4,8},{8,12},{12,0},{1,5},{5,9},{9,13},{13,1},{2,6},{6,10},{... | collective-permute-start | bytes 1572872 | tf_op jit(solution)/shard_map/ppermute | solution.py:120
  52.3 27.3 %collective-permute-start.17 = (bf16[256,1024]{1,0:T(8,128)(2,1)}, bf16[256,1024]{1,0:T(8,128)(2,1)S(1)}, u32[]{:S(2)}, u32[]{:S(2)}) collective-permute-start(bf16[256,1024]{1,0:T(8,128)(2,1)} %collective-permute-done.13.mine), channel_id=1, source_target_pairs={{0,4},{4,8},{8,12},{12,0},{1,5},{5,9},{9,13},{13,1},{2,6},{6,10},{... | collective-permute-start | bytes 1572872 | tf_op jit(solution)/shard_map/ppermute | solution.py:120
  57.7 28.1 %collective-permute-start.1 = (bf16[256,1024]{1,0:T(8,128)(2,1)S(1)}, bf16[256,1024]{1,0:T(8,128)(2,1)S(1)}, u32[]{:S(2)}, u32[]{:S(2)}) collective-permute-start(bf16[256,1024]{1,0:T(8,128)(2,1)S(1)} %get-tuple-element.20.mine), channel_id=1, source_target_pairs={{0,1},{1,0},{2,3},{3,2},{4,5},{5,4},{6,7},{7,6},{8,9},{9,8},{10,11... | collective-permute-start | bytes 1572872 | tf_op jit(solution)/shard_map/ppermute | solution.py:121
  59.8 9.0 %copy-start.2 = (bf16[256,1024]{1,0:T(8,128)(2,1)S(1)}, bf16[256,1024]{1,0:T(8,128)(2,1)}, u32[]{:S(2)}) copy-start(bf16[256,1024]{1,0:T(8,128)(2,1)} %copy-done.1) | copy-start | bytes 1572868
  59.9 22.4 %collective-permute-start.14 = (bf16[256,1024]{1,0:T(8,128)(2,1)}, bf16[256,1024]{1,0:T(8,128)(2,1)S(1)}, u32[]{:S(2)}, u32[]{:S(2)}) collective-permute-start(bf16[256,1024]{1,0:T(8,128)(2,1)} %collective-permute-done.13.mine), channel_id=1, source_target_pairs={{0,1},{1,0},{2,3},{3,2},{4,5},{5,4},{6,7},{7,6},{8,9},{9,8},{10,11... | collective-permute-start | bytes 1572872 | tf_op jit(solution)/shard_map/ppermute | solution.py:121
  62.4 19.2 %copy-start.8 = (bf16[1024,384]{1,0:T(8,128)(2,1)S(1)}, bf16[1024,384]{1,0:T(8,128)(2,1)}, u32[]{:S(2)}) copy-start(bf16[1024,384]{1,0:T(8,128)(2,1)} %get-tuple-element.16) | copy-start | bytes 2359300
  62.4 19.2 %copy-start.9 = (bf16[1024,384]{1,0:T(8,128)(2,1)S(1)}, bf16[1024,384]{1,0:T(8,128)(2,1)}, u32[]{:S(2)}) copy-start(bf16[1024,384]{1,0:T(8,128)(2,1)} %get-tuple-element.21) | copy-start | bytes 2359300
  68.8 15.8 %collective-permute-start.10 = (bf16[256,1024]{1,0:T(8,128)(2,1)S(1)}, bf16[256,1024]{1,0:T(8,128)(2,1)S(1)}, u32[]{:S(2)}, u32[]{:S(2)}) collective-permute-start(bf16[256,1024]{1,0:T(8,128)(2,1)S(1)} %copy-done.2), channel_id=1, source_target_pairs={{0,1},{1,0},{2,3},{3,2},{4,5},{5,4},{6,7},{7,6},{8,9},{9,8},{10,11... | collective-permute-start | bytes 1572872 | tf_op jit(solution)/shard_map/ppermute | solution.py:121
  79.6 10.1 %collective-permute-start.20 = (bf16[256,1024]{1,0:T(8,128)(2,1)S(1)}, bf16[256,1024]{1,0:T(8,128)(2,1)S(1)}, u32[]{:S(2)}, u32[]{:S(2)}) collective-permute-start(bf16[256,1024]{1,0:T(8,128)(2,1)S(1)} %collective-permute-done.19.mine), channel_id=1, source_target_pairs={{0,1},{1,0},{2,3},{3,2},{4,5},{5,4},{6,7},{7,6},{8,9},{9,8},{10,11... | collective-permute-start | bytes 1572872 | tf_op jit(solution)/shard_map/ppermute | solution.py:121
  79.6 11.1 %collective-permute-start.18 = (bf16[256,1024]{1,0:T(8,128)(2,1)S(1)}, bf16[256,1024]{1,0:T(8,128)(2,1)S(1)}, u32[]{:S(2)}, u32[]{:S(2)}) collective-permute-start(bf16[256,1024]{1,0:T(8,128)(2,1)S(1)} %collective-permute-done.17.mine), channel_id=1, source_target_pairs={{0,1},{1,0},{2,3},{3,2},{4,5},{5,4},{6,7},{7,6},{8,9},{9,8},{10,11... | collective-permute-start | bytes 1572872 | tf_op jit(solution)/shard_map/ppermute | solution.py:121
  81.6 0.7 copy-start.5
  82.3 10.9 %collective-permute-start = (f32[32,256]{1,0:T(8,128)S(1)}, f32[32,256]{1,0:T(8,128)S(1)}, u32[]{:S(2)}, u32[]{:S(2)}) collective-permute-start(f32[32,256]{1,0:T(8,128)S(1)} %fusion.grad_mine), channel_id=1, source_target_pairs={{0,1},{1,0},{2,3},{3,2},{4,5},{5,4},{6,7},{7,6},{8,9},{9,8},{10,11... | collective-permute-start | bytes 98312 | tf_op jit(solution)/shard_map/ppermute | solution.py:161
  84.6 9.3 %collective-permute-start.16 = (f32[32,256]{1,0:T(8,128)S(1)}, f32[32,256]{1,0:T(8,128)S(1)}, u32[]{:S(2)}, u32[]{:S(2)}) collective-permute-start(f32[32,256]{1,0:T(8,128)S(1)} %gate_up.13), channel_id=1, source_target_pairs={{0,8},{1,9},{4,12},{5,13},{8,0},{9,1},{12,4},{13,5},{2,10},{3,11},... | collective-permute-start | bytes 98312 | tf_op jit(solution)/shard_map/ppermute | solution.py:177
  85.8 8.3 %collective-permute-start.24 = (f32[32,256]{1,0:T(8,128)S(1)}, f32[32,256]{1,0:T(8,128)S(1)}, u32[]{:S(2)}, u32[]{:S(2)}) collective-permute-start(f32[32,256]{1,0:T(8,128)S(1)} %gate_up.13), channel_id=1, source_target_pairs={{0,9},{1,8},{4,13},{5,12},{8,1},{9,0},{12,5},{13,4},{2,11},{3,10},... | collective-permute-start | bytes 98312 | tf_op jit(solution)/shard_map/ppermute | solution.py:178
  89.7 5.9 %collective-permute-start.12 = (f32[32,256]{1,0:T(8,128)S(1)}, f32[32,256]{1,0:T(8,128)S(1)}, u32[]{:S(2)}, u32[]{:S(2)}) collective-permute-start(f32[32,256]{1,0:T(8,128)S(1)} %gate_up.11), channel_id=1, source_target_pairs={{0,12},{1,13},{4,0},{5,1},{8,4},{9,5},{12,8},{13,9},{2,14},{3,15},... | collective-permute-start | bytes 98312 | tf_op jit(solution)/shard_map/ppermute | solution.py:177
  90.7 8.9 %copy-start.6 = (s32[256,2]{0,1:T(2,128)S(1)}, s32[256,2]{0,1:T(2,128)}, u32[]{:S(2)}) copy-start(s32[256,2]{0,1:T(2,128)} %param.10) | copy-start | bytes 6148
  90.7 8.9 %copy-start.7 = (s32[1,256]{1,0:T(1,128)S(1)}, s32[1,256]{1,0:T(1,128)}, u32[]{:S(2)}) copy-start(s32[1,256]{1,0:T(1,128)} %docs.1) | copy-start | bytes 3076
  90.7 4.8 %collective-permute-start.23 = (f32[32,256]{1,0:T(8,128)S(1)}, f32[32,256]{1,0:T(8,128)S(1)}, u32[]{:S(2)}, u32[]{:S(2)}) collective-permute-start(f32[32,256]{1,0:T(8,128)S(1)} %gate_up.11), channel_id=1, source_target_pairs={{0,13},{1,12},{4,1},{5,0},{8,5},{9,4},{12,9},{13,8},{2,15},{3,14},... | collective-permute-start | bytes 98312 | tf_op jit(solution)/shard_map/ppermute | solution.py:178
  93.1 2.4 %collective-permute-start.22 = (f32[32,256]{1,0:T(8,128)S(1)}, f32[32,256]{1,0:T(8,128)S(1)}, u32[]{:S(2)}, u32[]{:S(2)}) collective-permute-start(f32[32,256]{1,0:T(8,128)S(1)} %gate_up.9.refs_0_), channel_id=1, source_target_pairs={{0,1},{1,0},{4,5},{5,4},{8,9},{9,8},{12,13},{13,12},{2,3},{3,2},{6... | collective-permute-start | bytes 98312 | tf_op jit(solution)/shard_map/ppermute | solution.py:178
  93.9 5.8 %collective-permute-start.21 = (f32[32,256]{1,0:T(8,128)S(1)}, f32[32,256]{1,0:T(8,128)S(1)}, u32[]{:S(2)}, u32[]{:S(2)}) collective-permute-start(f32[32,256]{1,0:T(8,128)S(1)} %gate_up.15), channel_id=1, source_target_pairs={{0,4},{1,5},{4,8},{5,9},{8,12},{9,13},{12,0},{13,1},{2,6},{3,7},{6... | collective-permute-start | bytes 98312 | tf_op jit(solution)/shard_map/ppermute | solution.py:177
  94.1 5.5 %collective-permute-start.25 = (f32[32,256]{1,0:T(8,128)S(1)}, f32[32,256]{1,0:T(8,128)S(1)}, u32[]{:S(2)}, u32[]{:S(2)}) collective-permute-start(f32[32,256]{1,0:T(8,128)S(1)} %gate_up.15), channel_id=1, source_target_pairs={{0,5},{1,4},{4,9},{5,8},{8,13},{9,12},{12,1},{13,0},{2,7},{3,6},{6... | collective-permute-start | bytes 98312 | tf_op jit(solution)/shard_map/ppermute | solution.py:178

commit v3 on v2

v3 whole, which is shorter than its diff:
```python
import functools

import jax
import jax.numpy as jnp
from jax import lax
from jax.experimental import pallas as pl
from jax.experimental.pallas import tpu as pltpu
from jax.sharding import PartitionSpec as P

DOCS_DEV = 4
SPLIT = (7, 9)
LANES = 128
GROUP = 3
WAVES = (9, 9, 8, 6)
PIN_BYTES = 24 * 2**20
FREE = pl.CostEstimate(flops=1, bytes_accessed=1, transcendentals=0)


def in_hbm(xs):
    pinned = lax.axis_size("exp") * 2**21 <= PIN_BYTES
    return [pltpu.with_memory_space_constraint(x, pltpu.HBM) if pinned else x for x in xs]


def ordered(turn, arrays, others=(), pin=True):
    hbm = pl.BlockSpec(memory_space=pltpu.HBM)
    kept = [turn, *arrays]
    pin = pin and lax.axis_size("exp") * 2**21 <= PIN_BYTES
    make = pltpu.HBM if pin else jax.ShapeDtypeStruct
    out = pl.pallas_call(
        lambda *refs: None,
        in_specs=[hbm] * len(kept) + [pl.BlockSpec(memory_space=pltpu.VMEM)] * len(others),
        out_specs=[hbm] * len(kept),
        out_shape=[make(x.shape, x.dtype) for x in kept],
        input_output_aliases={i: i for i in range(len(kept))},
        compiler_params=pltpu.CompilerParams(vmem_limit_bytes=2**20),
        name="ordered",
    )(*(in_hbm(kept) if pin else kept), *others)
    return out[0], list(out[1:])


def join_kernel(dats, edges, where, gate, up, *refs):
    pieces = len(edges) - 1
    count = (dats - 1) * pieces
    direct, swapped = refs[:count], refs[count : 2 * count]
    out, sem = refs[2 * count :]
    core, dat, grp = where[0], where[1], where[2]
    cols = gate.shape[1]
    per = dats // 2

    def at(k, i, upper):
        block = lax.rem(dat + k, dats)
        side = jnp.where(lax.div(block, per) == core, 0, 1)
        lanes = pl.ds(pl.multiple_of(upper * cols, LANES), cols)
        rows = pl.ds(edges[i] - edges[0], edges[i + 1] - edges[i])
        return out.at[side * per + lax.rem(block, per), rows, lanes]

    moves = []
    for i in range(pieces):
        rows = pl.ds(edges[i], edges[i + 1] - edges[i])
        moves += [(gate.at[rows], at(0, i, 0)), (up.at[rows], at(0, i, 1))]
        for k in range(1, dats):
            index = i * (dats - 1) + k - 1
            moves += [(direct[index], at(k, i, grp)), (swapped[index], at(k, i, 1 - grp))]
    copies = [pltpu.make_async_copy(a, b, sem.at[i]) for i, (a, b) in enumerate(moves)]
    for copy in copies:
        copy.start()
    for copy in copies:
        copy.wait()


def join(where, gate, up, direct, swapped, dats, edges):
    hbm, vmem = pl.BlockSpec(memory_space=pltpu.HBM), pl.BlockSpec(memory_space=pltpu.VMEM)
    return pl.pallas_call(
        functools.partial(join_kernel, dats, edges),
        in_specs=[pl.BlockSpec(memory_space=pltpu.SMEM)] + [hbm] * (2 + 2 * len(direct)),
        out_specs=vmem,
        out_shape=jax.ShapeDtypeStruct((dats, edges[-1] - edges[0], 2 * gate.shape[1]), gate.dtype),
        scratch_shapes=[pltpu.SemaphoreType.DMA((2 * (len(edges) - 1) * dats,))],
        compiler_params=pltpu.CompilerParams(vmem_limit_bytes=8 * 2**20),
        cost_estimate=FREE,
        name="join",
    )(where, *in_hbm([gate, up, *direct, *swapped]))


def gated(total):
    cols = total.shape[1] // 2
    gate, up = total[:, :cols], total[:, cols:]
    return (gate / (1.0 + jnp.exp(-gate)) * up).astype(jnp.bfloat16)


def segments(low, high, block, cut):
    found, at = [], low
    while at < high:
        start, off = at // block * block, at % block
        part = int(off >= cut)
        end = min(high, start + (block if part else cut))
        found.append((at, end, part, at // block, off - part * cut))
        at = end
    return found


def gate_up_dot(x_of, low, high, size, weights, total=None, parts=(0, 1)):
    per = weights[0].shape[0] // 2
    for start, end, part, block, row in segments(low, high, size, weights[0].shape[1]):
        if part in parts:
            for side in range(2):
                rows = weights[part][side * per + block, row : row + end - start]
                piece = jnp.dot(x_of(side, start, end), rows, preferred_element_type=jnp.float32)
                total = piece if total is None else total + piece
    return total


def codes_of(hidden, proj):
    return lax.dot_general(
        proj[...], hidden, (((1,), (1,)), ((), ())), preferred_element_type=jnp.float32
    )


def shards_kernel(spans, size, first, opened, shards, *refs):
    count = len(spans)
    refs = list(refs)
    sources = [refs.pop(0) for _ in range(2 * count * shards)]
    weights = [refs.pop(0) for _ in range(1 if first else 2)]
    sums = None if first or not opened else refs.pop(0)
    proj = None if first else refs.pop(0)
    out, held_early, held_late, sem = refs
    cut, per = weights[0].shape[1], weights[0].shape[0] // 2

    def copies(n):
        slot, at = n % 2, 0
        taken = (0,) if first else (1,) if n < opened else (0, 1)
        for i, (low, high) in enumerate(spans):
            for start, end, part, block, row in segments(low, high, size, cut):
                for side in range(2) if part in taken else ():
                    place = (side * per + block) * (size - cut if part else cut) + row
                    yield pltpu.make_async_copy(
                        sources[(2 * n + side) * count + i].at[:, pl.ds(start - low, end - start)],
                        (held_early, held_late)[part].at[slot, :, pl.ds(place, end - start)],
                        sem.at[slot, at],
                    )
                    at += 1

    def times(x, part):
        rows = weights[part][...]
        rows = rows.reshape(rows.shape[0] * rows.shape[1], rows.shape[2])
        return jnp.dot(x[...], rows, preferred_element_type=jnp.float32)

    for copy in copies(0):
        copy.start()
    for n in range(shards):
        for copy in copies(n):
            copy.wait()
        if n + 1 < shards:
            for copy in copies(n + 1):
                copy.start()
        if first:
            out[n] = times(held_early.at[n % 2], 0)
        else:
            total = sums[n] if n < opened else times(held_early.at[n % 2], 0)
            out[n] = codes_of(gated(total + times(held_late.at[n % 2], 1)), proj)


def part_kernel(span, size, first, last, mine, other, early, late, *refs):
    x_of = lambda side, start, end: (mine, other)[side][:, start - span[0] : end - span[0]]
    total = gate_up_dot(x_of, *span, size, (early, late), None if first else refs[0][...])
    refs[-1][...] = codes_of(gated(total), refs[-2]) if last else total


def vmem_call(kernel, args, shape, name, far=0, scratch=()):
    vmem, hbm = pl.BlockSpec(memory_space=pltpu.VMEM), pl.BlockSpec(memory_space=pltpu.HBM)
    return pl.pallas_call(
        kernel,
        in_specs=[hbm] * far + [vmem] * (len(args) - far),
        out_specs=vmem,
        out_shape=jax.ShapeDtypeStruct(shape, jnp.float32),
        scratch_shapes=scratch,
        compiler_params=pltpu.CompilerParams(vmem_limit_bytes=20 * 2**20),
        cost_estimate=FREE,
        name=name,
    )(*in_hbm(args[:far]), *args[far:])


def grads_kernel(experts, where, grad_mine, grad_other, docs, routes, *refs):
    codes_of_step, (cross, out, by_expert) = refs[:experts], refs[experts:]
    rank = grad_mine.shape[0]
    group = LANES // rank
    long = rank // group
    home = where[0]
    grad = grad_mine[...] + grad_other[...]
    masks = [docs[...] == d for d in range(DOCS_DEV)]
    left = jnp.concatenate(
        [
            jnp.where(mask, grad[q * long : (q + 1) * long], 0.0)
            for q in range(group)
            for mask in masks
        ],
        axis=0,
    )
    for k in range(experts):
        codes = codes_of_step[k][...]
        by_expert[lax.rem(home + k, experts)] = codes if k < experts - 1 else codes + cross[...]
    for expert in range(experts):
        named = (routes[0:1, :] == expert) | (routes[1:2, :] == expert)
        codes = jnp.where(named, by_expert[expert], 0.0)
        block = lax.dot_general(
            left,
            codes,
            (((1,), (1,)), ((), ())),
            precision=lax.Precision.HIGHEST,
            preferred_element_type=jnp.float32,
        )
        rows = DOCS_DEV * long
        wide = jnp.concatenate(
            [block[q * rows : (q + 1) * rows] for q in range(group)], axis=1
        )
        for d in range(DOCS_DEV):
            for i in range(long):
                at = d * long + i
                out[d, expert : expert + 1, i * LANES : (i + 1) * LANES] = wide[at : at + 1]


def on_device(tokens, cotangent, routes, doc_ids, gate_weight, up_weight, proj_in, proj_out):
    experts, dats = lax.axis_size("exp"), lax.axis_size("dat")
    home, dat = lax.axis_index("exp"), lax.axis_index("dat")
    core, grp = lax.axis_index("mdl"), lax.axis_index("grp")
    rank, half = proj_in.shape[0], tokens.shape[1]
    swap = [(0, 1), (1, 0)]
    gate, up = gate_weight[0], up_weight[0]

    group = LANES // rank
    reordered = proj_out.reshape(rank // group, group, half).transpose(1, 0, 2)
    grad_mine = lax.dot_general(
        reordered.reshape(rank, half),
        cotangent,
        (((1,), (1,)), ((), ())),
        preferred_element_type=jnp.float32,
    )
    grad_other = lax.ppermute(grad_mine, "mdl", swap)

    unit = half // sum(SPLIT)
    edges = [unit * sum(SPLIT[:j]) for j in range(len(SPLIT) + 1)]
    chunks = list(zip(edges, edges[1:]))
    count = len(chunks)
    ring = [(i, (i + 1) % experts) for i in range(experts)]
    held = [tokens[:, low:high] for low, high in chunks]
    mine, other = [held], [[lax.ppermute(x, "mdl", swap) for x in held]]

    block = gate.shape[0]
    row_edges = [0]
    for share in WAVES:
        row_edges.append(row_edges[-1] + block * share // sum(WAVES) // 16 * 16)
    row_edges[-2:] = [row_edges[-2] // LANES * LANES, block]
    sent = [
        jnp.where(grp == 0, gate[low:high], up[low:high])
        for low, high in zip(row_edges, row_edges[1:])
    ]
    waves = [[x] for x in sent]

    def along_dat(xs):
        return [
            lax.ppermute(x, "dat", [((z + k) % dats, z) for z in range(dats)])
            for x in xs
            for k in range(1, dats)
        ]

    def over_grp(xs):
        return [lax.ppermute(x, "grp", swap) for x in xs]

    arriving, swapping = along_dat(waves[0]), []
    direct, swapped = [], []

    turn = jnp.zeros((8, LANES), jnp.float32)
    exchanged, flat, wave = [[], other[0]], [], 0
    for step in range(1, experts):
        moved = [lax.ppermute(x, "exp", ring) for x in mine[-1]]
        mine.append(moved)
        if step == experts - 1:
            break
        for j in range(count):
            wave += 1
            late = waves[wave] if wave < len(waves) else []
            ready = exchanged.pop(0)
            sizes = [1, len(ready), len(arriving), len(swapping), len(late)]
            turn, got = ordered(turn, [moved[j], *ready, *arriving, *swapping, *late])
            got = [got[sum(sizes[:n]) : sum(sizes[: n + 1])] for n in range(len(sizes))]
            moved[j] = got[0][0]
            flat += got[1]
            direct += got[2]
            swapped += got[3]
            swapping, arriving = over_grp(got[2]), along_dat(got[4])
            exchanged.append([lax.ppermute(moved[j], "mdl", swap)])
    where = jnp.stack([core, dat, grp]).astype(jnp.int32)
    some = (len(waves) - 1) * (dats - 1)
    early = join(where, gate, up, direct[:some], swapped[:some], dats, row_edges[:-1])

    def shards_call(low, high, opened, weights, more, shape):
        first = len(weights) == 1
        args = [x for k in range(low, high) for x in (*mine[k], *other[k])]
        cut = row_edges[-2]
        pieces = sum(len(segments(*span, block, cut)) for span in chunks)
        return vmem_call(
            functools.partial(shards_kernel, chunks, block, first, opened, high - low),
            [*args, *weights, *more],
            (high - low, *shape),
            "shards",
            len(args),
            [
                pltpu.VMEM((2, tokens.shape[0], dats * cut), tokens.dtype),
                pltpu.VMEM((2, tokens.shape[0], dats * (block - cut)), tokens.dtype),
                pltpu.SemaphoreType.DMA((2, 2 * pieces)),
            ],
        )

    other = [flat[n : n + count] for n in range(0, len(flat), count)]
    begun = []
    for low in range(0, experts - 2, GROUP):
        high = min(low + GROUP, experts - 2)
        begun.append(
            shards_call(
                low, high, 0, (early,), (), (tokens.shape[0], early.shape[2])
            )
        )

    ready = exchanged.pop(0)
    turn, got = ordered(
        turn, [mine[-1][0], *ready, *swapping], [x[0, :8, :LANES] for x in begun]
    )
    mine[-1][0] = got[0]
    flat += got[1 : 1 + len(ready)] + exchanged.pop(0)
    swapped += got[1 + len(ready) :]
    other = [flat[n : n + count] for n in range(0, len(flat), count)]
    late = join(where, gate, up, direct[some:], swapped[some:], dats, row_edges[-2:])
    weights = (early, late)

    codes = []
    groups = [(n, min(n + GROUP, experts - 2)) for n in range(0, experts - 2, GROUP)]
    for low, high in [*groups, (experts - 2, experts - 1)]:
        opened = min(high, experts - 2) - low
        found = shards_call(
            low,
            high,
            opened,
            weights,
            (*begun[low // GROUP :][: int(opened > 0)], proj_in),
            (rank, tokens.shape[0]),
        )
        found = found + lax.ppermute(found, "mdl", swap)
        for k in range(low, high):
            back = [(z, (z - k) % experts) for z in range(experts)]
            codes.append(found[0] if k == 0 else lax.ppermute(found[k - low], "exp", back))

    made, total = [grad_other, codes[0], found[0]], None
    for j in range(count):
        last = j == count - 1
        turn, (x,) = ordered(turn, [mine[-1][j]], made, False) if j else (turn, [mine[-1][j]])
        args = [x, lax.ppermute(x, "mdl", swap), *weights]
        args += [] if total is None else [total]
        args += [proj_in] if last else []
        total = vmem_call(
            functools.partial(part_kernel, chunks[j], block, total is None, last),
            args,
            (rank, tokens.shape[0]) if last else (tokens.shape[0], early.shape[2]),
            "part",
        )
        made += [total[:8, :LANES]]
    home_pairs = [
        [
            (z * 2 + c, (z + 1) % experts * 2 + (c ^ flip))
            for z in range(experts)
            for c in range(2)
        ]
        for flip in range(2)
    ]
    codes.append(lax.ppermute(total, ("exp", "mdl"), home_pairs[0]))
    cross = lax.ppermute(total, ("exp", "mdl"), home_pairs[1])

    tok_count = tokens.shape[0]
    vmem = pl.BlockSpec(memory_space=pltpu.VMEM)
    return pl.pallas_call(
        functools.partial(grads_kernel, experts),
        in_specs=[pl.BlockSpec(memory_space=pltpu.SMEM)] + [vmem] * (5 + experts),
        out_specs=vmem,
        out_shape=jax.ShapeDtypeStruct((DOCS_DEV, experts, rank * rank), jnp.float32),
        scratch_shapes=[pltpu.VMEM((experts, rank, tok_count), jnp.float32)],
        compiler_params=pltpu.CompilerParams(vmem_limit_bytes=4 * 2**20),
        cost_estimate=pl.CostEstimate(
            flops=2 * experts * DOCS_DEV * rank * rank * tok_count,
            bytes_accessed=2**20,
            transcendentals=0,
        ),
        name="doc_grads",
    )(home.reshape(1), grad_mine, grad_other, doc_ids, routes.T, *codes, cross)


def solution(mesh):
    placed = (
        P(("grp", "exp", "dat"), "mdl"),
        P(("grp", "exp", "dat"), "mdl"),
        P(("grp", "exp", "dat"), None),
        P(("grp", "exp", "dat"), None),
        P("exp", "dat", "mdl"),
        P("exp", "dat", "mdl"),
        P(None, "mdl"),
        P(None, "mdl"),
    )
    return jax.shard_map(
        on_device,
        mesh=mesh,
        in_specs=placed,
        out_specs=P(("grp", "exp", "dat"), None, None),
        check_vma=False,
    )
```

time: 101 us -> 95.9 us (0.950)
  waiting for transfers between devices: 52.5 us -> 32.8 us
  Pallas kernels: 13.9 us -> 20.4 us
  starting transfers between devices: 20.6 us -> 26.6 us
  local copies, waits for them, and re-layouts: 6.06 us -> 8.3 us
    ppermute x25 -> x28, waiting for transfers between devices: 52.5 us -> 32.8 us  [the longest x4 14.7 us: along_dat(): lax.ppermute(x, 'dat', [((z + k) % dats, z) for z in range(dats)])]
    pallas_call x10 -> x13, Pallas kernels: 12.7 us -> 19.1 us  [the longest x5 14.3 us: vmem_call(): pl.pallas_call(kernel, in_specs=[hbm] * far + [vmem] * (len(args) - far),...]
    ppermute x25 -> x28, starting transfers between devices: 20.5 us -> 26.2 us  [the longest x6 6.29 us: on_device(): moved = [lax.ppermute(x, 'exp', ring) for x in mine[-1]]]
    slice x2 -> x3, local copies, waits for them, and re-layouts: 5.12 us -> 1.2 us  [the longest x2 1.2 us: on_device(): held = [tokens[:, low:high] for low, high in chunks]]
    unnamed x26 -> x54, local copies, waits for them, and re-layouts: 0.89 us -> 4.72 us
    reshape x1, local copies, waits for them, and re-layouts: 0.06 us -> 1.74 us  [on_device(): reordered = proj_out.reshape(rank // group, group, half).transpose(1, 0, 2)]
    select_n x5 -> x3, other arithmetic: 7.13 us -> 6.49 us  [on_device(): jnp.where(grp == 0, gate[low:high], up[low:high])]
  transfers between devices with their start and end apart: 26 -> 29, of which waited for: 7 -> 10; matrix products, arithmetic and copies ran while one was open for 11% -> 10% of each run, Pallas kernels for 13% -> 20%
where the time goes in v3:
time: 95.9 us; the launch traced here: 95.5 us
  waiting for transfers between devices  32.8 us (34%)
  starting transfers between devices  26.6 us (28%)
  Pallas kernels  20.4 us (21%)
  local copies, waits for them, and re-layouts  8.3 us (9%)
  other arithmetic  6.58 us (7%)
    ppermute x4, waiting for transfers between devices, along_dat(): lax.ppermute(x, 'dat', [((z + k) % dats, z) for z in range(dats)])  14.7 us
    pallas_call x5, Pallas kernels, vmem_call(): pl.pallas_call(kernel, in_specs=[hbm] * far + [vmem] * (len(args) - far),...  14.3 us
    ppermute x6, waiting for transfers between devices, on_device(): moved = [lax.ppermute(x, 'exp', ring) for x in mine[-1]]  12.8 us
    select_n x3, other arithmetic, on_device(): jnp.where(grp == 0, gate[low:high], up[low:high])  6.49 us
    ppermute x6, starting transfers between devices, on_device(): moved = [lax.ppermute(x, 'exp', ring) for x in mine[-1]]  6.29 us
    ppermute x4, starting transfers between devices, over_grp(): return [lax.ppermute(x, 'grp', swap) for x in xs]  5.98 us
    ppermute x4, starting transfers between devices, along_dat(): lax.ppermute(x, 'dat', [((z + k) % dats, z) for z in range(dats)])  5.96 us
    pallas_call x2, Pallas kernels, join(): pl.pallas_call(functools.partial(join_kernel, dats, edges), in_specs=[pl....  4.89 us
  transfers between devices with their start and end apart: 29, of which 10 were waited for; matrix products, arithmetic and copies ran while one was open for 10% of the time, Pallas kernels for 20%

profile of v3, /device:TPU:0, one launch (start us, length us, event | category | flops | bytes accessed | tf_op | source)
XLA Modules:
  0.0 95.5 jit_solution(9128075239869259808)
XLA Ops:
  0.0 1.1 %slice.50.refs_0_ = bf16[256,896]{1,0:T(8,128)(2,1)S(1)} slice(bf16[256,2048]{1,0:T(8,128)(2,1)} %param.8), slice={[0:256], [0:896]} | slice | bytes 917504 | tf_op jit(solution)/shard_map/slice | solution.py:245
  1.2 3.1 %collective-permute-start.1 = (bf16[256,896]{1,0:T(8,128)(2,1)S(1)}, bf16[256,896]{1,0:T(8,128)(2,1)}, u32[]{:S(2)}, u32[]{:S(2)}) collective-permute-start(bf16[256,896]{1,0:T(8,128)(2,1)S(1)} %slice.50.refs_0_), channel_id=1, source_target_pairs={{0,4},{4,8},{8,12},{12,0},{1,5},{5,9},{9,13},{13,1},{2,6},{6,10},{... | collective-permute-start | bytes 1376264 | tf_op jit(solution)/shard_map/ppermute | solution.py:275
  4.2 2.4 %select_bitcast_fusion = (bf16[576,384]{1,0:T(8,128)(2,1)}, bf16[576,384]{1,0:T(8,128)(2,1)S(1)}) fusion(bf16[1,2048,384]{2,1,0:T(8,128)(2,1)} %param.13, bf16[1,2048,384]{2,1,0:T(8,128)(2,1)} %param.12, pred[]{:T(512)S(6)} %eq.2), kind=kLoop, calls=%fused_computation | loop fusion | flops 442368 | bytes 2654209 | tf_op jit(solution)/shard_map/jit(_where)/select_n | solution.py:254
  6.6 1.5 %collective-permute-start.2 = (bf16[576,384]{1,0:T(8,128)(2,1)S(1)}, bf16[576,384]{1,0:T(8,128)(2,1)S(1)}, u32[]{:S(2)}, u32[]{:S(2)}) collective-permute-start(bf16[576,384]{1,0:T(8,128)(2,1)S(1)} %get-tuple-element.60), channel_id=1, source_target_pairs={{2,0},{0,2},{3,1},{1,3},{6,4},{4,6},{7,5},{5,7},{10,8},{8,10},{11,... | collective-permute-start | bytes 1327112 | tf_op jit(solution)/shard_map/ppermute | solution.py:261
  8.2 1.6 %collective-permute-start.3 = (bf16[256,1152]{1,0:T(8,128)(2,1)S(1)}, bf16[256,1152]{1,0:T(8,128)(2,1)S(1)}, u32[]{:S(2)}, u32[]{:S(2)}) collective-permute-start(bf16[256,1152]{1,0:T(8,128)(2,1)S(1)} %slice.51.refs_1_), channel_id=1, source_target_pairs={{0,4},{4,8},{8,12},{12,0},{1,5},{5,9},{9,13},{13,1},{2,6},{6,10},{... | collective-permute-start | bytes 1769480 | tf_op jit(solution)/shard_map/ppermute | solution.py:275
  9.8 0.5 collective-permute-start.5
  10.3 7.9 %collective-permute-done.2.refs_2_ = bf16[576,384]{1,0:T(8,128)(2,1)S(1)} collective-permute-done((bf16[576,384]{1,0:T(8,128)(2,1)S(1)}, bf16[576,384]{1,0:T(8,128)(2,1)S(1)}, u32[]{:S(2)}, u32[]{:S(2)}) %collective-permute-start.2) | collective-permute-done | bytes 442400 | tf_op jit(solution)/shard_map/ppermute | solution.py:261
  18.2 0.6 broadcast_in_dim.3.refs_0_
  19.0 1.5 %collective-permute-start.6 = (bf16[576,384]{1,0:T(8,128)(2,1)}, bf16[576,384]{1,0:T(8,128)(2,1)S(1)}, u32[]{:S(2)}, u32[]{:S(2)}) collective-permute-start(bf16[576,384]{1,0:T(8,128)(2,1)} %get-tuple-element.33), channel_id=1, source_target_pairs={{2,0},{0,2},{3,1},{1,3},{6,4},{4,6},{7,5},{5,7},{10,8},{8,10},{11,... | collective-permute-start | bytes 1327112 | tf_op jit(solution)/shard_map/ppermute | solution.py:261
  20.5 1.5 %collective-permute-start.7 = (bf16[576,384]{1,0:T(8,128)(2,1)}, bf16[576,384]{1,0:T(8,128)(2,1)S(1)}, u32[]{:S(2)}, u32[]{:S(2)}) collective-permute-start(bf16[576,384]{1,0:T(8,128)(2,1)} %get-tuple-element.34.refs_0_), channel_id=1, source_target_pairs={{0,16},{16,0},{1,17},{17,1},{2,18},{18,2},{3,19},{19,3},{4,20},{20... | collective-permute-start | bytes 1327112 | tf_op jit(solution)/shard_map/ppermute | solution.py:267
  22.0 1.6 %collective-permute-start.8 = (bf16[256,896]{1,0:T(8,128)(2,1)}, bf16[256,896]{1,0:T(8,128)(2,1)S(1)}, u32[]{:S(2)}, u32[]{:S(2)}) collective-permute-start(bf16[256,896]{1,0:T(8,128)(2,1)} %get-tuple-element.37.refs_4_), channel_id=1, source_target_pairs={{0,4},{4,8},{8,12},{12,0},{1,5},{5,9},{9,13},{13,1},{2,6},{6,10},{... | collective-permute-start | bytes 1376264 | tf_op jit(solution)/shard_map/ppermute | solution.py:275
  23.6 6.6 %collective-permute-done.3.refs_1_ = bf16[256,1152]{1,0:T(8,128)(2,1)S(1)} collective-permute-done((bf16[256,1152]{1,0:T(8,128)(2,1)S(1)}, bf16[256,1152]{1,0:T(8,128)(2,1)S(1)}, u32[]{:S(2)}, u32[]{:S(2)}) %collective-permute-start.3) | collective-permute-done | bytes 589856 | tf_op jit(solution)/shard_map/ppermute | solution.py:275
  30.3 2.1 %select_bitcast_fusion.2.refs_6_ = bf16[512,384]{1,0:T(8,128)(2,1)} fusion(bf16[1,2048,384]{2,1,0:T(8,128)(2,1)} %param.13, bf16[1,2048,384]{2,1,0:T(8,128)(2,1)} %param.12, pred[]{:T(512)S(6)} %eq.2), kind=kLoop, calls=%fused_computation.2 | loop fusion | flops 196608 | bytes 1179649 | tf_op jit(solution)/shard_map/jit(_where)/select_n | solution.py:254
  32.4 0.8 copy-done.10
  33.5 1.8 %collective-permute-start.11 = (bf16[576,384]{1,0:T(8,128)(2,1)}, bf16[576,384]{1,0:T(8,128)(2,1)S(1)}, u32[]{:S(2)}, u32[]{:S(2)}) collective-permute-start(bf16[576,384]{1,0:T(8,128)(2,1)} %get-tuple-element.41.refs_1_), channel_id=1, source_target_pairs={{0,16},{16,0},{1,17},{17,1},{2,18},{18,2},{3,19},{19,3},{4,20},{20... | collective-permute-start | bytes 1327112 | tf_op jit(solution)/shard_map/ppermute | solution.py:267
  35.2 1.5 %collective-permute-start.10 = (bf16[512,384]{1,0:T(8,128)(2,1)}, bf16[512,384]{1,0:T(8,128)(2,1)S(1)}, u32[]{:S(2)}, u32[]{:S(2)}) collective-permute-start(bf16[512,384]{1,0:T(8,128)(2,1)} %get-tuple-element.40), channel_id=1, source_target_pairs={{2,0},{0,2},{3,1},{1,3},{6,4},{4,6},{7,5},{5,7},{10,8},{8,10},{11,... | collective-permute-start | bytes 1179656 | tf_op jit(solution)/shard_map/ppermute | solution.py:261
  36.7 2.5 %collective-permute-done.8.refs_1_ = bf16[256,896]{1,0:T(8,128)(2,1)S(1)} collective-permute-done((bf16[256,896]{1,0:T(8,128)(2,1)}, bf16[256,896]{1,0:T(8,128)(2,1)S(1)}, u32[]{:S(2)}, u32[]{:S(2)}) %collective-permute-start.8) | collective-permute-done | bytes 458784 | tf_op jit(solution)/shard_map/ppermute | solution.py:275
  39.3 2.0 %select_bitcast_fusion.3.refs_5_ = bf16[384,384]{1,0:T(8,128)(2,1)} fusion(bf16[1,2048,384]{2,1,0:T(8,128)(2,1)} %param.13, bf16[1,2048,384]{2,1,0:T(8,128)(2,1)} %param.12, pred[]{:T(512)S(6)} %eq.2), kind=kLoop, calls=%fused_computation.3 | loop fusion | flops 147456 | bytes 884737 | tf_op jit(solution)/shard_map/jit(_where)/select_n | solution.py:254
  41.3 5.2 %collective-permute-done.10.refs_3_ = bf16[512,384]{1,0:T(8,128)(2,1)S(1)} collective-permute-done((bf16[512,384]{1,0:T(8,128)(2,1)}, bf16[512,384]{1,0:T(8,128)(2,1)S(1)}, u32[]{:S(2)}, u32[]{:S(2)}) %collective-permute-start.10) | collective-permute-done | bytes 393248 | tf_op jit(solution)/shard_map/ppermute | solution.py:261
  46.5 0.8 copy-done.22
  47.4 1.2 %collective-permute-start.15 = (bf16[512,384]{1,0:T(8,128)(2,1)}, bf16[512,384]{1,0:T(8,128)(2,1)S(1)}, u32[]{:S(2)}, u32[]{:S(2)}) collective-permute-start(bf16[512,384]{1,0:T(8,128)(2,1)} %get-tuple-element.45.refs_2_), channel_id=1, source_target_pairs={{0,16},{16,0},{1,17},{17,1},{2,18},{18,2},{3,19},{19,3},{4,20},{20... | collective-permute-start | bytes 1179656 | tf_op jit(solution)/shard_map/ppermute | solution.py:267
  48.6 1.5 %collective-permute-start.14 = (bf16[384,384]{1,0:T(8,128)(2,1)}, bf16[384,384]{1,0:T(8,128)(2,1)}, u32[]{:S(2)}, u32[]{:S(2)}) collective-permute-start(bf16[384,384]{1,0:T(8,128)(2,1)} %get-tuple-element.44), channel_id=1, source_target_pairs={{2,0},{0,2},{3,1},{1,3},{6,4},{4,6},{7,5},{5,7},{10,8},{8,10},{11,... | collective-permute-start | bytes 884744 | tf_op jit(solution)/shard_map/ppermute | solution.py:261
  50.1 3.7 %collective-permute-done.12.refs_1_ = bf16[256,1152]{1,0:T(8,128)(2,1)S(1)} collective-permute-done((bf16[256,1152]{1,0:T(8,128)(2,1)}, bf16[256,1152]{1,0:T(8,128)(2,1)S(1)}, u32[]{:S(2)}, u32[]{:S(2)}) %collective-permute-start.12) | collective-permute-done | bytes 589856 | tf_op jit(solution)/shard_map/ppermute | solution.py:275
  53.8 1.7 %reshape.26 = bf16[8,4,2048]{2,1,0:T(4,128)(2,1)} reshape(bf16[32,2048]{1,0:T(8,128)(2,1)} %param.15) | data formatting | bytes 262144 | tf_op jit(solution)/shard_map/reshape | solution.py:231
  55.5 1.5 %collective-permute-done.14.refs_3_ = bf16[384,384]{1,0:T(8,128)(2,1)} collective-permute-done((bf16[384,384]{1,0:T(8,128)(2,1)}, bf16[384,384]{1,0:T(8,128)(2,1)}, u32[]{:S(2)}, u32[]{:S(2)}) %collective-permute-start.14) | collective-permute-done | bytes 294944 | tf_op jit(solution)/shard_map/ppermute | solution.py:261
  57.0 0.8 collective-permute-done.15.refs_4_
  57.8 0.8 copy-done.21
  58.6 1.5 %collective-permute-start.18 = (bf16[384,384]{1,0:T(8,128)(2,1)}, bf16[384,384]{1,0:T(8,128)(2,1)S(1)}, u32[]{:S(2)}, u32[]{:S(2)}) collective-permute-start(bf16[384,384]{1,0:T(8,128)(2,1)} %get-tuple-element.50.refs_0_), channel_id=1, source_target_pairs={{0,16},{16,0},{1,17},{17,1},{2,18},{18,2},{3,19},{19,3},{4,20},{20... | collective-permute-start | bytes 884744 | tf_op jit(solution)/shard_map/ppermute | solution.py:267
  60.2 3.1 %join.2.refs_8_.refs_4_.early = bf16[2,1664,768]{2,1,0:T(8,128)(2,1)S(1)} custom-call(s32[3]{0:T(128)S(1)} %pad_add_fusion.where, bf16[2048,384]{1,0:T(8,128)(2,1)} %bitcast.31, bf16[2048,384]{1,0:T(8,128)(2,1)} %bitcast.29, bf16[576,384]{1,0:T(8,128)(2,1)} %get-tuple-element.34.refs_0_, bf16[576,384]{1,0:T(8,128)(2,1)} %get-tuple-element.41.refs_1_, ...), custom_call_target="tpu_custom_call" | custom-call | flops 1 | bytes 1 | tf_op jit(solution)/shard_map/join/pallas_call | solution.py:73
  63.3 5.3 %shards.3.refs_10_ = f32[2,256,768]{2,1,0:T(8,128)S(1)} custom-call(bf16[256,896]{1,0:T(8,128)(2,1)} %copy-done.11, bf16[256,1152]{1,0:T(8,128)(2,1)} %copy-done.8, bf16[256,896]{1,0:T(8,128)(2,1)} %get-tuple-element.35.refs_2_, bf16[256,1152]{1,0:T(8,128)(2,1)} %get-tuple-element.36.refs_3_, bf16[256,896]{1,0:T(8,128)(2,1)} %get-tuple-element.37.refs_4_, ...), custom_call_target="tpu_custom_call" | custom-call | flops 1 | bytes 1 | tf_op jit(solution)/shard_map/shards/pallas_call | solution.py:171
  68.7 0.7 copy-done.1
  69.7 1.8 %join.3.refs_9_.refs_5_.late = bf16[2,384,768]{2,1,0:T(8,128)(2,1)S(1)} custom-call(s32[3]{0:T(128)S(1)} %pad_add_fusion.where, bf16[2048,384]{1,0:T(8,128)(2,1)} %bitcast.32, bf16[2048,384]{1,0:T(8,128)(2,1)} %bitcast.30, bf16[384,384]{1,0:T(8,128)(2,1)} %get-tuple-element.50.refs_0_, bf16[384,384]{1,0:T(8,128)(2,1)} %get-tuple-element.53.refs_1_), custom_call_target="tpu_custom_call" | custom-call | flops 1 | bytes 1 | tf_op jit(solution)/shard_map/join/pallas_call | solution.py:73
  71.5 3.0 %shards.4 = f32[2,32,256]{2,1,0:T(8,128)S(1)} custom-call(bf16[256,896]{1,0:T(8,128)(2,1)} %copy-done.11, bf16[256,1152]{1,0:T(8,128)(2,1)} %copy-done.8, bf16[256,896]{1,0:T(8,128)(2,1)} %get-tuple-element.35.refs_2_, bf16[256,1152]{1,0:T(8,128)(2,1)} %get-tuple-element.36.refs_3_, bf16[256,896]{1,0:T(8,128)(2,1)} %get-tuple-element.37.refs_4_, ...), custom_call_target="tpu_custom_call" | custom-call | flops 1 | bytes 1 | tf_op jit(solution)/shard_map/shards/pallas_call | solution.py:171
  74.5 0.6 collective-permute-start.19
  75.2 0.4 fusion.grad_mine
  75.6 0.5 collective-permute-start
  76.1 0.8 copy-done.25
  76.9 3.6 %shards.5 = f32[1,32,256]{2,1,0:T(8,128)S(1)} custom-call(bf16[256,896]{1,0:T(8,128)(2,1)} %get-tuple-element.52.refs_0_, bf16[256,1152]{1,0:T(8,128)(2,1)} %get-tuple-element.54.refs_1_, bf16[256,896]{1,0:T(8,128)(2,1)} %get-tuple-element.55.refs_2_, bf16[256,1152]{1,0:T(8,128)(2,1)} %copy-done.25, bf16[2,1664,768]{2,1,0:T(8,128)(2,1)S(1)} %join.2.refs_8_.refs_4_.early, ...), custom_call_target="tpu_custom_call" | custom-call | flops 1 | bytes 1 | tf_op jit(solution)/shard_map/shards/pallas_call | solution.py:171
  80.5 0.3 collective-permute-start.22
  80.8 0.9 collective-permute-done.22
  81.8 1.0 %part.2.refs_0_ = f32[256,768]{1,0:T(8,128)S(1)} custom-call(bf16[256,896]{1,0:T(8,128)(2,1)S(1)} %copy-done.2, bf16[256,896]{1,0:T(8,128)(2,1)S(1)} %collective-permute-done.25.other, bf16[2,1664,768]{2,1,0:T(8,128)(2,1)S(1)} %join.2.refs_8_.refs_4_.early, bf16[2,384,768]{2,1,0:T(8,128)(2,1)S(1)} %join.3.refs_9_.refs_5_.late), custom_call_target="tpu_custom_call" | custom-call | flops 1 | bytes 1 | tf_op jit(solution)/shard_map/part/pallas_call | solution.py:171
  83.2 3.6 %collective-permute-start.20 = (f32[32,256]{1,0:T(8,128)S(1)}, f32[32,256]{1,0:T(8,128)S(1)}, u32[]{:S(2)}, u32[]{:S(2)}) collective-permute-start(f32[32,256]{1,0:T(8,128)S(1)} %get-tuple-element.61), channel_id=1, source_target_pairs={{0,12},{4,0},{8,4},{12,8},{1,13},{5,1},{9,5},{13,9},{2,14},{6,2},{... | collective-permute-start | bytes 98312 | tf_op jit(solution)/shard_map/ppermute | solution.py:350
  86.8 1.4 %part.3 = f32[32,256]{1,0:T(8,128)S(1)} custom-call(bf16[256,1152]{1,0:T(8,128)(2,1)S(1)} %get-tuple-element.58.mine, bf16[256,1152]{1,0:T(8,128)(2,1)S(1)} %collective-permute-done.26.other, bf16[2,1664,768]{2,1,0:T(8,128)(2,1)S(1)} %join.2.refs_8_.refs_4_.early, bf16[2,384,768]{2,1,0:T(8,128)(2,1)S(1)} %join.3.refs_9_.refs_5_.late, ...), custom_call_target="tpu_custom_call" | custom-call | flops 1 | bytes 1 | tf_op jit(solution)/shard_map/part/pallas_call | solution.py:171
  88.1 0.6 collective-permute-start.27
  88.7 1.9 %collective-permute-start.28 = (f32[32,256]{1,0:T(8,128)S(1)}, f32[32,256]{1,0:T(8,128)S(1)}, u32[]{:S(2)}, u32[]{:S(2)}) collective-permute-start(f32[32,256]{1,0:T(8,128)S(1)} %part.3), channel_id=1, source_target_pairs={{0,5},{1,4},{4,9},{5,8},{8,13},{9,12},{12,1},{13,0},{2,7},{3,6},{6... | collective-permute-start | bytes 98312 | tf_op jit(solution)/shard_map/ppermute | solution.py:375
  90.7 0.9 collective-permute-done.23.refs_2_
  91.6 2.6 %collective-permute-done.27.refs_3_ = f32[32,256]{1,0:T(8,128)S(1)} collective-permute-done((f32[32,256]{1,0:T(8,128)S(1)}, f32[32,256]{1,0:T(8,128)S(1)}, u32[]{:S(2)}, u32[]{:S(2)}) %collective-permute-start.27) | collective-permute-done | bytes 32800 | tf_op jit(solution)/shard_map/ppermute | solution.py:374
  94.2 1.3 %doc_grads.1 = f32[4,4,1024]{2,1,0:T(4,128)} custom-call(s32[1]{0:T(128)} %bitcast.where, f32[32,256]{1,0:T(8,128)S(1)} %fusion.grad_mine, f32[32,256]{1,0:T(8,128)S(1)} %collective-permute-done.refs_2_.grad_other, s32[1,256]{1,0:T(1,128)S(1)} %copy-done.6, s32[2,256]{1,0:T(2,128)S(1)} %bitcast.28, f32[32,256]{1,0:T(8,128)S(1)} %get-tuple-element.62.refs_3_.refs_0_, ...), custom_call_target="tpu_custom_call" | custom-call | flops 8388608 | bytes 1048576 | tf_op jit(solution)/shard_map/doc_grads/pallas_call | solution.py:379
  (92 shorter events, 1.5 us)
Async XLA Ops:
  0.0 75.2 %copy-start = (bf16[256,2048]{1,0:T(8,128)(2,1)S(1)}, bf16[256,2048]{1,0:T(8,128)(2,1)}, u32[]{:S(2)}) copy-start(bf16[256,2048]{1,0:T(8,128)(2,1)} %param.9) | copy-start | bytes 3145732
  1.1 8.7 %copy-start.11 = (bf16[256,896]{1,0:T(8,128)(2,1)}, bf16[256,896]{1,0:T(8,128)(2,1)S(1)}, u32[]{:S(2)}) copy-start(bf16[256,896]{1,0:T(8,128)(2,1)S(1)} %slice.50.refs_0_) | copy-start | bytes 1376260
  1.2 17.1 %collective-permute-start.1 = (bf16[256,896]{1,0:T(8,128)(2,1)S(1)}, bf16[256,896]{1,0:T(8,128)(2,1)}, u32[]{:S(2)}, u32[]{:S(2)}) collective-permute-start(bf16[256,896]{1,0:T(8,128)(2,1)S(1)} %slice.50.refs_0_), channel_id=1, source_target_pairs={{0,4},{4,8},{8,12},{12,0},{1,5},{5,9},{9,13},{13,1},{2,6},{6,10},{... | collective-permute-start | bytes 1376264 | tf_op jit(solution)/shard_map/ppermute | solution.py:275
  4.2 3.9 %copy-start.24 = (bf16[256,2048]{1,0:T(8,128)(2,1)S(1)}, bf16[256,2048]{1,0:T(8,128)(2,1)}, u32[]{:S(2)}) copy-start(bf16[256,2048]{1,0:T(8,128)(2,1)} %param.8) | copy-start | bytes 3145732
  6.6 11.6 %collective-permute-start.2 = (bf16[576,384]{1,0:T(8,128)(2,1)S(1)}, bf16[576,384]{1,0:T(8,128)(2,1)S(1)}, u32[]{:S(2)}, u32[]{:S(2)}) collective-permute-start(bf16[576,384]{1,0:T(8,128)(2,1)S(1)} %get-tuple-element.60), channel_id=1, source_target_pairs={{2,0},{0,2},{3,1},{1,3},{6,4},{4,6},{7,5},{5,7},{10,8},{8,10},{11,... | collective-permute-start | bytes 1327112 | tf_op jit(solution)/shard_map/ppermute | solution.py:261
  8.2 25.3 %copy-start.8 = (bf16[256,1152]{1,0:T(8,128)(2,1)}, bf16[256,1152]{1,0:T(8,128)(2,1)S(1)}, u32[]{:S(2)}) copy-start(bf16[256,1152]{1,0:T(8,128)(2,1)S(1)} %slice.51.refs_1_) | copy-start | bytes 1769476
  8.2 22.1 %collective-permute-start.3 = (bf16[256,1152]{1,0:T(8,128)(2,1)S(1)}, bf16[256,1152]{1,0:T(8,128)(2,1)S(1)}, u32[]{:S(2)}, u32[]{:S(2)}) collective-permute-start(bf16[256,1152]{1,0:T(8,128)(2,1)S(1)} %slice.51.refs_1_), channel_id=1, source_target_pairs={{0,4},{4,8},{8,12},{12,0},{1,5},{5,9},{9,13},{13,1},{2,6},{6,10},{... | collective-permute-start | bytes 1769480 | tf_op jit(solution)/shard_map/ppermute | solution.py:275
  9.8 12.2 %collective-permute-start.4 = (bf16[256,896]{1,0:T(8,128)(2,1)S(1)}, bf16[256,896]{1,0:T(8,128)(2,1)S(1)}, u32[]{:S(2)}, u32[]{:S(2)}) collective-permute-start(bf16[256,896]{1,0:T(8,128)(2,1)S(1)} %slice.50.refs_0_), channel_id=1, source_target_pairs={{0,1},{1,0},{2,3},{3,2},{4,5},{5,4},{6,7},{7,6},{8,9},{9,8},{10,11... | collective-permute-start | bytes 1376264 | tf_op jit(solution)/shard_map/ppermute | solution.py:246
  9.8 22.6 %collective-permute-start.5 = (bf16[256,1152]{1,0:T(8,128)(2,1)S(1)}, bf16[256,1152]{1,0:T(8,128)(2,1)S(1)}, u32[]{:S(2)}, u32[]{:S(2)}) collective-permute-start(bf16[256,1152]{1,0:T(8,128)(2,1)S(1)} %slice.51.refs_1_), channel_id=1, source_target_pairs={{0,1},{1,0},{2,3},{3,2},{4,5},{5,4},{6,7},{7,6},{8,9},{9,8},{10,11... | collective-permute-start | bytes 1769480 | tf_op jit(solution)/shard_map/ppermute | solution.py:246
  19.0 13.4 %collective-permute-start.6 = (bf16[576,384]{1,0:T(8,128)(2,1)}, bf16[576,384]{1,0:T(8,128)(2,1)S(1)}, u32[]{:S(2)}, u32[]{:S(2)}) collective-permute-start(bf16[576,384]{1,0:T(8,128)(2,1)} %get-tuple-element.33), channel_id=1, source_target_pairs={{2,0},{0,2},{3,1},{1,3},{6,4},{4,6},{7,5},{5,7},{10,8},{8,10},{11,... | collective-permute-start | bytes 1327112 | tf_op jit(solution)/shard_map/ppermute | solution.py:261
  20.5 11.9 %collective-permute-start.7 = (bf16[576,384]{1,0:T(8,128)(2,1)}, bf16[576,384]{1,0:T(8,128)(2,1)S(1)}, u32[]{:S(2)}, u32[]{:S(2)}) collective-permute-start(bf16[576,384]{1,0:T(8,128)(2,1)} %get-tuple-element.34.refs_0_), channel_id=1, source_target_pairs={{0,16},{16,0},{1,17},{17,1},{2,18},{18,2},{3,19},{19,3},{4,20},{20... | collective-permute-start | bytes 1327112 | tf_op jit(solution)/shard_map/ppermute | solution.py:267
  22.0 10.4 %copy-start.12 = (bf16[256,896]{1,0:T(8,128)(2,1)}, bf16[256,896]{1,0:T(8,128)(2,1)S(1)}, u32[]{:S(2)}) copy-start(bf16[256,896]{1,0:T(8,128)(2,1)S(1)} %collective-permute-done.4.refs_2_) | copy-start | bytes 1376260
  22.0 17.2 %collective-permute-start.8 = (bf16[256,896]{1,0:T(8,128)(2,1)}, bf16[256,896]{1,0:T(8,128)(2,1)S(1)}, u32[]{:S(2)}, u32[]{:S(2)}) collective-permute-start(bf16[256,896]{1,0:T(8,128)(2,1)} %get-tuple-element.37.refs_4_), channel_id=1, source_target_pairs={{0,4},{4,8},{8,12},{12,0},{1,5},{5,9},{9,13},{13,1},{2,6},{6,10},{... | collective-permute-start | bytes 1376264 | tf_op jit(solution)/shard_map/ppermute | solution.py:275
  30.3 2.2 %copy-start.9 = (bf16[256,1152]{1,0:T(8,128)(2,1)}, bf16[256,1152]{1,0:T(8,128)(2,1)S(1)}, u32[]{:S(2)}) copy-start(bf16[256,1152]{1,0:T(8,128)(2,1)S(1)} %collective-permute-done.3.refs_1_) | copy-start | bytes 1769476
  30.3 11.0 %collective-permute-start.9 = (bf16[256,896]{1,0:T(8,128)(2,1)}, bf16[256,896]{1,0:T(8,128)(2,1)S(1)}, u32[]{:S(2)}, u32[]{:S(2)}) collective-permute-start(bf16[256,896]{1,0:T(8,128)(2,1)} %get-tuple-element.37.refs_4_), channel_id=1, source_target_pairs={{0,1},{1,0},{2,3},{3,2},{4,5},{5,4},{6,7},{7,6},{8,9},{9,8},{10,11... | collective-permute-start | bytes 1376264 | tf_op jit(solution)/shard_map/ppermute | solution.py:291
  32.4 1.0 %copy-start.19 = (bf16[576,384]{1,0:T(8,128)(2,1)}, bf16[576,384]{1,0:T(8,128)(2,1)S(1)}, u32[]{:S(2)}) copy-start(bf16[576,384]{1,0:T(8,128)(2,1)S(1)} %collective-permute-done.6.refs_4_) | copy-start | bytes 1327108
  32.4 1.1 %copy-start.20 = (bf16[576,384]{1,0:T(8,128)(2,1)}, bf16[576,384]{1,0:T(8,128)(2,1)S(1)}, u32[]{:S(2)}) copy-start(bf16[576,384]{1,0:T(8,128)(2,1)S(1)} %collective-permute-done.7.refs_5_) | copy-start | bytes 1327108
  33.5 13.0 %collective-permute-start.11 = (bf16[576,384]{1,0:T(8,128)(2,1)}, bf16[576,384]{1,0:T(8,128)(2,1)S(1)}, u32[]{:S(2)}, u32[]{:S(2)}) collective-permute-start(bf16[576,384]{1,0:T(8,128)(2,1)} %get-tuple-element.41.refs_1_), channel_id=1, source_target_pairs={{0,16},{16,0},{1,17},{17,1},{2,18},{18,2},{3,19},{19,3},{4,20},{20... | collective-permute-start | bytes 1327112 | tf_op jit(solution)/shard_map/ppermute | solution.py:267
  35.2 11.2 %collective-permute-start.10 = (bf16[512,384]{1,0:T(8,128)(2,1)}, bf16[512,384]{1,0:T(8,128)(2,1)S(1)}, u32[]{:S(2)}, u32[]{:S(2)}) collective-permute-start(bf16[512,384]{1,0:T(8,128)(2,1)} %get-tuple-element.40), channel_id=1, source_target_pairs={{2,0},{0,2},{3,1},{1,3},{6,4},{4,6},{7,5},{5,7},{10,8},{8,10},{11,... | collective-permute-start | bytes 1179656 | tf_op jit(solution)/shard_map/ppermute | solution.py:261
  36.7 17.0 %collective-permute-start.12 = (bf16[256,1152]{1,0:T(8,128)(2,1)}, bf16[256,1152]{1,0:T(8,128)(2,1)S(1)}, u32[]{:S(2)}, u32[]{:S(2)}) collective-permute-start(bf16[256,1152]{1,0:T(8,128)(2,1)} %get-tuple-element.38.refs_5_), channel_id=1, source_target_pairs={{0,4},{4,8},{8,12},{12,0},{1,5},{5,9},{9,13},{13,1},{2,6},{6,10},{... | collective-permute-start | bytes 1769480 | tf_op jit(solution)/shard_map/ppermute | solution.py:275
  39.3 7.2 %copy-start.16 = (bf16[256,896]{1,0:T(8,128)(2,1)}, bf16[256,896]{1,0:T(8,128)(2,1)S(1)}, u32[]{:S(2)}) copy-start(bf16[256,896]{1,0:T(8,128)(2,1)S(1)} %collective-permute-done.8.refs_1_) | copy-start | bytes 1376260
  39.3 16.2 %collective-permute-start.13 = (bf16[256,1152]{1,0:T(8,128)(2,1)}, bf16[256,1152]{1,0:T(8,128)(2,1)S(1)}, u32[]{:S(2)}, u32[]{:S(2)}) collective-permute-start(bf16[256,1152]{1,0:T(8,128)(2,1)} %get-tuple-element.38.refs_5_), channel_id=1, source_target_pairs={{0,1},{1,0},{2,3},{3,2},{4,5},{5,4},{6,7},{7,6},{8,9},{9,8},{10,11... | collective-permute-start | bytes 1769480 | tf_op jit(solution)/shard_map/ppermute | solution.py:291
  41.3 5.2 %copy-start.13 = (bf16[256,896]{1,0:T(8,128)(2,1)}, bf16[256,896]{1,0:T(8,128)(2,1)S(1)}, u32[]{:S(2)}) copy-start(bf16[256,896]{1,0:T(8,128)(2,1)S(1)} %collective-permute-done.9.refs_2_) | copy-start | bytes 1376260
  47.4 10.4 %collective-permute-start.15 = (bf16[512,384]{1,0:T(8,128)(2,1)}, bf16[512,384]{1,0:T(8,128)(2,1)S(1)}, u32[]{:S(2)}, u32[]{:S(2)}) collective-permute-start(bf16[512,384]{1,0:T(8,128)(2,1)} %get-tuple-element.45.refs_2_), channel_id=1, source_target_pairs={{0,16},{16,0},{1,17},{17,1},{2,18},{18,2},{3,19},{19,3},{4,20},{20... | collective-permute-start | bytes 1179656 | tf_op jit(solution)/shard_map/ppermute | solution.py:267
  48.6 8.4 %collective-permute-start.14 = (bf16[384,384]{1,0:T(8,128)(2,1)}, bf16[384,384]{1,0:T(8,128)(2,1)}, u32[]{:S(2)}, u32[]{:S(2)}) collective-permute-start(bf16[384,384]{1,0:T(8,128)(2,1)} %get-tuple-element.44), channel_id=1, source_target_pairs={{2,0},{0,2},{3,1},{1,3},{6,4},{4,6},{7,5},{5,7},{10,8},{8,10},{11,... | collective-permute-start | bytes 884744 | tf_op jit(solution)/shard_map/ppermute | solution.py:261
  50.1 18.6 %collective-permute-start.16 = (bf16[256,896]{1,0:T(8,128)(2,1)}, bf16[256,896]{1,0:T(8,128)(2,1)S(1)}, u32[]{:S(2)}, u32[]{:S(2)}) collective-permute-start(bf16[256,896]{1,0:T(8,128)(2,1)} %get-tuple-element.52.refs_0_), channel_id=1, source_target_pairs={{0,4},{4,8},{8,12},{12,0},{1,5},{5,9},{9,13},{13,1},{2,6},{6,10},{... | collective-permute-start | bytes 1376264 | tf_op jit(solution)/shard_map/ppermute | solution.py:275
  53.7 4.1 %copy-start.14 = (bf16[256,1152]{1,0:T(8,128)(2,1)}, bf16[256,1152]{1,0:T(8,128)(2,1)S(1)}, u32[]{:S(2)}) copy-start(bf16[256,1152]{1,0:T(8,128)(2,1)S(1)} %collective-permute-done.12.refs_1_) | copy-start | bytes 1769476
  53.7 14.9 %collective-permute-start.17 = (bf16[256,896]{1,0:T(8,128)(2,1)}, bf16[256,896]{1,0:T(8,128)(2,1)S(1)}, u32[]{:S(2)}, u32[]{:S(2)}) collective-permute-start(bf16[256,896]{1,0:T(8,128)(2,1)} %get-tuple-element.52.refs_0_), channel_id=1, source_target_pairs={{0,1},{1,0},{2,3},{3,2},{4,5},{5,4},{6,7},{7,6},{8,9},{9,8},{10,11... | collective-permute-start | bytes 1376264 | tf_op jit(solution)/shard_map/ppermute | solution.py:291
  55.5 2.3 %copy-start.7 = (bf16[256,1152]{1,0:T(8,128)(2,1)}, bf16[256,1152]{1,0:T(8,128)(2,1)S(1)}, u32[]{:S(2)}) copy-start(bf16[256,1152]{1,0:T(8,128)(2,1)S(1)} %collective-permute-done.13.refs_2_) | copy-start | bytes 1769476
  58.6 10.1 %collective-permute-start.18 = (bf16[384,384]{1,0:T(8,128)(2,1)}, bf16[384,384]{1,0:T(8,128)(2,1)S(1)}, u32[]{:S(2)}, u32[]{:S(2)}) collective-permute-start(bf16[384,384]{1,0:T(8,128)(2,1)} %get-tuple-element.50.refs_0_), channel_id=1, source_target_pairs={{0,16},{16,0},{1,17},{17,1},{2,18},{18,2},{3,19},{19,3},{4,20},{20... | collective-permute-start | bytes 884744 | tf_op jit(solution)/shard_map/ppermute | solution.py:267
  60.1 16.0 %collective-permute-start.21 = (bf16[256,1152]{1,0:T(8,128)(2,1)}, bf16[256,1152]{1,0:T(8,128)(2,1)S(1)}, u32[]{:S(2)}, u32[]{:S(2)}) collective-permute-start(bf16[256,1152]{1,0:T(8,128)(2,1)} %get-tuple-element.54.refs_1_), channel_id=1, source_target_pairs={{0,1},{1,0},{2,3},{3,2},{4,5},{5,4},{6,7},{7,6},{8,9},{9,8},{10,11... | collective-permute-start | bytes 1769480 | tf_op jit(solution)/shard_map/ppermute | solution.py:291
  60.2 22.7 %collective-permute-start.24 = (bf16[256,1152]{1,0:T(8,128)(2,1)}, bf16[256,1152]{1,0:T(8,128)(2,1)S(1)}, u32[]{:S(2)}, u32[]{:S(2)}) collective-permute-start(bf16[256,1152]{1,0:T(8,128)(2,1)} %get-tuple-element.54.refs_1_), channel_id=1, source_target_pairs={{0,4},{4,8},{8,12},{12,0},{1,5},{5,9},{9,13},{13,1},{2,6},{6,10},{... | collective-permute-start | bytes 1769480 | tf_op jit(solution)/shard_map/ppermute | solution.py:275
  68.7 1.0 %copy-start.23 = (bf16[384,384]{1,0:T(8,128)(2,1)}, bf16[384,384]{1,0:T(8,128)(2,1)S(1)}, u32[]{:S(2)}) copy-start(bf16[384,384]{1,0:T(8,128)(2,1)S(1)} %collective-permute-done.18.refs_3_) | copy-start | bytes 884740
  69.7 1.8 %copy-start.3 = (bf16[32,384]{1,0:T(8,128)(2,1)S(1)}, bf16[32,384]{1,0:T(8,128)(2,1)}, u32[]{:S(2)}) copy-start(bf16[32,384]{1,0:T(8,128)(2,1)} %refs_1_.1) | copy-start | bytes 73732
  71.5 3.6 %copy-start.2 = (bf16[256,896]{1,0:T(8,128)(2,1)S(1)}, bf16[256,896]{1,0:T(8,128)(2,1)}, u32[]{:S(2)}) copy-start(bf16[256,896]{1,0:T(8,128)(2,1)} %get-tuple-element.57.mine) | copy-start | bytes 1376260
  71.5 3.6 %copy-start.26 = (bf16[8,4,2048]{2,1,0:T(4,128)(2,1)S(1)}, bf16[8,4,2048]{2,1,0:T(4,128)(2,1)}, u32[]{:S(2)}) copy-start(bf16[8,4,2048]{2,1,0:T(4,128)(2,1)} %reshape.26) | copy-start | bytes 393220
  74.5 1.6 %collective-permute-start.19 = (f32[2,32,256]{2,1,0:T(8,128)S(1)}, f32[2,32,256]{2,1,0:T(8,128)S(1)}, u32[]{:S(2)}, u32[]{:S(2)}) collective-permute-start(f32[2,32,256]{2,1,0:T(8,128)S(1)} %shards.4), channel_id=1, source_target_pairs={{0,1},{1,0},{2,3},{3,2},{4,5},{5,4},{6,7},{7,6},{8,9},{9,8},{10,11... | collective-permute-start | bytes 196616 | tf_op jit(solution)/shard_map/ppermute | solution.py:347
  75.1 6.7 %collective-permute-start.25 = (bf16[256,896]{1,0:T(8,128)(2,1)S(1)}, bf16[256,896]{1,0:T(8,128)(2,1)S(1)}, u32[]{:S(2)}, u32[]{:S(2)}) collective-permute-start(bf16[256,896]{1,0:T(8,128)(2,1)S(1)} %copy-done.2), channel_id=1, source_target_pairs={{0,1},{1,0},{2,3},{3,2},{4,5},{5,4},{6,7},{7,6},{8,9},{9,8},{10,11... | collective-permute-start | bytes 1376264 | tf_op jit(solution)/shard_map/ppermute | solution.py:356
  75.6 7.2 %collective-permute-start = (f32[32,256]{1,0:T(8,128)S(1)}, f32[32,256]{1,0:T(8,128)S(1)}, u32[]{:S(2)}, u32[]{:S(2)}) collective-permute-start(f32[32,256]{1,0:T(8,128)S(1)} %fusion.grad_mine), channel_id=1, source_target_pairs={{0,1},{1,0},{2,3},{3,2},{4,5},{5,4},{6,7},{7,6},{8,9},{9,8},{10,11... | collective-permute-start | bytes 98312 | tf_op jit(solution)/shard_map/ppermute | solution.py:238
  80.5 1.3 %collective-permute-start.22 = (f32[1,32,256]{2,1,0:T(8,128)S(1)}, f32[1,32,256]{2,1,0:T(8,128)S(1)}, u32[]{:S(2)}, u32[]{:S(2)}) collective-permute-start(f32[1,32,256]{2,1,0:T(8,128)S(1)} %shards.5), channel_id=1, source_target_pairs={{0,1},{1,0},{2,3},{3,2},{4,5},{5,4},{6,7},{7,6},{8,9},{9,8},{10,11... | collective-permute-start | bytes 98312 | tf_op jit(solution)/shard_map/ppermute | solution.py:347
  81.8 1.0 %copy-start.4 = (f32[8,128]{1,0:T(8,128)S(1)}, f32[8,128]{1,0:T(8,128)}, u32[]{:S(2)}) copy-start(f32[8,128]{1,0:T(8,128)} %get-tuple-element.56.refs_0_) | copy-start | bytes 12292
  82.9 3.9 %collective-permute-start.26 = (bf16[256,1152]{1,0:T(8,128)(2,1)S(1)}, bf16[256,1152]{1,0:T(8,128)(2,1)S(1)}, u32[]{:S(2)}, u32[]{:S(2)}) collective-permute-start(bf16[256,1152]{1,0:T(8,128)(2,1)S(1)} %get-tuple-element.58.mine), channel_id=1, source_target_pairs={{0,1},{1,0},{2,3},{3,2},{4,5},{5,4},{6,7},{7,6},{8,9},{9,8},{10,11... | collective-permute-start | bytes 1769480 | tf_op jit(solution)/shard_map/ppermute | solution.py:356
  83.2 11.0 %copy-start.5 = (s32[256,2]{0,1:T(2,128)S(1)}, s32[256,2]{0,1:T(2,128)}, u32[]{:S(2)}) copy-start(s32[256,2]{0,1:T(2,128)} %param.10) | copy-start | bytes 6148
  83.2 11.0 %copy-start.6 = (s32[1,256]{1,0:T(1,128)S(1)}, s32[1,256]{1,0:T(1,128)}, u32[]{:S(2)}) copy-start(s32[1,256]{1,0:T(1,128)} %docs.1) | copy-start | bytes 3076
  83.2 7.5 %collective-permute-start.20 = (f32[32,256]{1,0:T(8,128)S(1)}, f32[32,256]{1,0:T(8,128)S(1)}, u32[]{:S(2)}, u32[]{:S(2)}) collective-permute-start(f32[32,256]{1,0:T(8,128)S(1)} %get-tuple-element.61), channel_id=1, source_target_pairs={{0,12},{4,0},{8,4},{12,8},{1,13},{5,1},{9,5},{13,9},{2,14},{6,2},{... | collective-permute-start | bytes 98312 | tf_op jit(solution)/shard_map/ppermute | solution.py:350
  86.7 4.8 %collective-permute-start.23 = (f32[32,256]{1,0:T(8,128)S(1)}, f32[32,256]{1,0:T(8,128)S(1)}, u32[]{:S(2)}, u32[]{:S(2)}) collective-permute-start(f32[32,256]{1,0:T(8,128)S(1)} %add_bitcast_fusion.refs_4_), channel_id=1, source_target_pairs={{0,8},{4,12},{8,0},{12,4},{1,9},{5,13},{9,1},{13,5},{2,10},{6,14},... | collective-permute-start | bytes 98312 | tf_op jit(solution)/shard_map/ppermute | solution.py:350
  88.1 6.1 %collective-permute-start.27 = (f32[32,256]{1,0:T(8,128)S(1)}, f32[32,256]{1,0:T(8,128)S(1)}, u32[]{:S(2)}, u32[]{:S(2)}) collective-permute-start(f32[32,256]{1,0:T(8,128)S(1)} %part.3), channel_id=1, source_target_pairs={{0,4},{1,5},{4,8},{5,9},{8,12},{9,13},{12,0},{13,1},{2,6},{3,7},{6... | collective-permute-start | bytes 98312 | tf_op jit(solution)/shard_map/ppermute | solution.py:374
  88.7 5.5 %collective-permute-start.28 = (f32[32,256]{1,0:T(8,128)S(1)}, f32[32,256]{1,0:T(8,128)S(1)}, u32[]{:S(2)}, u32[]{:S(2)}) collective-permute-start(f32[32,256]{1,0:T(8,128)S(1)} %part.3), channel_id=1, source_target_pairs={{0,5},{1,4},{4,9},{5,8},{8,13},{9,12},{12,1},{13,0},{2,7},{3,6},{6... | collective-permute-start | bytes 98312 | tf_op jit(solution)/shard_map/ppermute | solution.py:375
  (8 other events, 6.6 us)

commit v4 on v3

--- a/solution.py
+++ b/solution.py
@@ -12,6 +12,7 @@
 LANES = 128
 GROUP = 3
 WAVES = (9, 9, 8, 6)
+CUTS = (3, 4)
 PIN_BYTES = 24 * 2**20
 FREE = pl.CostEstimate(flops=1, bytes_accessed=1, transcendentals=0)
 
@@ -88,26 +89,15 @@
     return (gate / (1.0 + jnp.exp(-gate)) * up).astype(jnp.bfloat16)
 
 
-def segments(low, high, block, cut):
-    found, at = [], low
+def segments(low, high, cuts):
+    found, at, size = [], low, cuts[-1]
     while at < high:
-        start, off = at // block * block, at % block
-        part = int(off >= cut)
-        end = min(high, start + (block if part else cut))
-        found.append((at, end, part, at // block, off - part * cut))
+        start, off = at // size * size, at % size
+        part = sum(off >= cut for cut in cuts)
+        end = min(high, start + cuts[part])
+        found.append((at, end, part, at // size, off - (cuts[part - 1] if part else 0)))
         at = end
     return found
-
-
-def gate_up_dot(x_of, low, high, size, weights, total=None, parts=(0, 1)):
-    per = weights[0].shape[0] // 2
-    for start, end, part, block, row in segments(low, high, size, weights[0].shape[1]):
-        if part in parts:
-            for side in range(2):
-                rows = weights[part][side * per + block, row : row + end - start]
-                piece = jnp.dot(x_of(side, start, end), rows, preferred_element_type=jnp.float32)
-                total = piece if total is None else total + piece
-    return total
 
 
 def codes_of(hidden, proj):
@@ -116,53 +106,63 @@
     )
 
 
-def shards_kernel(spans, size, first, opened, shards, *refs):
-    count = len(spans)
-    refs = list(refs)
-    sources = [refs.pop(0) for _ in range(2 * count * shards)]
-    weights = [refs.pop(0) for _ in range(1 if first else 2)]
-    sums = None if first or not opened else refs.pop(0)
-    proj = None if first else refs.pop(0)
-    out, held_early, held_late, sem = refs
-    cut, per = weights[0].shape[1], weights[0].shape[0] // 2
-
-    def copies(n):
-        slot, at = n % 2, 0
-        taken = (0,) if first else (1,) if n < opened else (0, 1)
+def shards_kernel(spans, cuts, plan, opened, last, *refs):
+    count, refs = len(spans), list(refs)
+    used = sorted({part for taken in plan for part in taken})
+    sources = [refs.pop(0) for _ in range(2 * count * len(plan))]
+    weights = {part: refs.pop(0) for part in used}
+    sums = refs.pop(0) if opened else None
+    proj = refs.pop(0) if last else None
+    out, sem = refs.pop(0), refs.pop(-1)
+    held = dict(zip(used, refs))
+    rows, per = sources[0].shape[0], weights[used[0]].shape[0] // 2
+
+    copies, at = {part: [] for part in used}, 0
+    for n, taken in enumerate(plan):
         for i, (low, high) in enumerate(spans):
-            for start, end, part, block, row in segments(low, high, size, cut):
+            for start, end, part, block, row in segments(low, high, cuts):
                 for side in range(2) if part in taken else ():
-                    place = (side * per + block) * (size - cut if part else cut) + row
-                    yield pltpu.make_async_copy(
-                        sources[(2 * n + side) * count + i].at[:, pl.ds(start - low, end - start)],
-                        (held_early, held_late)[part].at[slot, :, pl.ds(place, end - start)],
-                        sem.at[slot, at],
+                    place = (side * per + block) * weights[part].shape[1] + row
+                    copies[part].append(
+                        pltpu.make_async_copy(
+                            sources[(2 * n + side) * count + i].at[
+                                :, pl.ds(start - low, end - start)
+                            ],
+                            held[part].at[pl.ds(n * rows, rows), pl.ds(place, end - start)],
+                            sem.at[at],
+                        )
                     )
                     at += 1
-
-    def times(x, part):
-        rows = weights[part][...]
-        rows = rows.reshape(rows.shape[0] * rows.shape[1], rows.shape[2])
-        return jnp.dot(x[...], rows, preferred_element_type=jnp.float32)
-
-    for copy in copies(0):
-        copy.start()
-    for n in range(shards):
-        for copy in copies(n):
+    for part in used:
+        for copy in copies[part]:
+            copy.start()
+    totals = [sums[n] if n < opened else None for n in range(len(plan))]
+    for part in used:
+        for copy in copies[part]:
             copy.wait()
-        if n + 1 < shards:
-            for copy in copies(n + 1):
-                copy.start()
-        if first:
-            out[n] = times(held_early.at[n % 2], 0)
-        else:
-            total = sums[n] if n < opened else times(held_early.at[n % 2], 0)
-            out[n] = codes_of(gated(total + times(held_late.at[n % 2], 1)), proj)
-
-
-def part_kernel(span, size, first, last, mine, other, early, late, *refs):
-    x_of = lambda side, start, end: (mine, other)[side][:, start - span[0] : end - span[0]]
-    total = gate_up_dot(x_of, *span, size, (early, late), None if first else refs[0][...])
+        takers = [n for n, taken in enumerate(plan) if part in taken]
+        mat = weights[part][...]
+        mat = mat.reshape(mat.shape[0] * mat.shape[1], mat.shape[2])
+        x = held[part][takers[0] * rows : (takers[-1] + 1) * rows]
+        found = jnp.dot(x, mat, preferred_element_type=jnp.float32)
+        for n in takers:
+            own = found[(n - takers[0]) * rows : (n - takers[0] + 1) * rows]
+            totals[n] = own if totals[n] is None else totals[n] + own
+    for n, total in enumerate(totals):
+        out[n] = codes_of(gated(total), proj) if last else total
+
+
+def part_kernel(span, cuts, first, last, mine, other, *refs):
+    weights, refs = refs[: len(cuts)], refs[len(cuts) :]
+    per, total = weights[0].shape[0] // 2, None if first else refs[0][...]
+    for start, end, part, block, row in segments(*span, cuts):
+        for side, x in enumerate((mine, other)):
+            piece = jnp.dot(
+                x[:, start - span[0] : end - span[0]],
+                weights[part][side * per + block, row : row + end - start],
+                preferred_element_type=jnp.float32,
+            )
+            total = piece if total is None else total + piece
     refs[-1][...] = codes_of(gated(total), refs[-2]) if last else total
 
 
@@ -177,7 +177,7 @@
         compiler_params=pltpu.CompilerParams(vmem_limit_bytes=20 * 2**20),
         cost_estimate=FREE,
         name=name,
-    )(*in_hbm(args[:far]), *args[far:])
+    )(*args)
 
 
 def grads_kernel(experts, where, grad_mine, grad_other, docs, routes, *refs):
@@ -249,7 +249,9 @@
     row_edges = [0]
     for share in WAVES:
         row_edges.append(row_edges[-1] + block * share // sum(WAVES) // 16 * 16)
-    row_edges[-2:] = [row_edges[-2] // LANES * LANES, block]
+    for at in CUTS:
+        row_edges[at] = row_edges[at] // LANES * LANES
+    cuts = [row_edges[at] for at in CUTS]
     sent = [
         jnp.where(grp == 0, gate[low:high], up[low:high])
         for low, high in zip(row_edges, row_edges[1:])
@@ -269,8 +271,37 @@
     arriving, swapping = along_dat(waves[0]), []
     direct, swapped = [], []
 
+    where = jnp.stack([core, dat, grp]).astype(jnp.int32)
+
+    def joined(part):
+        low, high = ((0,) + CUTS)[part : part + 2]
+        moves = slice(low * (dats - 1), high * (dats - 1))
+        rows = row_edges[low : high + 1]
+        return join(where, gate, up, direct[moves], swapped[moves], dats, rows)
+
+    def shards_call(low, high, plan, opened, more, last):
+        args = [x for k in range(low, high) for x in (*mine[k], *other[k])]
+        used = sorted({part for taken in plan for part in taken})
+        rows, shards = tokens.shape[0], high - low
+        pieces = 2 * shards * sum(len(segments(*span, cuts)) for span in chunks)
+        shape = (rank, rows) if last else (rows, 2 * gate.shape[1])
+        return vmem_call(
+            functools.partial(shards_kernel, chunks, cuts, plan, opened, last),
+            [*args, *[weights[part] for part in used], *more],
+            (shards, *shape),
+            "shards",
+            len(args),
+            [
+                *[
+                    pltpu.VMEM((shards * rows, dats * weights[part].shape[1]), tokens.dtype)
+                    for part in used
+                ],
+                pltpu.SemaphoreType.DMA((pieces,)),
+            ],
+        )
+
     turn = jnp.zeros((8, LANES), jnp.float32)
-    exchanged, flat, wave = [[], other[0]], [], 0
+    exchanged, flat, wave, weights, begun = [[], other[0]], [], 0, [], []
     for step in range(1, experts):
         moved = [lax.ppermute(x, "exp", ring) for x in mine[-1]]
         mine.append(moved)
@@ -289,38 +320,12 @@
             swapped += got[3]
             swapping, arriving = over_grp(got[2]), along_dat(got[4])
             exchanged.append([lax.ppermute(moved[j], "mdl", swap)])
-    where = jnp.stack([core, dat, grp]).astype(jnp.int32)
-    some = (len(waves) - 1) * (dats - 1)
-    early = join(where, gate, up, direct[:some], swapped[:some], dats, row_edges[:-1])
-
-    def shards_call(low, high, opened, weights, more, shape):
-        first = len(weights) == 1
-        args = [x for k in range(low, high) for x in (*mine[k], *other[k])]
-        cut = row_edges[-2]
-        pieces = sum(len(segments(*span, block, cut)) for span in chunks)
-        return vmem_call(
-            functools.partial(shards_kernel, chunks, block, first, opened, high - low),
-            [*args, *weights, *more],
-            (high - low, *shape),
-            "shards",
-            len(args),
-            [
-                pltpu.VMEM((2, tokens.shape[0], dats * cut), tokens.dtype),
-                pltpu.VMEM((2, tokens.shape[0], dats * (block - cut)), tokens.dtype),
-                pltpu.SemaphoreType.DMA((2, 2 * pieces)),
-            ],
-        )
-
+
+    weights.append(joined(0))
     other = [flat[n : n + count] for n in range(0, len(flat), count)]
-    begun = []
-    for low in range(0, experts - 2, GROUP):
-        high = min(low + GROUP, experts - 2)
-        begun.append(
-            shards_call(
-                low, high, 0, (early,), (), (tokens.shape[0], early.shape[2])
-            )
-        )
-
+    groups = [(n, min(n + GROUP, experts - 2)) for n in range(0, experts - 2, GROUP)]
+    for low, high in groups:
+        begun.append(shards_call(low, high, [(0,)] * (high - low), 0, (), False))
     ready = exchanged.pop(0)
     turn, got = ordered(
         turn, [mine[-1][0], *ready, *swapping], [x[0, :8, :LANES] for x in begun]
@@ -329,27 +334,20 @@
     flat += got[1 : 1 + len(ready)] + exchanged.pop(0)
     swapped += got[1 + len(ready) :]
     other = [flat[n : n + count] for n in range(0, len(flat), count)]
-    late = join(where, gate, up, direct[some:], swapped[some:], dats, row_edges[-2:])
-    weights = (early, late)
+    weights.append(joined(1))
 
     codes = []
-    groups = [(n, min(n + GROUP, experts - 2)) for n in range(0, experts - 2, GROUP)]
-    for low, high in [*groups, (experts - 2, experts - 1)]:
-        opened = min(high, experts - 2) - low
-        found = shards_call(
-            low,
-            high,
-            opened,
-            weights,
-            (*begun[low // GROUP :][: int(opened > 0)], proj_in),
-            (rank, tokens.shape[0]),
-        )
-        found = found + lax.ppermute(found, "mdl", swap)
+    for n, (low, high) in enumerate([*groups, (experts - 2, experts - 1)]):
+        if high < experts - 1:
+            raw = shards_call(low, high, [(1,)] * (high - low), high - low, (begun[n], proj_in), True)
+        else:
+            raw = shards_call(low, high, [(0, 1)], 0, (proj_in,), True)
+        found = raw + lax.ppermute(raw, "mdl", swap)
         for k in range(low, high):
             back = [(z, (z - k) % experts) for z in range(experts)]
             codes.append(found[0] if k == 0 else lax.ppermute(found[k - low], "exp", back))
 
-    made, total = [grad_other, codes[0], found[0]], None
+    made, total = [grad_other, codes[0], raw[0]], None
     for j in range(count):
         last = j == count - 1
         turn, (x,) = ordered(turn, [mine[-1][j]], made, False) if j else (turn, [mine[-1][j]])
@@ -357,9 +355,9 @@
         args += [] if total is None else [total]
         args += [proj_in] if last else []
         total = vmem_call(
-            functools.partial(part_kernel, chunks[j], block, total is None, last),
+            functools.partial(part_kernel, chunks[j], cuts, total is None, last),
             args,
-            (rank, tokens.shape[0]) if last else (tokens.shape[0], early.shape[2]),
+            (rank, tokens.shape[0]) if last else (tokens.shape[0], 2 * gate.shape[1]),
             "part",
         )
         made += [total[:8, :LANES]]

time: 95.9 us -> 92.6 us (0.966)
  local copies, waits for them, and re-layouts: 8.3 us -> 4.98 us
  waiting for transfers between devices: 32.8 us -> 35.1 us
  Pallas kernels: 20.4 us -> 18.1 us
    pallas_call x5, Pallas kernels: 14.3 us -> 11.6 us  [vmem_call(): pl.pallas_call(kernel, in_specs=[hbm] * far + [vmem] * (len(args) - far),...]
    ppermute x4, waiting for transfers between devices: 14.7 us -> 16.4 us  [along_dat(): lax.ppermute(x, 'dat', [((z + k) % dats, z) for z in range(dats)])]
    unnamed x54 -> x62, local copies, waits for them, and re-layouts: 4.72 us -> 3.02 us
    reshape x1, local copies, waits for them, and re-layouts: 1.74 us -> 0.06 us  [on_device(): reordered = proj_out.reshape(rank // group, group, half).transpose(1, 0, 2)]
    ppermute x1, waiting for transfers between devices: 0.03 us -> 1.65 us  [on_device(): cross = lax.ppermute(total, ('exp', 'mdl'), home_pairs[1])]
    ppermute x1, starting transfers between devices: 1.93 us -> 0.4 us  [on_device(): cross = lax.ppermute(total, ('exp', 'mdl'), home_pairs[1])]
    ppermute x1, starting transfers between devices: 0.61 us -> 2.05 us  [on_device(): codes.append(lax.ppermute(total, ('exp', 'mdl'), home_pairs[0]))]
  transfers between devices with their start and end apart: 29 -> 29, of which waited for: 10 -> 10; matrix products, arithmetic and copies ran while one was open for 10% -> 8% of each run, Pallas kernels for 20% -> 18%
where the time goes in v4:
time: 92.6 us; the launch traced here: 92.2 us
  waiting for transfers between devices  35.1 us (38%)
  starting transfers between devices  26.6 us (29%)
  Pallas kernels  18.1 us (20%)
  other arithmetic  6.5 us (7%)
  local copies, waits for them, and re-layouts  4.98 us (5%)
    ppermute x4, waiting for transfers between devices, along_dat(): lax.ppermute(x, 'dat', [((z + k) % dats, z) for z in range(dats)])  16.4 us
    ppermute x6, waiting for transfers between devices, on_device(): moved = [lax.ppermute(x, 'exp', ring) for x in mine[-1]]  12.9 us
    pallas_call x5, Pallas kernels, vmem_call(): pl.pallas_call(kernel, in_specs=[hbm] * far + [vmem] * (len(args) - far),...  11.6 us
    select_n x3, other arithmetic, on_device(): jnp.where(grp == 0, gate[low:high], up[low:high])  6.41 us
    ppermute x6, starting transfers between devices, on_device(): moved = [lax.ppermute(x, 'exp', ring) for x in mine[-1]]  6.35 us
    ppermute x4, starting transfers between devices, along_dat(): lax.ppermute(x, 'dat', [((z + k) % dats, z) for z in range(dats)])  5.96 us
    ppermute x4, starting transfers between devices, over_grp(): return [lax.ppermute(x, 'grp', swap) for x in xs]  5.96 us
    pallas_call x2, Pallas kernels, join(): pl.pallas_call(functools.partial(join_kernel, dats, edges), in_specs=[pl....  5.18 us
  transfers between devices with their start and end apart: 29, of which 10 were waited for; matrix products, arithmetic and copies ran while one was open for 8% of the time, Pallas kernels for 18%

profile of v4, /device:TPU:0, one launch (start us, length us, event | category | flops | bytes accessed | tf_op | source)
XLA Modules:
  0.0 92.2 jit_solution(7141365755700079708)
XLA Ops:
  0.0 1.2 %slice.50.refs_0_ = bf16[256,896]{1,0:T(8,128)(2,1)S(1)} slice(bf16[256,2048]{1,0:T(8,128)(2,1)} %param.8), slice={[0:256], [0:896]} | slice | bytes 917504 | tf_op jit(solution)/shard_map/slice | solution.py:245
  1.2 3.1 %collective-permute-start.1 = (bf16[256,896]{1,0:T(8,128)(2,1)S(1)}, bf16[256,896]{1,0:T(8,128)(2,1)}, u32[]{:S(2)}, u32[]{:S(2)}) collective-permute-start(bf16[256,896]{1,0:T(8,128)(2,1)S(1)} %slice.50.refs_0_), channel_id=1, source_target_pairs={{0,4},{4,8},{8,12},{12,0},{1,5},{5,9},{9,13},{13,1},{2,6},{6,10},{... | collective-permute-start | bytes 1376264 | tf_op jit(solution)/shard_map/ppermute | solution.py:306
  4.3 2.3 %select_bitcast_fusion = (bf16[576,384]{1,0:T(8,128)(2,1)}, bf16[576,384]{1,0:T(8,128)(2,1)S(1)}) fusion(bf16[1,2048,384]{2,1,0:T(8,128)(2,1)} %param.13, bf16[1,2048,384]{2,1,0:T(8,128)(2,1)} %param.12, pred[]{:T(512)S(6)} %eq.2), kind=kLoop, calls=%fused_computation | loop fusion | flops 442368 | bytes 2654209 | tf_op jit(solution)/shard_map/jit(_where)/select_n | solution.py:256
  6.6 1.5 %collective-permute-start.2 = (bf16[576,384]{1,0:T(8,128)(2,1)S(1)}, bf16[576,384]{1,0:T(8,128)(2,1)S(1)}, u32[]{:S(2)}, u32[]{:S(2)}) collective-permute-start(bf16[576,384]{1,0:T(8,128)(2,1)S(1)} %get-tuple-element.60), channel_id=1, source_target_pairs={{2,0},{0,2},{3,1},{1,3},{6,4},{4,6},{7,5},{5,7},{10,8},{8,10},{11,... | collective-permute-start | bytes 1327112 | tf_op jit(solution)/shard_map/ppermute | solution.py:263
  8.1 1.6 %collective-permute-start.3 = (bf16[256,1152]{1,0:T(8,128)(2,1)S(1)}, bf16[256,1152]{1,0:T(8,128)(2,1)S(1)}, u32[]{:S(2)}, u32[]{:S(2)}) collective-permute-start(bf16[256,1152]{1,0:T(8,128)(2,1)S(1)} %slice.51.refs_1_), channel_id=1, source_target_pairs={{0,4},{4,8},{8,12},{12,0},{1,5},{5,9},{9,13},{13,1},{2,6},{6,10},{... | collective-permute-start | bytes 1769480 | tf_op jit(solution)/shard_map/ppermute | solution.py:306
  9.8 0.5 collective-permute-start.5
  10.3 7.9 %collective-permute-done.2.refs_2_ = bf16[576,384]{1,0:T(8,128)(2,1)S(1)} collective-permute-done((bf16[576,384]{1,0:T(8,128)(2,1)S(1)}, bf16[576,384]{1,0:T(8,128)(2,1)S(1)}, u32[]{:S(2)}, u32[]{:S(2)}) %collective-permute-start.2) | collective-permute-done | bytes 442400 | tf_op jit(solution)/shard_map/ppermute | solution.py:263
  18.2 0.6 broadcast_in_dim.3.refs_0_
  19.0 1.5 %collective-permute-start.6 = (bf16[576,384]{1,0:T(8,128)(2,1)}, bf16[576,384]{1,0:T(8,128)(2,1)S(1)}, u32[]{:S(2)}, u32[]{:S(2)}) collective-permute-start(bf16[576,384]{1,0:T(8,128)(2,1)} %get-tuple-element.33), channel_id=1, source_target_pairs={{2,0},{0,2},{3,1},{1,3},{6,4},{4,6},{7,5},{5,7},{10,8},{8,10},{11,... | collective-permute-start | bytes 1327112 | tf_op jit(solution)/shard_map/ppermute | solution.py:263
  20.5 1.5 %collective-permute-start.7 = (bf16[576,384]{1,0:T(8,128)(2,1)}, bf16[576,384]{1,0:T(8,128)(2,1)S(1)}, u32[]{:S(2)}, u32[]{:S(2)}) collective-permute-start(bf16[576,384]{1,0:T(8,128)(2,1)} %get-tuple-element.34.refs_0_), channel_id=1, source_target_pairs={{0,16},{16,0},{1,17},{17,1},{2,18},{18,2},{3,19},{19,3},{4,20},{20... | collective-permute-start | bytes 1327112 | tf_op jit(solution)/shard_map/ppermute | solution.py:269
  22.0 1.6 %collective-permute-start.8 = (bf16[256,896]{1,0:T(8,128)(2,1)}, bf16[256,896]{1,0:T(8,128)(2,1)S(1)}, u32[]{:S(2)}, u32[]{:S(2)}) collective-permute-start(bf16[256,896]{1,0:T(8,128)(2,1)} %get-tuple-element.37.refs_4_), channel_id=1, source_target_pairs={{0,4},{4,8},{8,12},{12,0},{1,5},{5,9},{9,13},{13,1},{2,6},{6,10},{... | collective-permute-start | bytes 1376264 | tf_op jit(solution)/shard_map/ppermute | solution.py:306
  23.6 6.8 %collective-permute-done.3.refs_1_ = bf16[256,1152]{1,0:T(8,128)(2,1)S(1)} collective-permute-done((bf16[256,1152]{1,0:T(8,128)(2,1)S(1)}, bf16[256,1152]{1,0:T(8,128)(2,1)S(1)}, u32[]{:S(2)}, u32[]{:S(2)}) %collective-permute-start.3) | collective-permute-done | bytes 589856 | tf_op jit(solution)/shard_map/ppermute | solution.py:306
  30.3 2.1 %select_bitcast_fusion.2.refs_6_ = bf16[512,384]{1,0:T(8,128)(2,1)} fusion(bf16[1,2048,384]{2,1,0:T(8,128)(2,1)} %param.13, bf16[1,2048,384]{2,1,0:T(8,128)(2,1)} %param.12, pred[]{:T(512)S(6)} %eq.2), kind=kLoop, calls=%fused_computation.2 | loop fusion | flops 196608 | bytes 1179649 | tf_op jit(solution)/shard_map/jit(_where)/select_n | solution.py:256
  32.5 0.8 copy-done.5
  33.3 0.1 copy-done.25
  33.4 0.2 copy-done.26
  33.6 1.8 %collective-permute-start.11 = (bf16[576,384]{1,0:T(8,128)(2,1)}, bf16[576,384]{1,0:T(8,128)(2,1)S(1)}, u32[]{:S(2)}, u32[]{:S(2)}) collective-permute-start(bf16[576,384]{1,0:T(8,128)(2,1)} %get-tuple-element.41.refs_1_), channel_id=1, source_target_pairs={{0,16},{16,0},{1,17},{17,1},{2,18},{18,2},{3,19},{19,3},{4,20},{20... | collective-permute-start | bytes 1327112 | tf_op jit(solution)/shard_map/ppermute | solution.py:269
  35.3 1.5 %collective-permute-start.10 = (bf16[512,384]{1,0:T(8,128)(2,1)}, bf16[512,384]{1,0:T(8,128)(2,1)S(1)}, u32[]{:S(2)}, u32[]{:S(2)}) collective-permute-start(bf16[512,384]{1,0:T(8,128)(2,1)} %get-tuple-element.40), channel_id=1, source_target_pairs={{2,0},{0,2},{3,1},{1,3},{6,4},{4,6},{7,5},{5,7},{10,8},{8,10},{11,... | collective-permute-start | bytes 1179656 | tf_op jit(solution)/shard_map/ppermute | solution.py:263
  36.8 2.5 %collective-permute-done.8.refs_1_ = bf16[256,896]{1,0:T(8,128)(2,1)S(1)} collective-permute-done((bf16[256,896]{1,0:T(8,128)(2,1)}, bf16[256,896]{1,0:T(8,128)(2,1)S(1)}, u32[]{:S(2)}, u32[]{:S(2)}) %collective-permute-start.8) | collective-permute-done | bytes 458784 | tf_op jit(solution)/shard_map/ppermute | solution.py:306
  39.3 2.0 %select_bitcast_fusion.3.refs_5_ = bf16[384,384]{1,0:T(8,128)(2,1)} fusion(bf16[1,2048,384]{2,1,0:T(8,128)(2,1)} %param.13, bf16[1,2048,384]{2,1,0:T(8,128)(2,1)} %param.12, pred[]{:T(512)S(6)} %eq.2), kind=kLoop, calls=%fused_computation.3 | loop fusion | flops 147456 | bytes 884737 | tf_op jit(solution)/shard_map/jit(_where)/select_n | solution.py:256
  41.3 5.3 %collective-permute-done.10.refs_3_ = bf16[512,384]{1,0:T(8,128)(2,1)S(1)} collective-permute-done((bf16[512,384]{1,0:T(8,128)(2,1)}, bf16[512,384]{1,0:T(8,128)(2,1)S(1)}, u32[]{:S(2)}, u32[]{:S(2)}) %collective-permute-start.10) | collective-permute-done | bytes 393248 | tf_op jit(solution)/shard_map/ppermute | solution.py:263
  46.6 0.8 copy-done.27
  47.5 1.2 %collective-permute-start.15 = (bf16[512,384]{1,0:T(8,128)(2,1)}, bf16[512,384]{1,0:T(8,128)(2,1)}, u32[]{:S(2)}, u32[]{:S(2)}) collective-permute-start(bf16[512,384]{1,0:T(8,128)(2,1)} %get-tuple-element.45.refs_2_), channel_id=1, source_target_pairs={{0,16},{16,0},{1,17},{17,1},{2,18},{18,2},{3,19},{19,3},{4,20},{20... | collective-permute-start | bytes 1179656 | tf_op jit(solution)/shard_map/ppermute | solution.py:269
  48.7 1.5 %collective-permute-start.14 = (bf16[384,384]{1,0:T(8,128)(2,1)}, bf16[384,384]{1,0:T(8,128)(2,1)}, u32[]{:S(2)}, u32[]{:S(2)}) collective-permute-start(bf16[384,384]{1,0:T(8,128)(2,1)} %get-tuple-element.44), channel_id=1, source_target_pairs={{2,0},{0,2},{3,1},{1,3},{6,4},{4,6},{7,5},{5,7},{10,8},{8,10},{11,... | collective-permute-start | bytes 884744 | tf_op jit(solution)/shard_map/ppermute | solution.py:263
  50.2 3.7 %collective-permute-done.12.refs_1_ = bf16[256,1152]{1,0:T(8,128)(2,1)S(1)} collective-permute-done((bf16[256,1152]{1,0:T(8,128)(2,1)}, bf16[256,1152]{1,0:T(8,128)(2,1)S(1)}, u32[]{:S(2)}, u32[]{:S(2)}) %collective-permute-start.12) | collective-permute-done | bytes 589856 | tf_op jit(solution)/shard_map/ppermute | solution.py:306
  53.9 3.2 %collective-permute-done.14.refs_3_ = bf16[384,384]{1,0:T(8,128)(2,1)} collective-permute-done((bf16[384,384]{1,0:T(8,128)(2,1)}, bf16[384,384]{1,0:T(8,128)(2,1)}, u32[]{:S(2)}, u32[]{:S(2)}) %collective-permute-start.14) | collective-permute-done | bytes 294944 | tf_op jit(solution)/shard_map/ppermute | solution.py:263
  57.1 0.9 collective-permute-done.15.refs_4_
  58.0 1.5 %collective-permute-start.18 = (bf16[384,384]{1,0:T(8,128)(2,1)}, bf16[384,384]{1,0:T(8,128)(2,1)S(1)}, u32[]{:S(2)}, u32[]{:S(2)}) collective-permute-start(bf16[384,384]{1,0:T(8,128)(2,1)} %get-tuple-element.47.refs_0_), channel_id=1, source_target_pairs={{0,16},{16,0},{1,17},{17,1},{2,18},{18,2},{3,19},{19,3},{4,20},{20... | collective-permute-start | bytes 884744 | tf_op jit(solution)/shard_map/ppermute | solution.py:269
  59.7 3.4 %join.2.refs_8_.refs_4_.refs_0_ = bf16[2,1664,768]{2,1,0:T(8,128)(2,1)S(1)} custom-call(s32[3]{0:T(128)S(1)} %pad_add_fusion.where, bf16[2048,384]{1,0:T(8,128)(2,1)} %bitcast.33, bf16[2048,384]{1,0:T(8,128)(2,1)} %bitcast.31, bf16[576,384]{1,0:T(8,128)(2,1)} %get-tuple-element.34.refs_0_, bf16[576,384]{1,0:T(8,128)(2,1)} %get-tuple-element.41.refs_1_, ...), custom_call_target="tpu_custom_call" | custom-call | flops 1 | bytes 1 | tf_op jit(solution)/shard_map/join/pallas_call | solution.py:74
  63.2 4.1 %shards.3.refs_9_ = f32[2,256,768]{2,1,0:T(8,128)S(1)} custom-call(bf16[256,896]{1,0:T(8,128)(2,1)S(1)} %copy-done.8, bf16[256,1152]{1,0:T(8,128)(2,1)S(1)} %slice.51.refs_1_, bf16[256,896]{1,0:T(8,128)(2,1)S(1)} %copy-done.10, bf16[256,1152]{1,0:T(8,128)(2,1)S(1)} %copy-done.6, bf16[256,896]{1,0:T(8,128)(2,1)} %get-tuple-element.37.refs_4_, ...), custom_call_target="tpu_custom_call" | custom-call | flops 1 | bytes 1 | tf_op jit(solution)/shard_map/shards/pallas_call | solution.py:171
  67.3 0.8 copy-done.15
  68.2 1.8 %join.3.refs_8_.refs_5_.refs_1_ = bf16[2,384,768]{2,1,0:T(8,128)(2,1)S(1)} custom-call(s32[3]{0:T(128)S(1)} %pad_add_fusion.where, bf16[2048,384]{1,0:T(8,128)(2,1)} %bitcast.34, bf16[2048,384]{1,0:T(8,128)(2,1)} %bitcast.32, bf16[384,384]{1,0:T(8,128)(2,1)} %get-tuple-element.47.refs_0_, bf16[384,384]{1,0:T(8,128)(2,1)} %get-tuple-element.53.refs_1_), custom_call_target="tpu_custom_call" | custom-call | flops 1 | bytes 1 | tf_op jit(solution)/shard_map/join/pallas_call | solution.py:74
  70.0 1.5 %shards.4 = f32[2,32,256]{2,1,0:T(8,128)S(1)} custom-call(bf16[256,896]{1,0:T(8,128)(2,1)S(1)} %copy-done.8, bf16[256,1152]{1,0:T(8,128)(2,1)S(1)} %slice.51.refs_1_, bf16[256,896]{1,0:T(8,128)(2,1)S(1)} %copy-done.10, bf16[256,1152]{1,0:T(8,128)(2,1)S(1)} %copy-done.6, bf16[256,896]{1,0:T(8,128)(2,1)} %get-tuple-element.37.refs_4_, ...), custom_call_target="tpu_custom_call" | custom-call | flops 1 | bytes 1 | tf_op jit(solution)/shard_map/shards/pallas_call | solution.py:171
  71.5 0.5 collective-permute-start.19
  72.1 0.4 fusion.grad_mine
  72.5 0.5 collective-permute-start
  73.0 2.7 %shards.5 = f32[1,32,256]{2,1,0:T(8,128)S(1)} custom-call(bf16[256,896]{1,0:T(8,128)(2,1)S(1)} %copy-done.18, bf16[256,1152]{1,0:T(8,128)(2,1)S(1)} %copy-done.14, bf16[256,896]{1,0:T(8,128)(2,1)S(1)} %copy-done.16, bf16[256,1152]{1,0:T(8,128)(2,1)S(1)} %collective-permute-done.21.refs_3_, bf16[2,1664,768]{2,1,0:T(8,128)(2,1)S(1)} %join.2.refs_8_.refs_4_.refs_0_, ...), custom_call_target="tpu_custom_call" | custom-call | flops 1 | bytes 1 | tf_op jit(solution)/shard_map/shards/pallas_call | solution.py:171
  75.7 2.0 %part.2.refs_2_ = f32[256,768]{1,0:T(8,128)S(1)} custom-call(bf16[256,896]{1,0:T(8,128)(2,1)} %get-tuple-element.57.mine, bf16[256,896]{1,0:T(8,128)(2,1)S(1)} %collective-permute-done.25.other, bf16[2,1664,768]{2,1,0:T(8,128)(2,1)S(1)} %join.2.refs_8_.refs_4_.refs_0_, bf16[2,384,768]{2,1,0:T(8,128)(2,1)S(1)} %join.3.refs_8_.refs_5_.refs_1_), custom_call_target="tpu_custom_call" | custom-call | flops 1 | bytes 1 | tf_op jit(solution)/shard_map/part/pallas_call | solution.py:171
  77.8 0.3 collective-permute-start.26
  78.1 0.2 collective-permute-start.22
  78.3 3.6 %collective-permute-start.20 = (f32[32,256]{1,0:T(8,128)S(1)}, f32[32,256]{1,0:T(8,128)S(1)}, u32[]{:S(2)}, u32[]{:S(2)}) collective-permute-start(f32[32,256]{1,0:T(8,128)S(1)} %get-tuple-element.61), channel_id=1, source_target_pairs={{0,12},{4,0},{8,4},{12,8},{1,13},{5,1},{9,5},{13,9},{2,14},{6,2},{... | collective-permute-start | bytes 98312 | tf_op jit(solution)/shard_map/ppermute | solution.py:348
  82.2 1.4 %part.3 = f32[32,256]{1,0:T(8,128)S(1)} custom-call(bf16[256,1152]{1,0:T(8,128)(2,1)S(1)} %get-tuple-element.58.mine, bf16[256,1152]{1,0:T(8,128)(2,1)S(1)} %collective-permute-done.26.other, bf16[2,1664,768]{2,1,0:T(8,128)(2,1)S(1)} %join.2.refs_8_.refs_4_.refs_0_, bf16[2,384,768]{2,1,0:T(8,128)(2,1)S(1)} %join.3.refs_8_.refs_5_.refs_1_, ...), custom_call_target="tpu_custom_call" | custom-call | flops 1 | bytes 1 | tf_op jit(solution)/shard_map/part/pallas_call | solution.py:171
  83.6 2.1 %collective-permute-start.27 = (f32[32,256]{1,0:T(8,128)S(1)}, f32[32,256]{1,0:T(8,128)S(1)}, u32[]{:S(2)}, u32[]{:S(2)}) collective-permute-start(f32[32,256]{1,0:T(8,128)S(1)} %part.3), channel_id=1, source_target_pairs={{0,4},{1,5},{4,8},{5,9},{8,12},{9,13},{12,0},{13,1},{2,6},{3,7},{6... | collective-permute-start | bytes 98312 | tf_op jit(solution)/shard_map/ppermute | solution.py:372
  85.6 0.4 collective-permute-start.28
  86.0 0.9 collective-permute-done.23.refs_2_
  86.9 2.4 %collective-permute-done.27.refs_3_ = f32[32,256]{1,0:T(8,128)S(1)} collective-permute-done((f32[32,256]{1,0:T(8,128)S(1)}, f32[32,256]{1,0:T(8,128)S(1)}, u32[]{:S(2)}, u32[]{:S(2)}) %collective-permute-start.27) | collective-permute-done | bytes 32800 | tf_op jit(solution)/shard_map/ppermute | solution.py:372
  89.3 1.7 %collective-permute-done.28.refs_4_ = f32[32,256]{1,0:T(8,128)S(1)} collective-permute-done((f32[32,256]{1,0:T(8,128)S(1)}, f32[32,256]{1,0:T(8,128)S(1)}, u32[]{:S(2)}, u32[]{:S(2)}) %collective-permute-start.28) | collective-permute-done | bytes 32800 | tf_op jit(solution)/shard_map/ppermute | solution.py:373
  91.0 1.3 %doc_grads.1 = f32[4,4,1024]{2,1,0:T(4,128)} custom-call(s32[1]{0:T(128)} %bitcast.where, f32[32,256]{1,0:T(8,128)S(1)} %fusion.grad_mine, f32[32,256]{1,0:T(8,128)S(1)} %collective-permute-done.refs_2_.grad_other, s32[1,256]{1,0:T(1,128)S(1)} %copy-done.22, s32[2,256]{1,0:T(2,128)S(1)} %bitcast.30, f32[32,256]{1,0:T(8,128)S(1)} %get-tuple-element.62.refs_3_.refs_0_, ...), custom_call_target="tpu_custom_call" | custom-call | flops 8388608 | bytes 1048576 | tf_op jit(solution)/shard_map/doc_grads/pallas_call | solution.py:377
  (100 shorter events, 1.0 us)
Async XLA Ops:
  0.0 72.1 %copy-start = (bf16[256,2048]{1,0:T(8,128)(2,1)S(1)}, bf16[256,2048]{1,0:T(8,128)(2,1)}, u32[]{:S(2)}) copy-start(bf16[256,2048]{1,0:T(8,128)(2,1)} %param.9) | copy-start | bytes 3145732
  0.0 8.1 %copy-start.29 = (bf16[256,2048]{1,0:T(8,128)(2,1)S(1)}, bf16[256,2048]{1,0:T(8,128)(2,1)}, u32[]{:S(2)}) copy-start(bf16[256,2048]{1,0:T(8,128)(2,1)} %param.8) | copy-start | bytes 3145732
  1.2 8.6 %copy-start.7 = (bf16[256,896]{1,0:T(8,128)(2,1)}, bf16[256,896]{1,0:T(8,128)(2,1)S(1)}, u32[]{:S(2)}) copy-start(bf16[256,896]{1,0:T(8,128)(2,1)S(1)} %slice.50.refs_0_) | copy-start | bytes 1376260
  1.2 17.0 %collective-permute-start.1 = (bf16[256,896]{1,0:T(8,128)(2,1)S(1)}, bf16[256,896]{1,0:T(8,128)(2,1)}, u32[]{:S(2)}, u32[]{:S(2)}) collective-permute-start(bf16[256,896]{1,0:T(8,128)(2,1)S(1)} %slice.50.refs_0_), channel_id=1, source_target_pairs={{0,4},{4,8},{8,12},{12,0},{1,5},{5,9},{9,13},{13,1},{2,6},{6,10},{... | collective-permute-start | bytes 1376264 | tf_op jit(solution)/shard_map/ppermute | solution.py:306
  6.6 11.6 %collective-permute-start.2 = (bf16[576,384]{1,0:T(8,128)(2,1)S(1)}, bf16[576,384]{1,0:T(8,128)(2,1)S(1)}, u32[]{:S(2)}, u32[]{:S(2)}) collective-permute-start(bf16[576,384]{1,0:T(8,128)(2,1)S(1)} %get-tuple-element.60), channel_id=1, source_target_pairs={{2,0},{0,2},{3,1},{1,3},{6,4},{4,6},{7,5},{5,7},{10,8},{8,10},{11,... | collective-permute-start | bytes 1327112 | tf_op jit(solution)/shard_map/ppermute | solution.py:263
  8.1 22.2 %collective-permute-start.3 = (bf16[256,1152]{1,0:T(8,128)(2,1)S(1)}, bf16[256,1152]{1,0:T(8,128)(2,1)S(1)}, u32[]{:S(2)}, u32[]{:S(2)}) collective-permute-start(bf16[256,1152]{1,0:T(8,128)(2,1)S(1)} %slice.51.refs_1_), channel_id=1, source_target_pairs={{0,4},{4,8},{8,12},{12,0},{1,5},{5,9},{9,13},{13,1},{2,6},{6,10},{... | collective-permute-start | bytes 1769480 | tf_op jit(solution)/shard_map/ppermute | solution.py:306
  9.8 12.2 %collective-permute-start.4 = (bf16[256,896]{1,0:T(8,128)(2,1)S(1)}, bf16[256,896]{1,0:T(8,128)(2,1)S(1)}, u32[]{:S(2)}, u32[]{:S(2)}) collective-permute-start(bf16[256,896]{1,0:T(8,128)(2,1)S(1)} %slice.50.refs_0_), channel_id=1, source_target_pairs={{0,1},{1,0},{2,3},{3,2},{4,5},{5,4},{6,7},{7,6},{8,9},{9,8},{10,11... | collective-permute-start | bytes 1376264 | tf_op jit(solution)/shard_map/ppermute | solution.py:246
  9.8 22.7 %collective-permute-start.5 = (bf16[256,1152]{1,0:T(8,128)(2,1)S(1)}, bf16[256,1152]{1,0:T(8,128)(2,1)S(1)}, u32[]{:S(2)}, u32[]{:S(2)}) collective-permute-start(bf16[256,1152]{1,0:T(8,128)(2,1)S(1)} %slice.51.refs_1_), channel_id=1, source_target_pairs={{0,1},{1,0},{2,3},{3,2},{4,5},{5,4},{6,7},{7,6},{8,9},{9,8},{10,11... | collective-permute-start | bytes 1769480 | tf_op jit(solution)/shard_map/ppermute | solution.py:246
  19.0 13.5 %collective-permute-start.6 = (bf16[576,384]{1,0:T(8,128)(2,1)}, bf16[576,384]{1,0:T(8,128)(2,1)S(1)}, u32[]{:S(2)}, u32[]{:S(2)}) collective-permute-start(bf16[576,384]{1,0:T(8,128)(2,1)} %get-tuple-element.33), channel_id=1, source_target_pairs={{2,0},{0,2},{3,1},{1,3},{6,4},{4,6},{7,5},{5,7},{10,8},{8,10},{11,... | collective-permute-start | bytes 1327112 | tf_op jit(solution)/shard_map/ppermute | solution.py:263
  20.5 12.0 %collective-permute-start.7 = (bf16[576,384]{1,0:T(8,128)(2,1)}, bf16[576,384]{1,0:T(8,128)(2,1)S(1)}, u32[]{:S(2)}, u32[]{:S(2)}) collective-permute-start(bf16[576,384]{1,0:T(8,128)(2,1)} %get-tuple-element.34.refs_0_), channel_id=1, source_target_pairs={{0,16},{16,0},{1,17},{17,1},{2,18},{18,2},{3,19},{19,3},{4,20},{20... | collective-permute-start | bytes 1327112 | tf_op jit(solution)/shard_map/ppermute | solution.py:269
  22.0 10.5 %copy-start.9 = (bf16[256,896]{1,0:T(8,128)(2,1)}, bf16[256,896]{1,0:T(8,128)(2,1)S(1)}, u32[]{:S(2)}) copy-start(bf16[256,896]{1,0:T(8,128)(2,1)S(1)} %collective-permute-done.4.refs_2_) | copy-start | bytes 1376260
  22.0 17.3 %collective-permute-start.8 = (bf16[256,896]{1,0:T(8,128)(2,1)}, bf16[256,896]{1,0:T(8,128)(2,1)S(1)}, u32[]{:S(2)}, u32[]{:S(2)}) collective-permute-start(bf16[256,896]{1,0:T(8,128)(2,1)} %get-tuple-element.37.refs_4_), channel_id=1, source_target_pairs={{0,4},{4,8},{8,12},{12,0},{1,5},{5,9},{9,13},{13,1},{2,6},{6,10},{... | collective-permute-start | bytes 1376264 | tf_op jit(solution)/shard_map/ppermute | solution.py:306
  30.3 2.2 %copy-start.3 = (bf16[256,1152]{1,0:T(8,128)(2,1)}, bf16[256,1152]{1,0:T(8,128)(2,1)S(1)}, u32[]{:S(2)}) copy-start(bf16[256,1152]{1,0:T(8,128)(2,1)S(1)} %collective-permute-done.3.refs_1_) | copy-start | bytes 1769476
  30.3 11.0 %collective-permute-start.9 = (bf16[256,896]{1,0:T(8,128)(2,1)}, bf16[256,896]{1,0:T(8,128)(2,1)S(1)}, u32[]{:S(2)}, u32[]{:S(2)}) collective-permute-start(bf16[256,896]{1,0:T(8,128)(2,1)} %get-tuple-element.37.refs_4_), channel_id=1, source_target_pairs={{0,1},{1,0},{2,3},{3,2},{4,5},{5,4},{6,7},{7,6},{8,9},{9,8},{10,11... | collective-permute-start | bytes 1376264 | tf_op jit(solution)/shard_map/ppermute | solution.py:322
  33.6 20.3 %copy-start.30 = (bf16[32,2048]{1,0:T(8,128)(2,1)S(1)}, bf16[32,2048]{1,0:T(8,128)(2,1)}, u32[]{:S(2)}) copy-start(bf16[32,2048]{1,0:T(8,128)(2,1)} %param.15) | copy-start | bytes 393220
  33.6 13.0 %collective-permute-start.11 = (bf16[576,384]{1,0:T(8,128)(2,1)}, bf16[576,384]{1,0:T(8,128)(2,1)S(1)}, u32[]{:S(2)}, u32[]{:S(2)}) collective-permute-start(bf16[576,384]{1,0:T(8,128)(2,1)} %get-tuple-element.41.refs_1_), channel_id=1, source_target_pairs={{0,16},{16,0},{1,17},{17,1},{2,18},{18,2},{3,19},{19,3},{4,20},{20... | collective-permute-start | bytes 1327112 | tf_op jit(solution)/shard_map/ppermute | solution.py:269
  35.3 11.2 %collective-permute-start.10 = (bf16[512,384]{1,0:T(8,128)(2,1)}, bf16[512,384]{1,0:T(8,128)(2,1)S(1)}, u32[]{:S(2)}, u32[]{:S(2)}) collective-permute-start(bf16[512,384]{1,0:T(8,128)(2,1)} %get-tuple-element.40), channel_id=1, source_target_pairs={{2,0},{0,2},{3,1},{1,3},{6,4},{4,6},{7,5},{5,7},{10,8},{8,10},{11,... | collective-permute-start | bytes 1179656 | tf_op jit(solution)/shard_map/ppermute | solution.py:263
  36.8 17.0 %collective-permute-start.12 = (bf16[256,1152]{1,0:T(8,128)(2,1)}, bf16[256,1152]{1,0:T(8,128)(2,1)S(1)}, u32[]{:S(2)}, u32[]{:S(2)}) collective-permute-start(bf16[256,1152]{1,0:T(8,128)(2,1)} %get-tuple-element.38.refs_5_), channel_id=1, source_target_pairs={{0,4},{4,8},{8,12},{12,0},{1,5},{5,9},{9,13},{13,1},{2,6},{6,10},{... | collective-permute-start | bytes 1769480 | tf_op jit(solution)/shard_map/ppermute | solution.py:306
  39.3 7.3 %copy-start.17 = (bf16[256,896]{1,0:T(8,128)(2,1)}, bf16[256,896]{1,0:T(8,128)(2,1)S(1)}, u32[]{:S(2)}) copy-start(bf16[256,896]{1,0:T(8,128)(2,1)S(1)} %collective-permute-done.8.refs_1_) | copy-start | bytes 1376260
  39.3 14.6 %collective-permute-start.13 = (bf16[256,1152]{1,0:T(8,128)(2,1)}, bf16[256,1152]{1,0:T(8,128)(2,1)S(1)}, u32[]{:S(2)}, u32[]{:S(2)}) collective-permute-start(bf16[256,1152]{1,0:T(8,128)(2,1)} %get-tuple-element.38.refs_5_), channel_id=1, source_target_pairs={{0,1},{1,0},{2,3},{3,2},{4,5},{5,4},{6,7},{7,6},{8,9},{9,8},{10,11... | collective-permute-start | bytes 1769480 | tf_op jit(solution)/shard_map/ppermute | solution.py:322
  41.3 5.3 %copy-start.11 = (bf16[256,896]{1,0:T(8,128)(2,1)}, bf16[256,896]{1,0:T(8,128)(2,1)S(1)}, u32[]{:S(2)}) copy-start(bf16[256,896]{1,0:T(8,128)(2,1)S(1)} %collective-permute-done.9.refs_2_) | copy-start | bytes 1376260
  47.5 10.5 %collective-permute-start.15 = (bf16[512,384]{1,0:T(8,128)(2,1)}, bf16[512,384]{1,0:T(8,128)(2,1)}, u32[]{:S(2)}, u32[]{:S(2)}) collective-permute-start(bf16[512,384]{1,0:T(8,128)(2,1)} %get-tuple-element.45.refs_2_), channel_id=1, source_target_pairs={{0,16},{16,0},{1,17},{17,1},{2,18},{18,2},{3,19},{19,3},{4,20},{20... | collective-permute-start | bytes 1179656 | tf_op jit(solution)/shard_map/ppermute | solution.py:269
  48.7 8.4 %collective-permute-start.14 = (bf16[384,384]{1,0:T(8,128)(2,1)}, bf16[384,384]{1,0:T(8,128)(2,1)}, u32[]{:S(2)}, u32[]{:S(2)}) collective-permute-start(bf16[384,384]{1,0:T(8,128)(2,1)} %get-tuple-element.44), channel_id=1, source_target_pairs={{2,0},{0,2},{3,1},{1,3},{6,4},{4,6},{7,5},{5,7},{10,8},{8,10},{11,... | collective-permute-start | bytes 884744 | tf_op jit(solution)/shard_map/ppermute | solution.py:263
  50.2 17.1 %collective-permute-start.16 = (bf16[256,896]{1,0:T(8,128)(2,1)}, bf16[256,896]{1,0:T(8,128)(2,1)}, u32[]{:S(2)}, u32[]{:S(2)}) collective-permute-start(bf16[256,896]{1,0:T(8,128)(2,1)} %get-tuple-element.49.refs_0_), channel_id=1, source_target_pairs={{0,4},{4,8},{8,12},{12,0},{1,5},{5,9},{9,13},{13,1},{2,6},{6,10},{... | collective-permute-start | bytes 1376264 | tf_op jit(solution)/shard_map/ppermute | solution.py:306
  53.8 4.2 %copy-start.13 = (bf16[256,1152]{1,0:T(8,128)(2,1)}, bf16[256,1152]{1,0:T(8,128)(2,1)S(1)}, u32[]{:S(2)}) copy-start(bf16[256,1152]{1,0:T(8,128)(2,1)S(1)} %collective-permute-done.12.refs_1_) | copy-start | bytes 1769476
  53.9 13.4 %collective-permute-start.17 = (bf16[256,896]{1,0:T(8,128)(2,1)}, bf16[256,896]{1,0:T(8,128)(2,1)S(1)}, u32[]{:S(2)}, u32[]{:S(2)}) collective-permute-start(bf16[256,896]{1,0:T(8,128)(2,1)} %get-tuple-element.49.refs_0_), channel_id=1, source_target_pairs={{0,1},{1,0},{2,3},{3,2},{4,5},{5,4},{6,7},{7,6},{8,9},{9,8},{10,11... | collective-permute-start | bytes 1376264 | tf_op jit(solution)/shard_map/ppermute | solution.py:322
  53.9 4.1 %copy-start.1 = (bf16[256,1152]{1,0:T(8,128)(2,1)}, bf16[256,1152]{1,0:T(8,128)(2,1)S(1)}, u32[]{:S(2)}) copy-start(bf16[256,1152]{1,0:T(8,128)(2,1)S(1)} %collective-permute-done.13.refs_2_) | copy-start | bytes 1769476
  58.0 9.3 %collective-permute-start.18 = (bf16[384,384]{1,0:T(8,128)(2,1)}, bf16[384,384]{1,0:T(8,128)(2,1)S(1)}, u32[]{:S(2)}, u32[]{:S(2)}) collective-permute-start(bf16[384,384]{1,0:T(8,128)(2,1)} %get-tuple-element.47.refs_0_), channel_id=1, source_target_pairs={{0,16},{16,0},{1,17},{17,1},{2,18},{18,2},{3,19},{19,3},{4,20},{20... | collective-permute-start | bytes 884744 | tf_op jit(solution)/shard_map/ppermute | solution.py:269
  59.6 13.4 %collective-permute-start.21 = (bf16[256,1152]{1,0:T(8,128)(2,1)}, bf16[256,1152]{1,0:T(8,128)(2,1)S(1)}, u32[]{:S(2)}, u32[]{:S(2)}) collective-permute-start(bf16[256,1152]{1,0:T(8,128)(2,1)} %get-tuple-element.54.refs_1_), channel_id=1, source_target_pairs={{0,1},{1,0},{2,3},{3,2},{4,5},{5,4},{6,7},{7,6},{8,9},{9,8},{10,11... | collective-permute-start | bytes 1769480 | tf_op jit(solution)/shard_map/ppermute | solution.py:322
  59.6 18.1 %collective-permute-start.24 = (bf16[256,1152]{1,0:T(8,128)(2,1)}, bf16[256,1152]{1,0:T(8,128)(2,1)S(1)}, u32[]{:S(2)}, u32[]{:S(2)}) collective-permute-start(bf16[256,1152]{1,0:T(8,128)(2,1)} %get-tuple-element.54.refs_1_), channel_id=1, source_target_pairs={{0,4},{4,8},{8,12},{12,0},{1,5},{5,9},{9,13},{13,1},{2,6},{6,10},{... | collective-permute-start | bytes 1769480 | tf_op jit(solution)/shard_map/ppermute | solution.py:306
  59.7 3.4 %copy-start.2 = (bf16[256,1152]{1,0:T(8,128)(2,1)S(1)}, bf16[256,1152]{1,0:T(8,128)(2,1)}, u32[]{:S(2)}) copy-start(bf16[256,1152]{1,0:T(8,128)(2,1)} %get-tuple-element.46.refs_7_) | copy-start | bytes 1769476
  59.7 3.4 %copy-start.4 = (bf16[256,1152]{1,0:T(8,128)(2,1)S(1)}, bf16[256,1152]{1,0:T(8,128)(2,1)}, u32[]{:S(2)}) copy-start(bf16[256,1152]{1,0:T(8,128)(2,1)} %get-tuple-element.38.refs_5_) | copy-start | bytes 1769476
  59.7 3.4 %copy-start.6 = (bf16[256,1152]{1,0:T(8,128)(2,1)S(1)}, bf16[256,1152]{1,0:T(8,128)(2,1)}, u32[]{:S(2)}) copy-start(bf16[256,1152]{1,0:T(8,128)(2,1)} %get-tuple-element.36.refs_3_) | copy-start | bytes 1769476
  59.7 3.4 %copy-start.8 = (bf16[256,896]{1,0:T(8,128)(2,1)S(1)}, bf16[256,896]{1,0:T(8,128)(2,1)}, u32[]{:S(2)}) copy-start(bf16[256,896]{1,0:T(8,128)(2,1)} %copy-done.7) | copy-start | bytes 1376260
  59.7 3.4 %copy-start.10 = (bf16[256,896]{1,0:T(8,128)(2,1)S(1)}, bf16[256,896]{1,0:T(8,128)(2,1)}, u32[]{:S(2)}) copy-start(bf16[256,896]{1,0:T(8,128)(2,1)} %get-tuple-element.35.refs_2_) | copy-start | bytes 1376260
  59.7 3.4 %copy-start.12 = (bf16[256,896]{1,0:T(8,128)(2,1)S(1)}, bf16[256,896]{1,0:T(8,128)(2,1)}, u32[]{:S(2)}) copy-start(bf16[256,896]{1,0:T(8,128)(2,1)} %get-tuple-element.42.refs_6_) | copy-start | bytes 1376260
  71.5 1.5 %collective-permute-start.19 = (f32[2,32,256]{2,1,0:T(8,128)S(1)}, f32[2,32,256]{2,1,0:T(8,128)S(1)}, u32[]{:S(2)}, u32[]{:S(2)}) collective-permute-start(f32[2,32,256]{2,1,0:T(8,128)S(1)} %shards.4), channel_id=1, source_target_pairs={{0,1},{1,0},{2,3},{3,2},{4,5},{5,4},{6,7},{7,6},{8,9},{9,8},{10,11... | collective-permute-start | bytes 196616 | tf_op jit(solution)/shard_map/ppermute | solution.py:345
  72.0 3.7 %collective-permute-start.25 = (bf16[256,896]{1,0:T(8,128)(2,1)}, bf16[256,896]{1,0:T(8,128)(2,1)S(1)}, u32[]{:S(2)}, u32[]{:S(2)}) collective-permute-start(bf16[256,896]{1,0:T(8,128)(2,1)} %get-tuple-element.57.mine), channel_id=1, source_target_pairs={{0,1},{1,0},{2,3},{3,2},{4,5},{5,4},{6,7},{7,6},{8,9},{9,8},{10,11... | collective-permute-start | bytes 1376264 | tf_op jit(solution)/shard_map/ppermute | solution.py:354
  72.5 5.2 %collective-permute-start = (f32[32,256]{1,0:T(8,128)S(1)}, f32[32,256]{1,0:T(8,128)S(1)}, u32[]{:S(2)}, u32[]{:S(2)}) collective-permute-start(f32[32,256]{1,0:T(8,128)S(1)} %fusion.grad_mine), channel_id=1, source_target_pairs={{0,1},{1,0},{2,3},{3,2},{4,5},{5,4},{6,7},{7,6},{8,9},{9,8},{10,11... | collective-permute-start | bytes 98312 | tf_op jit(solution)/shard_map/ppermute | solution.py:238
  75.7 2.0 %copy-start.20 = (f32[8,128]{1,0:T(8,128)S(1)}, f32[8,128]{1,0:T(8,128)}, u32[]{:S(2)}) copy-start(f32[8,128]{1,0:T(8,128)} %get-tuple-element.56.refs_0_) | copy-start | bytes 12292
  77.8 4.4 %collective-permute-start.26 = (bf16[256,1152]{1,0:T(8,128)(2,1)S(1)}, bf16[256,1152]{1,0:T(8,128)(2,1)S(1)}, u32[]{:S(2)}, u32[]{:S(2)}) collective-permute-start(bf16[256,1152]{1,0:T(8,128)(2,1)S(1)} %get-tuple-element.58.mine), channel_id=1, source_target_pairs={{0,1},{1,0},{2,3},{3,2},{4,5},{5,4},{6,7},{7,6},{8,9},{9,8},{10,11... | collective-permute-start | bytes 1769480 | tf_op jit(solution)/shard_map/ppermute | solution.py:354
  78.1 3.9 %collective-permute-start.22 = (f32[1,32,256]{2,1,0:T(8,128)S(1)}, f32[1,32,256]{2,1,0:T(8,128)S(1)}, u32[]{:S(2)}, u32[]{:S(2)}) collective-permute-start(f32[1,32,256]{2,1,0:T(8,128)S(1)} %shards.5), channel_id=1, source_target_pairs={{0,1},{1,0},{2,3},{3,2},{4,5},{5,4},{6,7},{7,6},{8,9},{9,8},{10,11... | collective-permute-start | bytes 98312 | tf_op jit(solution)/shard_map/ppermute | solution.py:345
  78.3 7.7 %collective-permute-start.20 = (f32[32,256]{1,0:T(8,128)S(1)}, f32[32,256]{1,0:T(8,128)S(1)}, u32[]{:S(2)}, u32[]{:S(2)}) collective-permute-start(f32[32,256]{1,0:T(8,128)S(1)} %get-tuple-element.61), channel_id=1, source_target_pairs={{0,12},{4,0},{8,4},{12,8},{1,13},{5,1},{9,5},{13,9},{2,14},{6,2},{... | collective-permute-start | bytes 98312 | tf_op jit(solution)/shard_map/ppermute | solution.py:348
  82.0 9.0 %copy-start.21 = (s32[256,2]{0,1:T(2,128)S(1)}, s32[256,2]{0,1:T(2,128)}, u32[]{:S(2)}) copy-start(s32[256,2]{0,1:T(2,128)} %param.10) | copy-start | bytes 6148
  82.0 8.9 %copy-start.22 = (s32[1,256]{1,0:T(1,128)S(1)}, s32[1,256]{1,0:T(1,128)}, u32[]{:S(2)}) copy-start(s32[1,256]{1,0:T(1,128)} %docs.1) | copy-start | bytes 3076
  82.0 4.9 %collective-permute-start.23 = (f32[32,256]{1,0:T(8,128)S(1)}, f32[32,256]{1,0:T(8,128)S(1)}, u32[]{:S(2)}, u32[]{:S(2)}) collective-permute-start(f32[32,256]{1,0:T(8,128)S(1)} %add_bitcast_fusion), channel_id=1, source_target_pairs={{0,8},{4,12},{8,0},{12,4},{1,9},{5,13},{9,1},{13,5},{2,10},{6,14},... | collective-permute-start | bytes 98312 | tf_op jit(solution)/shard_map/ppermute | solution.py:348
  83.6 5.7 %collective-permute-start.27 = (f32[32,256]{1,0:T(8,128)S(1)}, f32[32,256]{1,0:T(8,128)S(1)}, u32[]{:S(2)}, u32[]{:S(2)}) collective-permute-start(f32[32,256]{1,0:T(8,128)S(1)} %part.3), channel_id=1, source_target_pairs={{0,4},{1,5},{4,8},{5,9},{8,12},{9,13},{12,0},{13,1},{2,6},{3,7},{6... | collective-permute-start | bytes 98312 | tf_op jit(solution)/shard_map/ppermute | solution.py:372
  85.6 5.3 %collective-permute-start.28 = (f32[32,256]{1,0:T(8,128)S(1)}, f32[32,256]{1,0:T(8,128)S(1)}, u32[]{:S(2)}, u32[]{:S(2)}) collective-permute-start(f32[32,256]{1,0:T(8,128)S(1)} %part.3), channel_id=1, source_target_pairs={{0,5},{1,4},{4,9},{5,8},{8,13},{9,12},{12,1},{13,0},{2,7},{3,6},{6... | collective-permute-start | bytes 98312 | tf_op jit(solution)/shard_map/ppermute | solution.py:373
  (12 other events, 13.4 us)

commit v5 on v4

--- a/solution.py
+++ b/solution.py
@@ -180,8 +180,12 @@
     )(*args)
 
 
-def grads_kernel(experts, where, grad_mine, grad_other, docs, routes, *refs):
-    codes_of_step, (cross, out, by_expert) = refs[:experts], refs[experts:]
+def grads_kernel(steps, experts, where, grad_mine, grad_other, docs, routes, *refs):
+    refs = list(refs)
+    codes_of_step = [refs.pop(0) for _ in steps]
+    cross = refs.pop(0) if experts - 1 in steps else None
+    before = refs.pop(0) if cross is not None else None
+    out, by_expert = refs
     rank = grad_mine.shape[0]
     group = LANES // rank
     long = rank // group
@@ -196,10 +200,14 @@
         ],
         axis=0,
     )
-    for k in range(experts):
-        codes = codes_of_step[k][...]
-        by_expert[lax.rem(home + k, experts)] = codes if k < experts - 1 else codes + cross[...]
-    for expert in range(experts):
+    here = [lax.rem(home + k, experts) for k in steps]
+    for expert, codes in zip(here, codes_of_step):
+        by_expert[expert] = codes[...] if cross is None else codes[...] + cross[...]
+    if before is not None:
+        out[...] = before[...]
+    else:
+        by_expert[lax.rem(home + experts - 1, experts)] = jnp.zeros_like(by_expert[0])
+    for expert in range(experts) if before is None else here:
         named = (routes[0:1, :] == expert) | (routes[1:2, :] == expert)
         codes = jnp.where(named, by_expert[expert], 0.0)
         block = lax.dot_general(
@@ -213,10 +221,17 @@
         wide = jnp.concatenate(
             [block[q * rows : (q + 1) * rows] for q in range(group)], axis=1
         )
-        for d in range(DOCS_DEV):
-            for i in range(long):
-                at = d * long + i
-                out[d, expert : expert + 1, i * LANES : (i + 1) * LANES] = wide[at : at + 1]
+        for place in range(experts):
+            def store():
+                for d in range(DOCS_DEV):
+                    for i in range(long):
+                        at, lanes = d * long + i, slice(i * LANES, (i + 1) * LANES)
+                        out[d, place : place + 1, lanes] = wide[at : at + 1]
+
+            if before is not None:
+                pl.when(expert == place)(store)
+            elif expert == place:
+                store()
 
 
 def on_device(tokens, cotangent, routes, doc_ids, gate_weight, up_weight, proj_in, proj_out):
@@ -309,10 +324,12 @@
             break
         for j in range(count):
             wave += 1
-            late = waves[wave] if wave < len(waves) else []
+            late, others = waves[wave] if wave < len(waves) else [], []
             ready = exchanged.pop(0)
+            if wave == 3:
+                others = [grad_other]
             sizes = [1, len(ready), len(arriving), len(swapping), len(late)]
-            turn, got = ordered(turn, [moved[j], *ready, *arriving, *swapping, *late])
+            turn, got = ordered(turn, [moved[j], *ready, *arriving, *swapping, *late], others)
             got = [got[sum(sizes[:n]) : sum(sizes[: n + 1])] for n in range(len(sizes))]
             moved[j] = got[0][0]
             flat += got[1]
@@ -347,7 +364,7 @@
             back = [(z, (z - k) % experts) for z in range(experts)]
             codes.append(found[0] if k == 0 else lax.ppermute(found[k - low], "exp", back))
 
-    made, total = [grad_other, codes[0], raw[0]], None
+    made, total = [codes[0], raw[0]], None
     for j in range(count):
         last = j == count - 1
         turn, (x,) = ordered(turn, [mine[-1][j]], made, False) if j else (turn, [mine[-1][j]])
@@ -360,7 +377,6 @@
             (rank, tokens.shape[0]) if last else (tokens.shape[0], 2 * gate.shape[1]),
             "part",
         )
-        made += [total[:8, :LANES]]
     home_pairs = [
         [
             (z * 2 + c, (z + 1) % experts * 2 + (c ^ flip))
@@ -372,22 +388,22 @@
     codes.append(lax.ppermute(total, ("exp", "mdl"), home_pairs[0]))
     cross = lax.ppermute(total, ("exp", "mdl"), home_pairs[1])
 
-    tok_count = tokens.shape[0]
-    vmem = pl.BlockSpec(memory_space=pltpu.VMEM)
-    return pl.pallas_call(
-        functools.partial(grads_kernel, experts),
-        in_specs=[pl.BlockSpec(memory_space=pltpu.SMEM)] + [vmem] * (5 + experts),
-        out_specs=vmem,
-        out_shape=jax.ShapeDtypeStruct((DOCS_DEV, experts, rank * rank), jnp.float32),
-        scratch_shapes=[pltpu.VMEM((experts, rank, tok_count), jnp.float32)],
-        compiler_params=pltpu.CompilerParams(vmem_limit_bytes=4 * 2**20),
-        cost_estimate=pl.CostEstimate(
-            flops=2 * experts * DOCS_DEV * rank * rank * tok_count,
-            bytes_accessed=2**20,
-            transcendentals=0,
-        ),
-        name="doc_grads",
-    )(home.reshape(1), grad_mine, grad_other, doc_ids, routes.T, *codes, cross)
+    def grads(steps, more):
+        vmem = pl.BlockSpec(memory_space=pltpu.VMEM)
+        args = [grad_mine, grad_other, doc_ids, routes.T, *[codes[k] for k in steps], *more]
+        return pl.pallas_call(
+            functools.partial(grads_kernel, steps, experts),
+            in_specs=[pl.BlockSpec(memory_space=pltpu.SMEM)] + [vmem] * len(args),
+            out_specs=vmem,
+            out_shape=jax.ShapeDtypeStruct((DOCS_DEV, experts, rank * rank), jnp.float32),
+            scratch_shapes=[pltpu.VMEM((experts, rank, tokens.shape[0]), jnp.float32)],
+            compiler_params=pltpu.CompilerParams(vmem_limit_bytes=4 * 2**20),
+            cost_estimate=FREE,
+            name="doc_grads",
+        )(home.reshape(1), *args)
+
+    first = grads(range(experts - 1), ())
+    return grads(range(experts - 1, experts), (cross, first))
 
 
 def solution(mesh):

time: 92.6 us -> 90.7 us (0.979)
  starting transfers between devices: 26.6 us -> 24.1 us
  Pallas kernels: 18.1 us -> 19.2 us
    ppermute x4, waiting for transfers between devices: 16.4 us -> 12.7 us  [along_dat(): lax.ppermute(x, 'dat', [((z + k) % dats, z) for z in range(dats)])]
    ppermute x6, waiting for transfers between devices: 12.9 us -> 15.2 us  [on_device(): moved = [lax.ppermute(x, 'exp', ring) for x in mine[-1]]]
    ppermute x2, starting transfers between devices: 3.77 us -> 2 us  [on_device(): lax.ppermute(found[k - low], 'exp', back)]
    ppermute x2, waiting for transfers between devices: 0.01 us -> 1.44 us  [on_device(): found = raw + lax.ppermute(raw, 'mdl', swap)]
    ppermute x1, waiting for transfers between devices: 0.01 us -> 1.19 us  [on_device(): grad_other = lax.ppermute(grad_mine, 'mdl', swap)]
    unnamed x62 -> x54, local copies, waits for them, and re-layouts: 3.02 us -> 2.69 us
  transfers between devices with their start and end apart: 29 -> 29, of which waited for: 10 -> 15; matrix products, arithmetic and copies ran while one was open for 8% -> 8% of each run, Pallas kernels for 18% -> 20%
where the time goes in v5:
time: 90.7 us; the launch traced here: 90.4 us
  waiting for transfers between devices  35.5 us (39%)
  starting transfers between devices  24.1 us (27%)
  Pallas kernels  19.2 us (21%)
  other arithmetic  6.12 us (7%)
  local copies, waits for them, and re-layouts  4.65 us (5%)
    ppermute x6, waiting for transfers between devices, on_device(): moved = [lax.ppermute(x, 'exp', ring) for x in mine[-1]]  15.2 us
    ppermute x4, waiting for transfers between devices, along_dat(): lax.ppermute(x, 'dat', [((z + k) % dats, z) for z in range(dats)])  12.7 us
    pallas_call x5, Pallas kernels, vmem_call(): pl.pallas_call(kernel, in_specs=[hbm] * far + [vmem] * (len(args) - far),...  12.4 us
    ppermute x6, starting transfers between devices, on_device(): moved = [lax.ppermute(x, 'exp', ring) for x in mine[-1]]  6.47 us
    ppermute x4, starting transfers between devices, over_grp(): return [lax.ppermute(x, 'grp', swap) for x in xs]  6.05 us
    select_n x3, other arithmetic, on_device(): jnp.where(grp == 0, gate[low:high], up[low:high])  6.03 us
    ppermute x4, starting transfers between devices, along_dat(): lax.ppermute(x, 'dat', [((z + k) % dats, z) for z in range(dats)])  5.96 us
    pallas_call x2, Pallas kernels, join(): pl.pallas_call(functools.partial(join_kernel, dats, edges), in_specs=[pl....  5.17 us
  transfers between devices with their start and end apart: 29, of which 15 were waited for; matrix products, arithmetic and copies ran while one was open for 8% of the time, Pallas kernels for 20%

profile of v5, /device:TPU:0, one launch (start us, length us, event | category | flops | bytes accessed | tf_op | source)
XLA Modules:
  0.0 90.4 jit_solution(5506259356101243129)
XLA Ops:
  0.0 1.2 %slice.47.refs_0_ = bf16[256,896]{1,0:T(8,128)(2,1)S(1)} slice(bf16[256,2048]{1,0:T(8,128)(2,1)} %param.8), slice={[0:256], [0:896]} | slice | bytes 917504 | tf_op jit(solution)/shard_map/slice | solution.py:260
  1.2 3.1 %collective-permute-start.1 = (bf16[256,896]{1,0:T(8,128)(2,1)S(1)}, bf16[256,896]{1,0:T(8,128)(2,1)}, u32[]{:S(2)}, u32[]{:S(2)}) collective-permute-start(bf16[256,896]{1,0:T(8,128)(2,1)S(1)} %slice.47.refs_0_), channel_id=1, source_target_pairs={{0,4},{4,8},{8,12},{12,0},{1,5},{5,9},{9,13},{13,1},{2,6},{6,10},{... | collective-permute-start | bytes 1376264 | tf_op jit(solution)/shard_map/ppermute | solution.py:321
  4.3 2.3 %select_bitcast_fusion = (bf16[576,384]{1,0:T(8,128)(2,1)}, bf16[576,384]{1,0:T(8,128)(2,1)S(1)}) fusion(bf16[1,2048,384]{2,1,0:T(8,128)(2,1)} %param.13, bf16[1,2048,384]{2,1,0:T(8,128)(2,1)} %param.12, pred[]{:T(512)S(6)} %eq.2), kind=kLoop, calls=%fused_computation | loop fusion | flops 442368 | bytes 2654209 | tf_op jit(solution)/shard_map/jit(_where)/select_n | solution.py:271
  6.6 1.5 %collective-permute-start.2 = (bf16[576,384]{1,0:T(8,128)(2,1)S(1)}, bf16[576,384]{1,0:T(8,128)(2,1)S(1)}, u32[]{:S(2)}, u32[]{:S(2)}) collective-permute-start(bf16[576,384]{1,0:T(8,128)(2,1)S(1)} %get-tuple-element.60), channel_id=1, source_target_pairs={{2,0},{0,2},{3,1},{1,3},{6,4},{4,6},{7,5},{5,7},{10,8},{8,10},{11,... | collective-permute-start | bytes 1327112 | tf_op jit(solution)/shard_map/ppermute | solution.py:278
  8.2 1.6 %collective-permute-start.3 = (bf16[256,1152]{1,0:T(8,128)(2,1)S(1)}, bf16[256,1152]{1,0:T(8,128)(2,1)S(1)}, u32[]{:S(2)}, u32[]{:S(2)}) collective-permute-start(bf16[256,1152]{1,0:T(8,128)(2,1)S(1)} %slice.52.refs_1_), channel_id=1, source_target_pairs={{0,4},{4,8},{8,12},{12,0},{1,5},{5,9},{9,13},{13,1},{2,6},{6,10},{... | collective-permute-start | bytes 1769480 | tf_op jit(solution)/shard_map/ppermute | solution.py:321
  10.0 8.2 %collective-permute-done.2.refs_2_ = bf16[576,384]{1,0:T(8,128)(2,1)S(1)} collective-permute-done((bf16[576,384]{1,0:T(8,128)(2,1)S(1)}, bf16[576,384]{1,0:T(8,128)(2,1)S(1)}, u32[]{:S(2)}, u32[]{:S(2)}) %collective-permute-start.2) | collective-permute-done | bytes 442400 | tf_op jit(solution)/shard_map/ppermute | solution.py:278
  18.2 0.6 broadcast_in_dim.3.refs_0_
  19.0 1.5 %collective-permute-start.7 = (bf16[576,384]{1,0:T(8,128)(2,1)}, bf16[576,384]{1,0:T(8,128)(2,1)}, u32[]{:S(2)}, u32[]{:S(2)}) collective-permute-start(bf16[576,384]{1,0:T(8,128)(2,1)} %get-tuple-element.34.refs_0_), channel_id=1, source_target_pairs={{0,16},{16,0},{1,17},{17,1},{2,18},{18,2},{3,19},{19,3},{4,20},{20... | collective-permute-start | bytes 1327112 | tf_op jit(solution)/shard_map/ppermute | solution.py:284
  20.5 1.5 %collective-permute-start.6 = (bf16[576,384]{1,0:T(8,128)(2,1)}, bf16[576,384]{1,0:T(8,128)(2,1)}, u32[]{:S(2)}, u32[]{:S(2)}) collective-permute-start(bf16[576,384]{1,0:T(8,128)(2,1)} %get-tuple-element.33), channel_id=1, source_target_pairs={{2,0},{0,2},{3,1},{1,3},{6,4},{4,6},{7,5},{5,7},{10,8},{8,10},{11,... | collective-permute-start | bytes 1327112 | tf_op jit(solution)/shard_map/ppermute | solution.py:278
  22.0 0.8 copy-done.11
  22.8 1.6 %collective-permute-start.8 = (bf16[256,896]{1,0:T(8,128)(2,1)}, bf16[256,896]{1,0:T(8,128)(2,1)}, u32[]{:S(2)}, u32[]{:S(2)}) collective-permute-start(bf16[256,896]{1,0:T(8,128)(2,1)} %get-tuple-element.36.refs_4_), channel_id=1, source_target_pairs={{0,4},{4,8},{8,12},{12,0},{1,5},{5,9},{9,13},{13,1},{2,6},{6,10},{... | collective-permute-start | bytes 1376264 | tf_op jit(solution)/shard_map/ppermute | solution.py:321
  24.4 1.9 %select_bitcast_fusion.2.refs_6_ = bf16[512,384]{1,0:T(8,128)(2,1)} fusion(bf16[1,2048,384]{2,1,0:T(8,128)(2,1)} %param.13, bf16[1,2048,384]{2,1,0:T(8,128)(2,1)} %param.12, pred[]{:T(512)S(6)} %eq.2), kind=kLoop, calls=%fused_computation.2 | loop fusion | flops 196608 | bytes 1179649 | tf_op jit(solution)/shard_map/jit(_where)/select_n | solution.py:271
  26.3 4.0 %collective-permute-done.3.refs_1_ = bf16[256,1152]{1,0:T(8,128)(2,1)S(1)} collective-permute-done((bf16[256,1152]{1,0:T(8,128)(2,1)S(1)}, bf16[256,1152]{1,0:T(8,128)(2,1)S(1)}, u32[]{:S(2)}, u32[]{:S(2)}) %collective-permute-start.3) | collective-permute-done | bytes 589856 | tf_op jit(solution)/shard_map/ppermute | solution.py:321
  30.3 1.0 %collective-permute-done.6.refs_4_ = bf16[576,384]{1,0:T(8,128)(2,1)} collective-permute-done((bf16[576,384]{1,0:T(8,128)(2,1)}, bf16[576,384]{1,0:T(8,128)(2,1)}, u32[]{:S(2)}, u32[]{:S(2)}) %collective-permute-start.6) | collective-permute-done | bytes 442400 | tf_op jit(solution)/shard_map/ppermute | solution.py:278
  31.4 1.8 %collective-permute-start.11 = (bf16[576,384]{1,0:T(8,128)(2,1)}, bf16[576,384]{1,0:T(8,128)(2,1)S(1)}, u32[]{:S(2)}, u32[]{:S(2)}) collective-permute-start(bf16[576,384]{1,0:T(8,128)(2,1)} %get-tuple-element.38.refs_1_), channel_id=1, source_target_pairs={{0,16},{16,0},{1,17},{17,1},{2,18},{18,2},{3,19},{19,3},{4,20},{20... | collective-permute-start | bytes 1327112 | tf_op jit(solution)/shard_map/ppermute | solution.py:284
  33.2 1.5 %collective-permute-start.10 = (bf16[512,384]{1,0:T(8,128)(2,1)}, bf16[512,384]{1,0:T(8,128)(2,1)S(1)}, u32[]{:S(2)}, u32[]{:S(2)}) collective-permute-start(bf16[512,384]{1,0:T(8,128)(2,1)} %get-tuple-element.37), channel_id=1, source_target_pairs={{2,0},{0,2},{3,1},{1,3},{6,4},{4,6},{7,5},{5,7},{10,8},{8,10},{11,... | collective-permute-start | bytes 1179656 | tf_op jit(solution)/shard_map/ppermute | solution.py:278
  34.6 0.4 fusion.grad_mine
  35.1 1.2 %collective-permute-done.refs_6_.grad_other = f32[32,256]{1,0:T(8,128)S(1)} collective-permute-done((f32[32,256]{1,0:T(8,128)S(1)}, f32[32,256]{1,0:T(8,128)S(1)}, u32[]{:S(2)}, u32[]{:S(2)}) %collective-permute-start) | collective-permute-done | bytes 32800 | tf_op jit(solution)/shard_map/ppermute | solution.py:253
  36.5 2.9 %collective-permute-done.8.refs_1_ = bf16[256,896]{1,0:T(8,128)(2,1)} collective-permute-done((bf16[256,896]{1,0:T(8,128)(2,1)}, bf16[256,896]{1,0:T(8,128)(2,1)}, u32[]{:S(2)}, u32[]{:S(2)}) %collective-permute-start.8) | collective-permute-done | bytes 458784 | tf_op jit(solution)/shard_map/ppermute | solution.py:321
  39.4 1.8 %select_bitcast_fusion.3.refs_5_ = bf16[384,384]{1,0:T(8,128)(2,1)} fusion(bf16[1,2048,384]{2,1,0:T(8,128)(2,1)} %param.13, bf16[1,2048,384]{2,1,0:T(8,128)(2,1)} %param.12, pred[]{:T(512)S(6)} %eq.2), kind=kLoop, calls=%fused_computation.3 | loop fusion | flops 147456 | bytes 884737 | tf_op jit(solution)/shard_map/jit(_where)/select_n | solution.py:271
  41.3 3.1 %collective-permute-done.10.refs_3_ = bf16[512,384]{1,0:T(8,128)(2,1)S(1)} collective-permute-done((bf16[512,384]{1,0:T(8,128)(2,1)}, bf16[512,384]{1,0:T(8,128)(2,1)S(1)}, u32[]{:S(2)}, u32[]{:S(2)}) %collective-permute-start.10) | collective-permute-done | bytes 393248 | tf_op jit(solution)/shard_map/ppermute | solution.py:278
  44.4 0.8 copy-done.23
  45.3 1.2 %collective-permute-start.15 = (bf16[512,384]{1,0:T(8,128)(2,1)}, bf16[512,384]{1,0:T(8,128)(2,1)}, u32[]{:S(2)}, u32[]{:S(2)}) collective-permute-start(bf16[512,384]{1,0:T(8,128)(2,1)} %get-tuple-element.42.refs_2_), channel_id=1, source_target_pairs={{0,16},{16,0},{1,17},{17,1},{2,18},{18,2},{3,19},{19,3},{4,20},{20... | collective-permute-start | bytes 1179656 | tf_op jit(solution)/shard_map/ppermute | solution.py:284
  46.5 1.5 %collective-permute-start.14 = (bf16[384,384]{1,0:T(8,128)(2,1)}, bf16[384,384]{1,0:T(8,128)(2,1)}, u32[]{:S(2)}, u32[]{:S(2)}) collective-permute-start(bf16[384,384]{1,0:T(8,128)(2,1)} %get-tuple-element.41), channel_id=1, source_target_pairs={{2,0},{0,2},{3,1},{1,3},{6,4},{4,6},{7,5},{5,7},{10,8},{8,10},{11,... | collective-permute-start | bytes 884744 | tf_op jit(solution)/shard_map/ppermute | solution.py:278
  48.0 6.5 %collective-permute-done.12.refs_1_ = bf16[256,1152]{1,0:T(8,128)(2,1)S(1)} collective-permute-done((bf16[256,1152]{1,0:T(8,128)(2,1)}, bf16[256,1152]{1,0:T(8,128)(2,1)S(1)}, u32[]{:S(2)}, u32[]{:S(2)}) %collective-permute-start.12) | collective-permute-done | bytes 589856 | tf_op jit(solution)/shard_map/ppermute | solution.py:321
  54.5 0.4 collective-permute-done.14.refs_3_
  54.9 0.9 collective-permute-done.15.refs_4_
  55.9 1.6 %collective-permute-start.18 = (bf16[384,384]{1,0:T(8,128)(2,1)}, bf16[384,384]{1,0:T(8,128)(2,1)S(1)}, u32[]{:S(2)}, u32[]{:S(2)}) collective-permute-start(bf16[384,384]{1,0:T(8,128)(2,1)} %get-tuple-element.45.refs_0_), channel_id=1, source_target_pairs={{0,16},{16,0},{1,17},{17,1},{2,18},{18,2},{3,19},{19,3},{4,20},{20... | collective-permute-start | bytes 884744 | tf_op jit(solution)/shard_map/ppermute | solution.py:284
  57.5 3.4 %join.2.refs_8_.refs_4_.refs_0_ = bf16[2,1664,768]{2,1,0:T(8,128)(2,1)S(1)} custom-call(s32[3]{0:T(128)S(1)} %pad_add_fusion.where, bf16[2048,384]{1,0:T(8,128)(2,1)} %bitcast.34, bf16[2048,384]{1,0:T(8,128)(2,1)} %bitcast.32, bf16[576,384]{1,0:T(8,128)(2,1)} %get-tuple-element.34.refs_0_, bf16[576,384]{1,0:T(8,128)(2,1)} %get-tuple-element.38.refs_1_, ...), custom_call_target="tpu_custom_call" | custom-call | flops 1 | bytes 1 | tf_op jit(solution)/shard_map/join/pallas_call | solution.py:74
  61.0 4.1 %shards.3.refs_9_ = f32[2,256,768]{2,1,0:T(8,128)S(1)} custom-call(bf16[256,896]{1,0:T(8,128)(2,1)S(1)} %copy-done.8, bf16[256,1152]{1,0:T(8,128)(2,1)S(1)} %slice.52.refs_1_, bf16[256,896]{1,0:T(8,128)(2,1)S(1)} %copy-done.12, bf16[256,1152]{1,0:T(8,128)(2,1)S(1)} %copy-done.6, bf16[256,896]{1,0:T(8,128)(2,1)} %get-tuple-element.36.refs_4_, ...), custom_call_target="tpu_custom_call" | custom-call | flops 1 | bytes 1 | tf_op jit(solution)/shard_map/shards/pallas_call | solution.py:171
  65.1 0.3 collective-permute-done.18.refs_3_
  65.4 0.5 copy-done.15
  65.9 0.3 copy-done.24
  66.1 1.8 %join.3.refs_8_.refs_5_.refs_1_ = bf16[2,384,768]{2,1,0:T(8,128)(2,1)S(1)} custom-call(s32[3]{0:T(128)S(1)} %pad_add_fusion.where, bf16[2048,384]{1,0:T(8,128)(2,1)} %bitcast.35, bf16[2048,384]{1,0:T(8,128)(2,1)} %bitcast.33, bf16[384,384]{1,0:T(8,128)(2,1)} %get-tuple-element.45.refs_0_, bf16[384,384]{1,0:T(8,128)(2,1)} %get-tuple-element.55.refs_1_), custom_call_target="tpu_custom_call" | custom-call | flops 1 | bytes 1 | tf_op jit(solution)/shard_map/join/pallas_call | solution.py:74
  68.0 1.5 %shards.4 = f32[2,32,256]{2,1,0:T(8,128)S(1)} custom-call(bf16[256,896]{1,0:T(8,128)(2,1)S(1)} %copy-done.8, bf16[256,1152]{1,0:T(8,128)(2,1)S(1)} %slice.52.refs_1_, bf16[256,896]{1,0:T(8,128)(2,1)S(1)} %copy-done.12, bf16[256,1152]{1,0:T(8,128)(2,1)S(1)} %copy-done.6, bf16[256,896]{1,0:T(8,128)(2,1)} %get-tuple-element.36.refs_4_, ...), custom_call_target="tpu_custom_call" | custom-call | flops 1 | bytes 1 | tf_op jit(solution)/shard_map/shards/pallas_call | solution.py:171
  69.6 1.2 %collective-permute-done.20 = f32[2,32,256]{2,1,0:T(8,128)S(1)} collective-permute-done((f32[2,32,256]{2,1,0:T(8,128)S(1)}, f32[2,32,256]{2,1,0:T(8,128)S(1)}, u32[]{:S(2)}, u32[]{:S(2)}) %collective-permute-start.20) | collective-permute-done | bytes 65568 | tf_op jit(solution)/shard_map/ppermute | solution.py:362
  70.9 3.5 %shards.5 = f32[1,32,256]{2,1,0:T(8,128)S(1)} custom-call(bf16[256,896]{1,0:T(8,128)(2,1)} %get-tuple-element.44.refs_0_, bf16[256,1152]{1,0:T(8,128)(2,1)S(1)} %copy-done.14, bf16[256,896]{1,0:T(8,128)(2,1)S(1)} %copy-done.16, bf16[256,1152]{1,0:T(8,128)(2,1)S(1)} %collective-permute-done.21.refs_3_, bf16[2,1664,768]{2,1,0:T(8,128)(2,1)S(1)} %join.2.refs_8_.refs_4_.refs_0_, ...), custom_call_target="tpu_custom_call" | custom-call | flops 1 | bytes 1 | tf_op jit(solution)/shard_map/shards/pallas_call | solution.py:171
  74.4 1.8 %collective-permute-done.19.refs_1_ = bf16[256,1152]{1,0:T(8,128)(2,1)S(1)} collective-permute-done((bf16[256,1152]{1,0:T(8,128)(2,1)}, bf16[256,1152]{1,0:T(8,128)(2,1)S(1)}, u32[]{:S(2)}, u32[]{:S(2)}) %collective-permute-start.19) | collective-permute-done | bytes 589856 | tf_op jit(solution)/shard_map/ppermute | solution.py:321
  76.2 0.5 collective-permute-start.23
  76.7 2.0 %collective-permute-start.26 = (f32[32,256]{1,0:T(8,128)S(1)}, f32[32,256]{1,0:T(8,128)S(1)}, u32[]{:S(2)}, u32[]{:S(2)}) collective-permute-start(f32[32,256]{1,0:T(8,128)S(1)} %get-tuple-element.61), channel_id=1, source_target_pairs={{0,12},{4,0},{8,4},{12,8},{1,13},{5,1},{9,5},{13,9},{2,14},{6,2},{... | collective-permute-start | bytes 98312 | tf_op jit(solution)/shard_map/ppermute | solution.py:365
  78.9 2.0 %part.2.refs_2_ = f32[256,768]{1,0:T(8,128)S(1)} custom-call(bf16[256,896]{1,0:T(8,128)(2,1)} %get-tuple-element.58.mine, bf16[256,896]{1,0:T(8,128)(2,1)S(1)} %collective-permute-done.23.other, bf16[2,1664,768]{2,1,0:T(8,128)(2,1)S(1)} %join.2.refs_8_.refs_4_.refs_0_, bf16[2,384,768]{2,1,0:T(8,128)(2,1)S(1)} %join.3.refs_8_.refs_5_.refs_1_), custom_call_target="tpu_custom_call" | custom-call | flops 1 | bytes 1 | tf_op jit(solution)/shard_map/part/pallas_call | solution.py:171
  81.0 1.4 %part.3 = f32[32,256]{1,0:T(8,128)S(1)} custom-call(bf16[256,1152]{1,0:T(8,128)(2,1)S(1)} %get-tuple-element.57.mine, bf16[256,1152]{1,0:T(8,128)(2,1)S(1)} %collective-permute-done.22.other, bf16[2,1664,768]{2,1,0:T(8,128)(2,1)S(1)} %join.2.refs_8_.refs_4_.refs_0_, bf16[2,384,768]{2,1,0:T(8,128)(2,1)S(1)} %join.3.refs_8_.refs_5_.refs_1_, ...), custom_call_target="tpu_custom_call" | custom-call | flops 1 | bytes 1 | tf_op jit(solution)/shard_map/part/pallas_call | solution.py:171
  82.3 1.8 %collective-permute-start.24 = (f32[32,256]{1,0:T(8,128)S(1)}, f32[32,256]{1,0:T(8,128)S(1)}, u32[]{:S(2)}, u32[]{:S(2)}) collective-permute-start(f32[32,256]{1,0:T(8,128)S(1)} %part.3), channel_id=1, source_target_pairs={{0,4},{1,5},{4,8},{5,9},{8,12},{9,13},{12,0},{13,1},{2,6},{3,7},{6... | collective-permute-start | bytes 98312 | tf_op jit(solution)/shard_map/ppermute | solution.py:388
  84.2 0.9 collective-permute-start.25
  85.1 0.7 doc_grads.2.refs_2_
  85.7 2.4 %collective-permute-done.24.refs_0_ = f32[32,256]{1,0:T(8,128)S(1)} collective-permute-done((f32[32,256]{1,0:T(8,128)S(1)}, f32[32,256]{1,0:T(8,128)S(1)}, u32[]{:S(2)}, u32[]{:S(2)}) %collective-permute-start.24) | collective-permute-done | bytes 32800 | tf_op jit(solution)/shard_map/ppermute | solution.py:388
  88.1 1.3 %collective-permute-done.25.refs_1_ = f32[32,256]{1,0:T(8,128)S(1)} collective-permute-done((f32[32,256]{1,0:T(8,128)S(1)}, f32[32,256]{1,0:T(8,128)S(1)}, u32[]{:S(2)}, u32[]{:S(2)}) %collective-permute-start.25) | collective-permute-done | bytes 32800 | tf_op jit(solution)/shard_map/ppermute | solution.py:389
  89.4 1.0 %doc_grads.3 = f32[4,4,1024]{2,1,0:T(4,128)} custom-call(s32[1]{0:T(128)} %bitcast.where, f32[32,256]{1,0:T(8,128)S(1)} %fusion.grad_mine, f32[32,256]{1,0:T(8,128)S(1)} %collective-permute-done.refs_6_.grad_other, s32[1,256]{1,0:T(1,128)S(1)} %copy-done.20, s32[2,256]{1,0:T(2,128)S(1)} %bitcast.31, f32[32,256]{1,0:T(8,128)S(1)} %collective-permute-done.24.refs_0_, ...), custom_call_target="tpu_custom_call" | custom-call | flops 1 | bytes 1 | tf_op jit(solution)/shard_map/doc_grads/pallas_call | solution.py:394
  (92 shorter events, 1.5 us)
Async XLA Ops:
  0.0 34.6 %copy-start = (bf16[256,2048]{1,0:T(8,128)(2,1)S(1)}, bf16[256,2048]{1,0:T(8,128)(2,1)}, u32[]{:S(2)}) copy-start(bf16[256,2048]{1,0:T(8,128)(2,1)} %param.9) | copy-start | bytes 3145732
  0.0 8.1 %copy-start.25 = (bf16[256,2048]{1,0:T(8,128)(2,1)S(1)}, bf16[256,2048]{1,0:T(8,128)(2,1)}, u32[]{:S(2)}) copy-start(bf16[256,2048]{1,0:T(8,128)(2,1)} %param.8) | copy-start | bytes 3145732
  1.2 6.9 %copy-start.7 = (bf16[256,896]{1,0:T(8,128)(2,1)}, bf16[256,896]{1,0:T(8,128)(2,1)S(1)}, u32[]{:S(2)}) copy-start(bf16[256,896]{1,0:T(8,128)(2,1)S(1)} %slice.47.refs_0_) | copy-start | bytes 1376260
  1.2 17.0 %collective-permute-start.1 = (bf16[256,896]{1,0:T(8,128)(2,1)S(1)}, bf16[256,896]{1,0:T(8,128)(2,1)}, u32[]{:S(2)}, u32[]{:S(2)}) collective-permute-start(bf16[256,896]{1,0:T(8,128)(2,1)S(1)} %slice.47.refs_0_), channel_id=1, source_target_pairs={{0,4},{4,8},{8,12},{12,0},{1,5},{5,9},{9,13},{13,1},{2,6},{6,10},{... | collective-permute-start | bytes 1376264 | tf_op jit(solution)/shard_map/ppermute | solution.py:321
  6.6 19.7 %copy-start.26 = (bf16[32,2048]{1,0:T(8,128)(2,1)S(1)}, bf16[32,2048]{1,0:T(8,128)(2,1)}, u32[]{:S(2)}) copy-start(bf16[32,2048]{1,0:T(8,128)(2,1)} %param.15) | copy-start | bytes 393220
  6.6 11.6 %collective-permute-start.2 = (bf16[576,384]{1,0:T(8,128)(2,1)S(1)}, bf16[576,384]{1,0:T(8,128)(2,1)S(1)}, u32[]{:S(2)}, u32[]{:S(2)}) collective-permute-start(bf16[576,384]{1,0:T(8,128)(2,1)S(1)} %get-tuple-element.60), channel_id=1, source_target_pairs={{2,0},{0,2},{3,1},{1,3},{6,4},{4,6},{7,5},{5,7},{10,8},{8,10},{11,... | collective-permute-start | bytes 1327112 | tf_op jit(solution)/shard_map/ppermute | solution.py:278
  8.1 13.9 %collective-permute-start.4 = (bf16[256,896]{1,0:T(8,128)(2,1)S(1)}, bf16[256,896]{1,0:T(8,128)(2,1)S(1)}, u32[]{:S(2)}, u32[]{:S(2)}) collective-permute-start(bf16[256,896]{1,0:T(8,128)(2,1)S(1)} %slice.47.refs_0_), channel_id=1, source_target_pairs={{0,1},{1,0},{2,3},{3,2},{4,5},{5,4},{6,7},{7,6},{8,9},{9,8},{10,11... | collective-permute-start | bytes 1376264 | tf_op jit(solution)/shard_map/ppermute | solution.py:261
  8.2 22.2 %collective-permute-start.3 = (bf16[256,1152]{1,0:T(8,128)(2,1)S(1)}, bf16[256,1152]{1,0:T(8,128)(2,1)S(1)}, u32[]{:S(2)}, u32[]{:S(2)}) collective-permute-start(bf16[256,1152]{1,0:T(8,128)(2,1)S(1)} %slice.52.refs_1_), channel_id=1, source_target_pairs={{0,4},{4,8},{8,12},{12,0},{1,5},{5,9},{9,13},{13,1},{2,6},{6,10},{... | collective-permute-start | bytes 1769480 | tf_op jit(solution)/shard_map/ppermute | solution.py:321
  9.8 20.5 %collective-permute-start.5 = (bf16[256,1152]{1,0:T(8,128)(2,1)S(1)}, bf16[256,1152]{1,0:T(8,128)(2,1)S(1)}, u32[]{:S(2)}, u32[]{:S(2)}) collective-permute-start(bf16[256,1152]{1,0:T(8,128)(2,1)S(1)} %slice.52.refs_1_), channel_id=1, source_target_pairs={{0,1},{1,0},{2,3},{3,2},{4,5},{5,4},{6,7},{7,6},{8,9},{9,8},{10,11... | collective-permute-start | bytes 1769480 | tf_op jit(solution)/shard_map/ppermute | solution.py:261
  19.0 11.4 %collective-permute-start.7 = (bf16[576,384]{1,0:T(8,128)(2,1)}, bf16[576,384]{1,0:T(8,128)(2,1)}, u32[]{:S(2)}, u32[]{:S(2)}) collective-permute-start(bf16[576,384]{1,0:T(8,128)(2,1)} %get-tuple-element.34.refs_0_), channel_id=1, source_target_pairs={{0,16},{16,0},{1,17},{17,1},{2,18},{18,2},{3,19},{19,3},{4,20},{20... | collective-permute-start | bytes 1327112 | tf_op jit(solution)/shard_map/ppermute | solution.py:284
  20.5 10.9 %collective-permute-start.6 = (bf16[576,384]{1,0:T(8,128)(2,1)}, bf16[576,384]{1,0:T(8,128)(2,1)}, u32[]{:S(2)}, u32[]{:S(2)}) collective-permute-start(bf16[576,384]{1,0:T(8,128)(2,1)} %get-tuple-element.33), channel_id=1, source_target_pairs={{2,0},{0,2},{3,1},{1,3},{6,4},{4,6},{7,5},{5,7},{10,8},{8,10},{11,... | collective-permute-start | bytes 1327112 | tf_op jit(solution)/shard_map/ppermute | solution.py:278
  22.8 16.6 %collective-permute-start.8 = (bf16[256,896]{1,0:T(8,128)(2,1)}, bf16[256,896]{1,0:T(8,128)(2,1)}, u32[]{:S(2)}, u32[]{:S(2)}) collective-permute-start(bf16[256,896]{1,0:T(8,128)(2,1)} %get-tuple-element.36.refs_4_), channel_id=1, source_target_pairs={{0,4},{4,8},{8,12},{12,0},{1,5},{5,9},{9,13},{13,1},{2,6},{6,10},{... | collective-permute-start | bytes 1376264 | tf_op jit(solution)/shard_map/ppermute | solution.py:321
  30.3 10.9 %collective-permute-start.9 = (bf16[256,896]{1,0:T(8,128)(2,1)}, bf16[256,896]{1,0:T(8,128)(2,1)S(1)}, u32[]{:S(2)}, u32[]{:S(2)}) collective-permute-start(bf16[256,896]{1,0:T(8,128)(2,1)} %get-tuple-element.36.refs_4_), channel_id=1, source_target_pairs={{0,1},{1,0},{2,3},{3,2},{4,5},{5,4},{6,7},{7,6},{8,9},{9,8},{10,11... | collective-permute-start | bytes 1376264 | tf_op jit(solution)/shard_map/ppermute | solution.py:339
  31.4 13.0 %collective-permute-start.11 = (bf16[576,384]{1,0:T(8,128)(2,1)}, bf16[576,384]{1,0:T(8,128)(2,1)S(1)}, u32[]{:S(2)}, u32[]{:S(2)}) collective-permute-start(bf16[576,384]{1,0:T(8,128)(2,1)} %get-tuple-element.38.refs_1_), channel_id=1, source_target_pairs={{0,16},{16,0},{1,17},{17,1},{2,18},{18,2},{3,19},{19,3},{4,20},{20... | collective-permute-start | bytes 1327112 | tf_op jit(solution)/shard_map/ppermute | solution.py:284
  33.2 11.2 %collective-permute-start.10 = (bf16[512,384]{1,0:T(8,128)(2,1)}, bf16[512,384]{1,0:T(8,128)(2,1)S(1)}, u32[]{:S(2)}, u32[]{:S(2)}) collective-permute-start(bf16[512,384]{1,0:T(8,128)(2,1)} %get-tuple-element.37), channel_id=1, source_target_pairs={{2,0},{0,2},{3,1},{1,3},{6,4},{4,6},{7,5},{5,7},{10,8},{8,10},{11,... | collective-permute-start | bytes 1179656 | tf_op jit(solution)/shard_map/ppermute | solution.py:278
  35.1 1.3 %collective-permute-start = (f32[32,256]{1,0:T(8,128)S(1)}, f32[32,256]{1,0:T(8,128)S(1)}, u32[]{:S(2)}, u32[]{:S(2)}) collective-permute-start(f32[32,256]{1,0:T(8,128)S(1)} %fusion.grad_mine), channel_id=1, source_target_pairs={{0,1},{1,0},{2,3},{3,2},{4,5},{5,4},{6,7},{7,6},{8,9},{9,8},{10,11... | collective-permute-start | bytes 98312 | tf_op jit(solution)/shard_map/ppermute | solution.py:253
  36.3 18.2 %collective-permute-start.12 = (bf16[256,1152]{1,0:T(8,128)(2,1)}, bf16[256,1152]{1,0:T(8,128)(2,1)S(1)}, u32[]{:S(2)}, u32[]{:S(2)}) collective-permute-start(bf16[256,1152]{1,0:T(8,128)(2,1)} %get-tuple-element.40.refs_5_), channel_id=1, source_target_pairs={{0,4},{4,8},{8,12},{12,0},{1,5},{5,9},{9,13},{13,1},{2,6},{6,10},{... | collective-permute-start | bytes 1769480 | tf_op jit(solution)/shard_map/ppermute | solution.py:321
  39.4 15.1 %collective-permute-start.13 = (bf16[256,1152]{1,0:T(8,128)(2,1)}, bf16[256,1152]{1,0:T(8,128)(2,1)S(1)}, u32[]{:S(2)}, u32[]{:S(2)}) collective-permute-start(bf16[256,1152]{1,0:T(8,128)(2,1)} %get-tuple-element.40.refs_5_), channel_id=1, source_target_pairs={{0,1},{1,0},{2,3},{3,2},{4,5},{5,4},{6,7},{7,6},{8,9},{9,8},{10,11... | collective-permute-start | bytes 1769480 | tf_op jit(solution)/shard_map/ppermute | solution.py:339
  41.3 3.1 %copy-start.9 = (bf16[256,896]{1,0:T(8,128)(2,1)}, bf16[256,896]{1,0:T(8,128)(2,1)S(1)}, u32[]{:S(2)}) copy-start(bf16[256,896]{1,0:T(8,128)(2,1)S(1)} %collective-permute-done.9.refs_2_) | copy-start | bytes 1376260
  45.3 10.5 %collective-permute-start.15 = (bf16[512,384]{1,0:T(8,128)(2,1)}, bf16[512,384]{1,0:T(8,128)(2,1)}, u32[]{:S(2)}, u32[]{:S(2)}) collective-permute-start(bf16[512,384]{1,0:T(8,128)(2,1)} %get-tuple-element.42.refs_2_), channel_id=1, source_target_pairs={{0,16},{16,0},{1,17},{17,1},{2,18},{18,2},{3,19},{19,3},{4,20},{20... | collective-permute-start | bytes 1179656 | tf_op jit(solution)/shard_map/ppermute | solution.py:284
  46.5 8.4 %collective-permute-start.14 = (bf16[384,384]{1,0:T(8,128)(2,1)}, bf16[384,384]{1,0:T(8,128)(2,1)}, u32[]{:S(2)}, u32[]{:S(2)}) collective-permute-start(bf16[384,384]{1,0:T(8,128)(2,1)} %get-tuple-element.41), channel_id=1, source_target_pairs={{2,0},{0,2},{3,1},{1,3},{6,4},{4,6},{7,5},{5,7},{10,8},{8,10},{11,... | collective-permute-start | bytes 884744 | tf_op jit(solution)/shard_map/ppermute | solution.py:278
  48.0 17.1 %collective-permute-start.16 = (bf16[256,896]{1,0:T(8,128)(2,1)}, bf16[256,896]{1,0:T(8,128)(2,1)}, u32[]{:S(2)}, u32[]{:S(2)}) collective-permute-start(bf16[256,896]{1,0:T(8,128)(2,1)} %get-tuple-element.44.refs_0_), channel_id=1, source_target_pairs={{0,4},{4,8},{8,12},{12,0},{1,5},{5,9},{9,13},{13,1},{2,6},{6,10},{... | collective-permute-start | bytes 1376264 | tf_op jit(solution)/shard_map/ppermute | solution.py:321
  54.5 1.3 %copy-start.13 = (bf16[256,1152]{1,0:T(8,128)(2,1)}, bf16[256,1152]{1,0:T(8,128)(2,1)S(1)}, u32[]{:S(2)}) copy-start(bf16[256,1152]{1,0:T(8,128)(2,1)S(1)} %collective-permute-done.12.refs_1_) | copy-start | bytes 1769476
  54.5 10.6 %collective-permute-start.17 = (bf16[256,896]{1,0:T(8,128)(2,1)}, bf16[256,896]{1,0:T(8,128)(2,1)S(1)}, u32[]{:S(2)}, u32[]{:S(2)}) collective-permute-start(bf16[256,896]{1,0:T(8,128)(2,1)} %get-tuple-element.44.refs_0_), channel_id=1, source_target_pairs={{0,1},{1,0},{2,3},{3,2},{4,5},{5,4},{6,7},{7,6},{8,9},{9,8},{10,11... | collective-permute-start | bytes 1376264 | tf_op jit(solution)/shard_map/ppermute | solution.py:339
  54.5 1.3 %copy-start.1 = (bf16[256,1152]{1,0:T(8,128)(2,1)}, bf16[256,1152]{1,0:T(8,128)(2,1)S(1)}, u32[]{:S(2)}) copy-start(bf16[256,1152]{1,0:T(8,128)(2,1)S(1)} %collective-permute-done.13.refs_2_) | copy-start | bytes 1769476
  55.8 15.1 %collective-permute-start.21 = (bf16[256,1152]{1,0:T(8,128)(2,1)}, bf16[256,1152]{1,0:T(8,128)(2,1)S(1)}, u32[]{:S(2)}, u32[]{:S(2)}) collective-permute-start(bf16[256,1152]{1,0:T(8,128)(2,1)} %get-tuple-element.54.refs_1_), channel_id=1, source_target_pairs={{0,1},{1,0},{2,3},{3,2},{4,5},{5,4},{6,7},{7,6},{8,9},{9,8},{10,11... | collective-permute-start | bytes 1769480 | tf_op jit(solution)/shard_map/ppermute | solution.py:339
  55.9 20.3 %collective-permute-start.19 = (bf16[256,1152]{1,0:T(8,128)(2,1)}, bf16[256,1152]{1,0:T(8,128)(2,1)S(1)}, u32[]{:S(2)}, u32[]{:S(2)}) collective-permute-start(bf16[256,1152]{1,0:T(8,128)(2,1)} %get-tuple-element.54.refs_1_), channel_id=1, source_target_pairs={{0,4},{4,8},{8,12},{12,0},{1,5},{5,9},{9,13},{13,1},{2,6},{6,10},{... | collective-permute-start | bytes 1769480 | tf_op jit(solution)/shard_map/ppermute | solution.py:321
  55.9 9.6 %collective-permute-start.18 = (bf16[384,384]{1,0:T(8,128)(2,1)}, bf16[384,384]{1,0:T(8,128)(2,1)S(1)}, u32[]{:S(2)}, u32[]{:S(2)}) collective-permute-start(bf16[384,384]{1,0:T(8,128)(2,1)} %get-tuple-element.45.refs_0_), channel_id=1, source_target_pairs={{0,16},{16,0},{1,17},{17,1},{2,18},{18,2},{3,19},{19,3},{4,20},{20... | collective-permute-start | bytes 884744 | tf_op jit(solution)/shard_map/ppermute | solution.py:284
  57.5 3.4 %copy-start.2 = (bf16[256,1152]{1,0:T(8,128)(2,1)S(1)}, bf16[256,1152]{1,0:T(8,128)(2,1)}, u32[]{:S(2)}) copy-start(bf16[256,1152]{1,0:T(8,128)(2,1)} %get-tuple-element.49.refs_7_) | copy-start | bytes 1769476
  57.5 3.4 %copy-start.4 = (bf16[256,1152]{1,0:T(8,128)(2,1)S(1)}, bf16[256,1152]{1,0:T(8,128)(2,1)}, u32[]{:S(2)}) copy-start(bf16[256,1152]{1,0:T(8,128)(2,1)} %get-tuple-element.40.refs_5_) | copy-start | bytes 1769476
  57.5 3.4 %copy-start.6 = (bf16[256,1152]{1,0:T(8,128)(2,1)S(1)}, bf16[256,1152]{1,0:T(8,128)(2,1)}, u32[]{:S(2)}) copy-start(bf16[256,1152]{1,0:T(8,128)(2,1)} %get-tuple-element.47.refs_3_) | copy-start | bytes 1769476
  57.5 3.4 %copy-start.8 = (bf16[256,896]{1,0:T(8,128)(2,1)S(1)}, bf16[256,896]{1,0:T(8,128)(2,1)}, u32[]{:S(2)}) copy-start(bf16[256,896]{1,0:T(8,128)(2,1)} %copy-done.7) | copy-start | bytes 1376260
  57.5 3.4 %copy-start.10 = (bf16[256,896]{1,0:T(8,128)(2,1)S(1)}, bf16[256,896]{1,0:T(8,128)(2,1)}, u32[]{:S(2)}) copy-start(bf16[256,896]{1,0:T(8,128)(2,1)} %get-tuple-element.48.refs_6_) | copy-start | bytes 1376260
  57.5 3.4 %copy-start.12 = (bf16[256,896]{1,0:T(8,128)(2,1)S(1)}, bf16[256,896]{1,0:T(8,128)(2,1)}, u32[]{:S(2)}) copy-start(bf16[256,896]{1,0:T(8,128)(2,1)} %get-tuple-element.46.refs_2_) | copy-start | bytes 1376260
  66.1 1.8 %copy-start.17 = (bf16[32,384]{1,0:T(8,128)(2,1)S(1)}, bf16[32,384]{1,0:T(8,128)(2,1)}, u32[]{:S(2)}) copy-start(bf16[32,384]{1,0:T(8,128)(2,1)} %refs_3_.1) | copy-start | bytes 73732
  68.0 2.9 %copy-start.14 = (bf16[256,1152]{1,0:T(8,128)(2,1)S(1)}, bf16[256,1152]{1,0:T(8,128)(2,1)}, u32[]{:S(2)}) copy-start(bf16[256,1152]{1,0:T(8,128)(2,1)} %get-tuple-element.54.refs_1_) | copy-start | bytes 1769476
  68.0 2.9 %copy-start.16 = (bf16[256,896]{1,0:T(8,128)(2,1)S(1)}, bf16[256,896]{1,0:T(8,128)(2,1)}, u32[]{:S(2)}) copy-start(bf16[256,896]{1,0:T(8,128)(2,1)} %get-tuple-element.56.refs_2_) | copy-start | bytes 1376260
  69.5 1.3 %collective-permute-start.20 = (f32[2,32,256]{2,1,0:T(8,128)S(1)}, f32[2,32,256]{2,1,0:T(8,128)S(1)}, u32[]{:S(2)}, u32[]{:S(2)}) collective-permute-start(f32[2,32,256]{2,1,0:T(8,128)S(1)} %shards.4), channel_id=1, source_target_pairs={{0,1},{1,0},{2,3},{3,2},{4,5},{5,4},{6,7},{7,6},{8,9},{9,8},{10,11... | collective-permute-start | bytes 196616 | tf_op jit(solution)/shard_map/ppermute | solution.py:362
  70.9 5.3 %copy-start.18 = (f32[8,128]{1,0:T(8,128)S(1)}, f32[8,128]{1,0:T(8,128)}, u32[]{:S(2)}) copy-start(f32[8,128]{1,0:T(8,128)} %get-tuple-element.53.refs_0_) | copy-start | bytes 12292
  76.2 4.8 %collective-permute-start.22 = (bf16[256,1152]{1,0:T(8,128)(2,1)S(1)}, bf16[256,1152]{1,0:T(8,128)(2,1)S(1)}, u32[]{:S(2)}, u32[]{:S(2)}) collective-permute-start(bf16[256,1152]{1,0:T(8,128)(2,1)S(1)} %get-tuple-element.57.mine), channel_id=1, source_target_pairs={{0,1},{1,0},{2,3},{3,2},{4,5},{5,4},{6,7},{7,6},{8,9},{9,8},{10,11... | collective-permute-start | bytes 1769480 | tf_op jit(solution)/shard_map/ppermute | solution.py:371
  76.2 2.7 %collective-permute-start.23 = (bf16[256,896]{1,0:T(8,128)(2,1)}, bf16[256,896]{1,0:T(8,128)(2,1)S(1)}, u32[]{:S(2)}, u32[]{:S(2)}) collective-permute-start(bf16[256,896]{1,0:T(8,128)(2,1)} %get-tuple-element.58.mine), channel_id=1, source_target_pairs={{0,1},{1,0},{2,3},{3,2},{4,5},{5,4},{6,7},{7,6},{8,9},{9,8},{10,11... | collective-permute-start | bytes 1376264 | tf_op jit(solution)/shard_map/ppermute | solution.py:371
  76.7 2.2 %collective-permute-start.27 = (f32[1,32,256]{2,1,0:T(8,128)S(1)}, f32[1,32,256]{2,1,0:T(8,128)S(1)}, u32[]{:S(2)}, u32[]{:S(2)}) collective-permute-start(f32[1,32,256]{2,1,0:T(8,128)S(1)} %shards.5), channel_id=1, source_target_pairs={{0,1},{1,0},{2,3},{3,2},{4,5},{5,4},{6,7},{7,6},{8,9},{9,8},{10,11... | collective-permute-start | bytes 98312 | tf_op jit(solution)/shard_map/ppermute | solution.py:362
  76.7 8.3 %collective-permute-start.26 = (f32[32,256]{1,0:T(8,128)S(1)}, f32[32,256]{1,0:T(8,128)S(1)}, u32[]{:S(2)}, u32[]{:S(2)}) collective-permute-start(f32[32,256]{1,0:T(8,128)S(1)} %get-tuple-element.61), channel_id=1, source_target_pairs={{0,12},{4,0},{8,4},{12,8},{1,13},{5,1},{9,5},{13,9},{2,14},{6,2},{... | collective-permute-start | bytes 98312 | tf_op jit(solution)/shard_map/ppermute | solution.py:365
  78.9 6.1 %collective-permute-start.28 = (f32[32,256]{1,0:T(8,128)S(1)}, f32[32,256]{1,0:T(8,128)S(1)}, u32[]{:S(2)}, u32[]{:S(2)}) collective-permute-start(f32[32,256]{1,0:T(8,128)S(1)} %add_bitcast_fusion), channel_id=1, source_target_pairs={{0,8},{4,12},{8,0},{12,4},{1,9},{5,13},{9,1},{13,5},{2,10},{6,14},... | collective-permute-start | bytes 98312 | tf_op jit(solution)/shard_map/ppermute | solution.py:365
  80.9 4.1 %copy-start.19 = (s32[256,2]{0,1:T(2,128)S(1)}, s32[256,2]{0,1:T(2,128)}, u32[]{:S(2)}) copy-start(s32[256,2]{0,1:T(2,128)} %param.10) | copy-start | bytes 6148
  80.9 4.1 %copy-start.20 = (s32[1,256]{1,0:T(1,128)S(1)}, s32[1,256]{1,0:T(1,128)}, u32[]{:S(2)}) copy-start(s32[1,256]{1,0:T(1,128)} %docs.3) | copy-start | bytes 3076
  82.3 5.7 %collective-permute-start.24 = (f32[32,256]{1,0:T(8,128)S(1)}, f32[32,256]{1,0:T(8,128)S(1)}, u32[]{:S(2)}, u32[]{:S(2)}) collective-permute-start(f32[32,256]{1,0:T(8,128)S(1)} %part.3), channel_id=1, source_target_pairs={{0,4},{1,5},{4,8},{5,9},{8,12},{9,13},{12,0},{13,1},{2,6},{3,7},{6... | collective-permute-start | bytes 98312 | tf_op jit(solution)/shard_map/ppermute | solution.py:388
  84.2 5.3 %collective-permute-start.25 = (f32[32,256]{1,0:T(8,128)S(1)}, f32[32,256]{1,0:T(8,128)S(1)}, u32[]{:S(2)}, u32[]{:S(2)}) collective-permute-start(f32[32,256]{1,0:T(8,128)S(1)} %part.3), channel_id=1, source_target_pairs={{0,5},{1,4},{4,9},{5,8},{8,13},{9,12},{12,1},{13,0},{2,7},{3,6},{6... | collective-permute-start | bytes 98312 | tf_op jit(solution)/shard_map/ppermute | solution.py:389
  (8 other events, 6.9 us)

commit v6 on v5

--- a/solution.py
+++ b/solution.py
@@ -183,8 +183,7 @@
 def grads_kernel(steps, experts, where, grad_mine, grad_other, docs, routes, *refs):
     refs = list(refs)
     codes_of_step = [refs.pop(0) for _ in steps]
-    cross = refs.pop(0) if experts - 1 in steps else None
-    before = refs.pop(0) if cross is not None else None
+    before = refs.pop(0) if experts - 1 in steps else None
     out, by_expert = refs
     rank = grad_mine.shape[0]
     group = LANES // rank
@@ -202,7 +201,7 @@
     )
     here = [lax.rem(home + k, experts) for k in steps]
     for expert, codes in zip(here, codes_of_step):
-        by_expert[expert] = codes[...] if cross is None else codes[...] + cross[...]
+        by_expert[expert] = codes[...]
     if before is not None:
         out[...] = before[...]
     else:
@@ -377,16 +376,8 @@
             (rank, tokens.shape[0]) if last else (tokens.shape[0], 2 * gate.shape[1]),
             "part",
         )
-    home_pairs = [
-        [
-            (z * 2 + c, (z + 1) % experts * 2 + (c ^ flip))
-            for z in range(experts)
-            for c in range(2)
-        ]
-        for flip in range(2)
-    ]
-    codes.append(lax.ppermute(total, ("exp", "mdl"), home_pairs[0]))
-    cross = lax.ppermute(total, ("exp", "mdl"), home_pairs[1])
+    total = total + lax.ppermute(total, "mdl", swap)
+    codes.append(lax.ppermute(total, "exp", ring))
 
     def grads(steps, more):
         vmem = pl.BlockSpec(memory_space=pltpu.VMEM)
@@ -403,7 +394,7 @@
         )(home.reshape(1), *args)
 
     first = grads(range(experts - 1), ())
-    return grads(range(experts - 1, experts), (cross, first))
+    return grads(range(experts - 1, experts), (first,))
 
 
 def solution(mesh):

time: 90.7 us -> 90.6 us (level)
    ppermute x2, waiting for transfers between devices: 0.01 us -> 2.19 us  [on_device(): lax.ppermute(found[k - low], 'exp', back)]
    ppermute x2, waiting for transfers between devices: 3.71 us -> 1.56 us  [the longest x1 1.17 us: on_device(): codes.append(lax.ppermute(total, 'exp', ring))]
  transfers between devices with their start and end apart: 29 -> 29, of which waited for: 15 -> 16; matrix products, arithmetic and copies ran while one was open for 8% -> 8% of each run, Pallas kernels for 20% -> 20%
where the time goes in v6:
time: 90.6 us; the launch traced here: 90.3 us
  waiting for transfers between devices  35.5 us (39%)
  starting transfers between devices  23.9 us (26%)
  Pallas kernels  19.2 us (21%)
  other arithmetic  6.13 us (7%)
  local copies, waits for them, and re-layouts  4.65 us (5%)
    ppermute x6, waiting for transfers between devices, on_device(): moved = [lax.ppermute(x, 'exp', ring) for x in mine[-1]]  15.2 us
    ppermute x4, waiting for transfers between devices, along_dat(): lax.ppermute(x, 'dat', [((z + k) % dats, z) for z in range(dats)])  12.7 us
    pallas_call x5, Pallas kernels, vmem_call(): pl.pallas_call(kernel, in_specs=[hbm] * far + [vmem] * (len(args) - far),...  12.4 us
    ppermute x6, starting transfers between devices, on_device(): moved = [lax.ppermute(x, 'exp', ring) for x in mine[-1]]  6.47 us
    ppermute x4, starting transfers between devices, over_grp(): return [lax.ppermute(x, 'grp', swap) for x in xs]  6.05 us
    select_n x3, other arithmetic, on_device(): jnp.where(grp == 0, gate[low:high], up[low:high])  6.03 us
    ppermute x4, starting transfers between devices, along_dat(): lax.ppermute(x, 'dat', [((z + k) % dats, z) for z in range(dats)])  5.96 us
    pallas_call x2, Pallas kernels, join(): pl.pallas_call(functools.partial(join_kernel, dats, edges), in_specs=[pl....  5.17 us
  transfers between devices with their start and end apart: 29, of which 16 were waited for; matrix products, arithmetic and copies ran while one was open for 8% of the time, Pallas kernels for 20%

profile of v6, /device:TPU:0, one launch (start us, length us, event | category | flops | bytes accessed | tf_op | source)
XLA Modules:
  0.0 90.3 jit_solution(5077240978502757047)
XLA Ops:
  0.0 1.2 %slice.47.refs_0_ = bf16[256,896]{1,0:T(8,128)(2,1)S(1)} slice(bf16[256,2048]{1,0:T(8,128)(2,1)} %param.8), slice={[0:256], [0:896]} | slice | bytes 917504 | tf_op jit(solution)/shard_map/slice | solution.py:259
  1.2 3.1 %collective-permute-start.1 = (bf16[256,896]{1,0:T(8,128)(2,1)S(1)}, bf16[256,896]{1,0:T(8,128)(2,1)}, u32[]{:S(2)}, u32[]{:S(2)}) collective-permute-start(bf16[256,896]{1,0:T(8,128)(2,1)S(1)} %slice.47.refs_0_), channel_id=1, source_target_pairs={{0,4},{4,8},{8,12},{12,0},{1,5},{5,9},{9,13},{13,1},{2,6},{6,10},{... | collective-permute-start | bytes 1376264 | tf_op jit(solution)/shard_map/ppermute | solution.py:320
  4.3 2.3 %select_bitcast_fusion = (bf16[576,384]{1,0:T(8,128)(2,1)}, bf16[576,384]{1,0:T(8,128)(2,1)S(1)}) fusion(bf16[1,2048,384]{2,1,0:T(8,128)(2,1)} %param.13, bf16[1,2048,384]{2,1,0:T(8,128)(2,1)} %param.12, pred[]{:T(512)S(6)} %eq.2), kind=kLoop, calls=%fused_computation | loop fusion | flops 442368 | bytes 2654209 | tf_op jit(solution)/shard_map/jit(_where)/select_n | solution.py:270
  6.6 1.5 %collective-permute-start.2 = (bf16[576,384]{1,0:T(8,128)(2,1)S(1)}, bf16[576,384]{1,0:T(8,128)(2,1)S(1)}, u32[]{:S(2)}, u32[]{:S(2)}) collective-permute-start(bf16[576,384]{1,0:T(8,128)(2,1)S(1)} %get-tuple-element.60), channel_id=1, source_target_pairs={{2,0},{0,2},{3,1},{1,3},{6,4},{4,6},{7,5},{5,7},{10,8},{8,10},{11,... | collective-permute-start | bytes 1327112 | tf_op jit(solution)/shard_map/ppermute | solution.py:277
  8.2 1.6 %collective-permute-start.3 = (bf16[256,1152]{1,0:T(8,128)(2,1)S(1)}, bf16[256,1152]{1,0:T(8,128)(2,1)S(1)}, u32[]{:S(2)}, u32[]{:S(2)}) collective-permute-start(bf16[256,1152]{1,0:T(8,128)(2,1)S(1)} %slice.52.refs_1_), channel_id=1, source_target_pairs={{0,4},{4,8},{8,12},{12,0},{1,5},{5,9},{9,13},{13,1},{2,6},{6,10},{... | collective-permute-start | bytes 1769480 | tf_op jit(solution)/shard_map/ppermute | solution.py:320
  10.0 8.2 %collective-permute-done.2.refs_2_ = bf16[576,384]{1,0:T(8,128)(2,1)S(1)} collective-permute-done((bf16[576,384]{1,0:T(8,128)(2,1)S(1)}, bf16[576,384]{1,0:T(8,128)(2,1)S(1)}, u32[]{:S(2)}, u32[]{:S(2)}) %collective-permute-start.2) | collective-permute-done | bytes 442400 | tf_op jit(solution)/shard_map/ppermute | solution.py:277
  18.2 0.6 broadcast_in_dim.3.refs_0_
  19.0 1.5 %collective-permute-start.7 = (bf16[576,384]{1,0:T(8,128)(2,1)}, bf16[576,384]{1,0:T(8,128)(2,1)}, u32[]{:S(2)}, u32[]{:S(2)}) collective-permute-start(bf16[576,384]{1,0:T(8,128)(2,1)} %get-tuple-element.34.refs_0_), channel_id=1, source_target_pairs={{0,16},{16,0},{1,17},{17,1},{2,18},{18,2},{3,19},{19,3},{4,20},{20... | collective-permute-start | bytes 1327112 | tf_op jit(solution)/shard_map/ppermute | solution.py:283
  20.5 1.5 %collective-permute-start.6 = (bf16[576,384]{1,0:T(8,128)(2,1)}, bf16[576,384]{1,0:T(8,128)(2,1)}, u32[]{:S(2)}, u32[]{:S(2)}) collective-permute-start(bf16[576,384]{1,0:T(8,128)(2,1)} %get-tuple-element.33), channel_id=1, source_target_pairs={{2,0},{0,2},{3,1},{1,3},{6,4},{4,6},{7,5},{5,7},{10,8},{8,10},{11,... | collective-permute-start | bytes 1327112 | tf_op jit(solution)/shard_map/ppermute | solution.py:277
  22.0 0.8 copy-done.11
  22.8 1.6 %collective-permute-start.8 = (bf16[256,896]{1,0:T(8,128)(2,1)}, bf16[256,896]{1,0:T(8,128)(2,1)}, u32[]{:S(2)}, u32[]{:S(2)}) collective-permute-start(bf16[256,896]{1,0:T(8,128)(2,1)} %get-tuple-element.36.refs_4_), channel_id=1, source_target_pairs={{0,4},{4,8},{8,12},{12,0},{1,5},{5,9},{9,13},{13,1},{2,6},{6,10},{... | collective-permute-start | bytes 1376264 | tf_op jit(solution)/shard_map/ppermute | solution.py:320
  24.4 1.9 %select_bitcast_fusion.2.refs_6_ = bf16[512,384]{1,0:T(8,128)(2,1)} fusion(bf16[1,2048,384]{2,1,0:T(8,128)(2,1)} %param.13, bf16[1,2048,384]{2,1,0:T(8,128)(2,1)} %param.12, pred[]{:T(512)S(6)} %eq.2), kind=kLoop, calls=%fused_computation.2 | loop fusion | flops 196608 | bytes 1179649 | tf_op jit(solution)/shard_map/jit(_where)/select_n | solution.py:270
  26.3 4.0 %collective-permute-done.3.refs_1_ = bf16[256,1152]{1,0:T(8,128)(2,1)S(1)} collective-permute-done((bf16[256,1152]{1,0:T(8,128)(2,1)S(1)}, bf16[256,1152]{1,0:T(8,128)(2,1)S(1)}, u32[]{:S(2)}, u32[]{:S(2)}) %collective-permute-start.3) | collective-permute-done | bytes 589856 | tf_op jit(solution)/shard_map/ppermute | solution.py:320
  30.3 1.0 %collective-permute-done.6.refs_4_ = bf16[576,384]{1,0:T(8,128)(2,1)} collective-permute-done((bf16[576,384]{1,0:T(8,128)(2,1)}, bf16[576,384]{1,0:T(8,128)(2,1)}, u32[]{:S(2)}, u32[]{:S(2)}) %collective-permute-start.6) | collective-permute-done | bytes 442400 | tf_op jit(solution)/shard_map/ppermute | solution.py:277
  31.4 1.8 %collective-permute-start.11 = (bf16[576,384]{1,0:T(8,128)(2,1)}, bf16[576,384]{1,0:T(8,128)(2,1)S(1)}, u32[]{:S(2)}, u32[]{:S(2)}) collective-permute-start(bf16[576,384]{1,0:T(8,128)(2,1)} %get-tuple-element.38.refs_1_), channel_id=1, source_target_pairs={{0,16},{16,0},{1,17},{17,1},{2,18},{18,2},{3,19},{19,3},{4,20},{20... | collective-permute-start | bytes 1327112 | tf_op jit(solution)/shard_map/ppermute | solution.py:283
  33.2 1.5 %collective-permute-start.10 = (bf16[512,384]{1,0:T(8,128)(2,1)}, bf16[512,384]{1,0:T(8,128)(2,1)S(1)}, u32[]{:S(2)}, u32[]{:S(2)}) collective-permute-start(bf16[512,384]{1,0:T(8,128)(2,1)} %get-tuple-element.37), channel_id=1, source_target_pairs={{2,0},{0,2},{3,1},{1,3},{6,4},{4,6},{7,5},{5,7},{10,8},{8,10},{11,... | collective-permute-start | bytes 1179656 | tf_op jit(solution)/shard_map/ppermute | solution.py:277
  34.6 0.4 fusion.grad_mine
  35.1 1.2 %collective-permute-done.refs_6_.grad_other = f32[32,256]{1,0:T(8,128)S(1)} collective-permute-done((f32[32,256]{1,0:T(8,128)S(1)}, f32[32,256]{1,0:T(8,128)S(1)}, u32[]{:S(2)}, u32[]{:S(2)}) %collective-permute-start) | collective-permute-done | bytes 32800 | tf_op jit(solution)/shard_map/ppermute | solution.py:252
  36.5 2.9 %collective-permute-done.8.refs_1_ = bf16[256,896]{1,0:T(8,128)(2,1)} collective-permute-done((bf16[256,896]{1,0:T(8,128)(2,1)}, bf16[256,896]{1,0:T(8,128)(2,1)}, u32[]{:S(2)}, u32[]{:S(2)}) %collective-permute-start.8) | collective-permute-done | bytes 458784 | tf_op jit(solution)/shard_map/ppermute | solution.py:320
  39.4 1.8 %select_bitcast_fusion.3.refs_5_ = bf16[384,384]{1,0:T(8,128)(2,1)} fusion(bf16[1,2048,384]{2,1,0:T(8,128)(2,1)} %param.13, bf16[1,2048,384]{2,1,0:T(8,128)(2,1)} %param.12, pred[]{:T(512)S(6)} %eq.2), kind=kLoop, calls=%fused_computation.3 | loop fusion | flops 147456 | bytes 884737 | tf_op jit(solution)/shard_map/jit(_where)/select_n | solution.py:270
  41.3 3.1 %collective-permute-done.10.refs_3_ = bf16[512,384]{1,0:T(8,128)(2,1)S(1)} collective-permute-done((bf16[512,384]{1,0:T(8,128)(2,1)}, bf16[512,384]{1,0:T(8,128)(2,1)S(1)}, u32[]{:S(2)}, u32[]{:S(2)}) %collective-permute-start.10) | collective-permute-done | bytes 393248 | tf_op jit(solution)/shard_map/ppermute | solution.py:277
  44.4 0.8 copy-done.23
  45.3 1.2 %collective-permute-start.15 = (bf16[512,384]{1,0:T(8,128)(2,1)}, bf16[512,384]{1,0:T(8,128)(2,1)}, u32[]{:S(2)}, u32[]{:S(2)}) collective-permute-start(bf16[512,384]{1,0:T(8,128)(2,1)} %get-tuple-element.42.refs_2_), channel_id=1, source_target_pairs={{0,16},{16,0},{1,17},{17,1},{2,18},{18,2},{3,19},{19,3},{4,20},{20... | collective-permute-start | bytes 1179656 | tf_op jit(solution)/shard_map/ppermute | solution.py:283
  46.5 1.5 %collective-permute-start.14 = (bf16[384,384]{1,0:T(8,128)(2,1)}, bf16[384,384]{1,0:T(8,128)(2,1)}, u32[]{:S(2)}, u32[]{:S(2)}) collective-permute-start(bf16[384,384]{1,0:T(8,128)(2,1)} %get-tuple-element.41), channel_id=1, source_target_pairs={{2,0},{0,2},{3,1},{1,3},{6,4},{4,6},{7,5},{5,7},{10,8},{8,10},{11,... | collective-permute-start | bytes 884744 | tf_op jit(solution)/shard_map/ppermute | solution.py:277
  48.0 6.5 %collective-permute-done.12.refs_1_ = bf16[256,1152]{1,0:T(8,128)(2,1)S(1)} collective-permute-done((bf16[256,1152]{1,0:T(8,128)(2,1)}, bf16[256,1152]{1,0:T(8,128)(2,1)S(1)}, u32[]{:S(2)}, u32[]{:S(2)}) %collective-permute-start.12) | collective-permute-done | bytes 589856 | tf_op jit(solution)/shard_map/ppermute | solution.py:320
  54.5 0.4 collective-permute-done.14.refs_3_
  54.9 0.9 collective-permute-done.15.refs_4_
  55.9 1.6 %collective-permute-start.18 = (bf16[384,384]{1,0:T(8,128)(2,1)}, bf16[384,384]{1,0:T(8,128)(2,1)S(1)}, u32[]{:S(2)}, u32[]{:S(2)}) collective-permute-start(bf16[384,384]{1,0:T(8,128)(2,1)} %get-tuple-element.45.refs_0_), channel_id=1, source_target_pairs={{0,16},{16,0},{1,17},{17,1},{2,18},{18,2},{3,19},{19,3},{4,20},{20... | collective-permute-start | bytes 884744 | tf_op jit(solution)/shard_map/ppermute | solution.py:283
  57.5 3.4 %join.2.refs_8_.refs_4_.refs_0_ = bf16[2,1664,768]{2,1,0:T(8,128)(2,1)S(1)} custom-call(s32[3]{0:T(128)S(1)} %pad_add_fusion.where, bf16[2048,384]{1,0:T(8,128)(2,1)} %bitcast.34, bf16[2048,384]{1,0:T(8,128)(2,1)} %bitcast.32, bf16[576,384]{1,0:T(8,128)(2,1)} %get-tuple-element.34.refs_0_, bf16[576,384]{1,0:T(8,128)(2,1)} %get-tuple-element.38.refs_1_, ...), custom_call_target="tpu_custom_call" | custom-call | flops 1 | bytes 1 | tf_op jit(solution)/shard_map/join/pallas_call | solution.py:74
  61.0 4.1 %shards.3.refs_9_ = f32[2,256,768]{2,1,0:T(8,128)S(1)} custom-call(bf16[256,896]{1,0:T(8,128)(2,1)S(1)} %copy-done.8, bf16[256,1152]{1,0:T(8,128)(2,1)S(1)} %slice.52.refs_1_, bf16[256,896]{1,0:T(8,128)(2,1)S(1)} %copy-done.12, bf16[256,1152]{1,0:T(8,128)(2,1)S(1)} %copy-done.6, bf16[256,896]{1,0:T(8,128)(2,1)} %get-tuple-element.36.refs_4_, ...), custom_call_target="tpu_custom_call" | custom-call | flops 1 | bytes 1 | tf_op jit(solution)/shard_map/shards/pallas_call | solution.py:171
  65.1 0.3 collective-permute-done.18.refs_3_
  65.4 0.5 copy-done.15
  66.1 1.8 %join.3.refs_8_.refs_5_.refs_1_ = bf16[2,384,768]{2,1,0:T(8,128)(2,1)S(1)} custom-call(s32[3]{0:T(128)S(1)} %pad_add_fusion.where, bf16[2048,384]{1,0:T(8,128)(2,1)} %bitcast.35, bf16[2048,384]{1,0:T(8,128)(2,1)} %bitcast.33, bf16[384,384]{1,0:T(8,128)(2,1)} %get-tuple-element.45.refs_0_, bf16[384,384]{1,0:T(8,128)(2,1)} %get-tuple-element.55.refs_1_), custom_call_target="tpu_custom_call" | custom-call | flops 1 | bytes 1 | tf_op jit(solution)/shard_map/join/pallas_call | solution.py:74
  68.0 1.5 %shards.4 = f32[2,32,256]{2,1,0:T(8,128)S(1)} custom-call(bf16[256,896]{1,0:T(8,128)(2,1)S(1)} %copy-done.8, bf16[256,1152]{1,0:T(8,128)(2,1)S(1)} %slice.52.refs_1_, bf16[256,896]{1,0:T(8,128)(2,1)S(1)} %copy-done.12, bf16[256,1152]{1,0:T(8,128)(2,1)S(1)} %copy-done.6, bf16[256,896]{1,0:T(8,128)(2,1)} %get-tuple-element.36.refs_4_, ...), custom_call_target="tpu_custom_call" | custom-call | flops 1 | bytes 1 | tf_op jit(solution)/shard_map/shards/pallas_call | solution.py:171
  69.6 1.2 %collective-permute-done.20 = f32[2,32,256]{2,1,0:T(8,128)S(1)} collective-permute-done((f32[2,32,256]{2,1,0:T(8,128)S(1)}, f32[2,32,256]{2,1,0:T(8,128)S(1)}, u32[]{:S(2)}, u32[]{:S(2)}) %collective-permute-start.20) | collective-permute-done | bytes 65568 | tf_op jit(solution)/shard_map/ppermute | solution.py:361
  70.9 3.5 %shards.5 = f32[1,32,256]{2,1,0:T(8,128)S(1)} custom-call(bf16[256,896]{1,0:T(8,128)(2,1)} %get-tuple-element.44.refs_0_, bf16[256,1152]{1,0:T(8,128)(2,1)S(1)} %copy-done.14, bf16[256,896]{1,0:T(8,128)(2,1)S(1)} %copy-done.16, bf16[256,1152]{1,0:T(8,128)(2,1)S(1)} %collective-permute-done.21.refs_3_, bf16[2,1664,768]{2,1,0:T(8,128)(2,1)S(1)} %join.2.refs_8_.refs_4_.refs_0_, ...), custom_call_target="tpu_custom_call" | custom-call | flops 1 | bytes 1 | tf_op jit(solution)/shard_map/shards/pallas_call | solution.py:171
  74.4 1.8 %collective-permute-done.19.refs_1_ = bf16[256,1152]{1,0:T(8,128)(2,1)S(1)} collective-permute-done((bf16[256,1152]{1,0:T(8,128)(2,1)}, bf16[256,1152]{1,0:T(8,128)(2,1)S(1)}, u32[]{:S(2)}, u32[]{:S(2)}) %collective-permute-start.19) | collective-permute-done | bytes 589856 | tf_op jit(solution)/shard_map/ppermute | solution.py:320
  76.2 0.5 collective-permute-start.23
  76.7 2.0 %collective-permute-start.26 = (f32[32,256]{1,0:T(8,128)S(1)}, f32[32,256]{1,0:T(8,128)S(1)}, u32[]{:S(2)}, u32[]{:S(2)}) collective-permute-start(f32[32,256]{1,0:T(8,128)S(1)} %get-tuple-element.61), channel_id=1, source_target_pairs={{0,12},{4,0},{8,4},{12,8},{1,13},{5,1},{9,5},{13,9},{2,14},{6,2},{... | collective-permute-start | bytes 98312 | tf_op jit(solution)/shard_map/ppermute | solution.py:364
  78.9 2.0 %part.2.refs_2_ = f32[256,768]{1,0:T(8,128)S(1)} custom-call(bf16[256,896]{1,0:T(8,128)(2,1)} %get-tuple-element.58.mine, bf16[256,896]{1,0:T(8,128)(2,1)S(1)} %collective-permute-done.23.other, bf16[2,1664,768]{2,1,0:T(8,128)(2,1)S(1)} %join.2.refs_8_.refs_4_.refs_0_, bf16[2,384,768]{2,1,0:T(8,128)(2,1)S(1)} %join.3.refs_8_.refs_5_.refs_1_), custom_call_target="tpu_custom_call" | custom-call | flops 1 | bytes 1 | tf_op jit(solution)/shard_map/part/pallas_call | solution.py:171
  81.0 1.4 %part.3 = f32[32,256]{1,0:T(8,128)S(1)} custom-call(bf16[256,1152]{1,0:T(8,128)(2,1)S(1)} %get-tuple-element.57.mine, bf16[256,1152]{1,0:T(8,128)(2,1)S(1)} %collective-permute-done.22.other, bf16[2,1664,768]{2,1,0:T(8,128)(2,1)S(1)} %join.2.refs_8_.refs_4_.refs_0_, bf16[2,384,768]{2,1,0:T(8,128)(2,1)S(1)} %join.3.refs_8_.refs_5_.refs_1_, ...), custom_call_target="tpu_custom_call" | custom-call | flops 1 | bytes 1 | tf_op jit(solution)/shard_map/part/pallas_call | solution.py:171
  82.6 0.6 collective-permute-start.28
  83.2 0.4 collective-permute-done.24
  83.6 1.7 %collective-permute-start.25 = (f32[32,256]{1,0:T(8,128)S(1)}, f32[32,256]{1,0:T(8,128)S(1)}, u32[]{:S(2)}, u32[]{:S(2)}) collective-permute-start(f32[32,256]{1,0:T(8,128)S(1)} %add.10), channel_id=1, source_target_pairs={{0,4},{4,8},{8,12},{12,0},{1,5},{5,9},{9,13},{13,1},{2,6},{6,10},{... | collective-permute-start | bytes 98312 | tf_op jit(solution)/shard_map/ppermute | solution.py:380
  85.3 2.2 %collective-permute-done.28.refs_2_ = f32[32,256]{1,0:T(8,128)S(1)} collective-permute-done((f32[32,256]{1,0:T(8,128)S(1)}, f32[32,256]{1,0:T(8,128)S(1)}, u32[]{:S(2)}, u32[]{:S(2)}) %collective-permute-start.28) | collective-permute-done | bytes 32800 | tf_op jit(solution)/shard_map/ppermute | solution.py:364
  87.5 0.6 doc_grads.2.refs_1_
  88.1 1.2 %collective-permute-done.25.refs_0_ = f32[32,256]{1,0:T(8,128)S(1)} collective-permute-done((f32[32,256]{1,0:T(8,128)S(1)}, f32[32,256]{1,0:T(8,128)S(1)}, u32[]{:S(2)}, u32[]{:S(2)}) %collective-permute-start.25) | collective-permute-done | bytes 32800 | tf_op jit(solution)/shard_map/ppermute | solution.py:380
  89.3 1.0 %doc_grads.3 = f32[4,4,1024]{2,1,0:T(4,128)} custom-call(s32[1]{0:T(128)} %bitcast.where, f32[32,256]{1,0:T(8,128)S(1)} %fusion.grad_mine, f32[32,256]{1,0:T(8,128)S(1)} %collective-permute-done.refs_6_.grad_other, s32[1,256]{1,0:T(1,128)S(1)} %copy-done.20, s32[2,256]{1,0:T(2,128)S(1)} %bitcast.31, f32[32,256]{1,0:T(8,128)S(1)} %collective-permute-done.25.refs_0_, ...), custom_call_target="tpu_custom_call" | custom-call | flops 1 | bytes 1 | tf_op jit(solution)/shard_map/doc_grads/pallas_call | solution.py:385
  (93 shorter events, 2.0 us)
Async XLA Ops:
  0.0 34.6 %copy-start = (bf16[256,2048]{1,0:T(8,128)(2,1)S(1)}, bf16[256,2048]{1,0:T(8,128)(2,1)}, u32[]{:S(2)}) copy-start(bf16[256,2048]{1,0:T(8,128)(2,1)} %param.9) | copy-start | bytes 3145732
  0.0 8.1 %copy-start.25 = (bf16[256,2048]{1,0:T(8,128)(2,1)S(1)}, bf16[256,2048]{1,0:T(8,128)(2,1)}, u32[]{:S(2)}) copy-start(bf16[256,2048]{1,0:T(8,128)(2,1)} %param.8) | copy-start | bytes 3145732
  1.2 6.9 %copy-start.7 = (bf16[256,896]{1,0:T(8,128)(2,1)}, bf16[256,896]{1,0:T(8,128)(2,1)S(1)}, u32[]{:S(2)}) copy-start(bf16[256,896]{1,0:T(8,128)(2,1)S(1)} %slice.47.refs_0_) | copy-start | bytes 1376260
  1.2 17.0 %collective-permute-start.1 = (bf16[256,896]{1,0:T(8,128)(2,1)S(1)}, bf16[256,896]{1,0:T(8,128)(2,1)}, u32[]{:S(2)}, u32[]{:S(2)}) collective-permute-start(bf16[256,896]{1,0:T(8,128)(2,1)S(1)} %slice.47.refs_0_), channel_id=1, source_target_pairs={{0,4},{4,8},{8,12},{12,0},{1,5},{5,9},{9,13},{13,1},{2,6},{6,10},{... | collective-permute-start | bytes 1376264 | tf_op jit(solution)/shard_map/ppermute | solution.py:320
  6.6 19.7 %copy-start.26 = (bf16[32,2048]{1,0:T(8,128)(2,1)S(1)}, bf16[32,2048]{1,0:T(8,128)(2,1)}, u32[]{:S(2)}) copy-start(bf16[32,2048]{1,0:T(8,128)(2,1)} %param.15) | copy-start | bytes 393220
  6.6 11.6 %collective-permute-start.2 = (bf16[576,384]{1,0:T(8,128)(2,1)S(1)}, bf16[576,384]{1,0:T(8,128)(2,1)S(1)}, u32[]{:S(2)}, u32[]{:S(2)}) collective-permute-start(bf16[576,384]{1,0:T(8,128)(2,1)S(1)} %get-tuple-element.60), channel_id=1, source_target_pairs={{2,0},{0,2},{3,1},{1,3},{6,4},{4,6},{7,5},{5,7},{10,8},{8,10},{11,... | collective-permute-start | bytes 1327112 | tf_op jit(solution)/shard_map/ppermute | solution.py:277
  8.1 13.9 %collective-permute-start.4 = (bf16[256,896]{1,0:T(8,128)(2,1)S(1)}, bf16[256,896]{1,0:T(8,128)(2,1)S(1)}, u32[]{:S(2)}, u32[]{:S(2)}) collective-permute-start(bf16[256,896]{1,0:T(8,128)(2,1)S(1)} %slice.47.refs_0_), channel_id=1, source_target_pairs={{0,1},{1,0},{2,3},{3,2},{4,5},{5,4},{6,7},{7,6},{8,9},{9,8},{10,11... | collective-permute-start | bytes 1376264 | tf_op jit(solution)/shard_map/ppermute | solution.py:260
  8.2 22.2 %collective-permute-start.3 = (bf16[256,1152]{1,0:T(8,128)(2,1)S(1)}, bf16[256,1152]{1,0:T(8,128)(2,1)S(1)}, u32[]{:S(2)}, u32[]{:S(2)}) collective-permute-start(bf16[256,1152]{1,0:T(8,128)(2,1)S(1)} %slice.52.refs_1_), channel_id=1, source_target_pairs={{0,4},{4,8},{8,12},{12,0},{1,5},{5,9},{9,13},{13,1},{2,6},{6,10},{... | collective-permute-start | bytes 1769480 | tf_op jit(solution)/shard_map/ppermute | solution.py:320
  9.8 20.5 %collective-permute-start.5 = (bf16[256,1152]{1,0:T(8,128)(2,1)S(1)}, bf16[256,1152]{1,0:T(8,128)(2,1)S(1)}, u32[]{:S(2)}, u32[]{:S(2)}) collective-permute-start(bf16[256,1152]{1,0:T(8,128)(2,1)S(1)} %slice.52.refs_1_), channel_id=1, source_target_pairs={{0,1},{1,0},{2,3},{3,2},{4,5},{5,4},{6,7},{7,6},{8,9},{9,8},{10,11... | collective-permute-start | bytes 1769480 | tf_op jit(solution)/shard_map/ppermute | solution.py:260
  19.0 11.4 %collective-permute-start.7 = (bf16[576,384]{1,0:T(8,128)(2,1)}, bf16[576,384]{1,0:T(8,128)(2,1)}, u32[]{:S(2)}, u32[]{:S(2)}) collective-permute-start(bf16[576,384]{1,0:T(8,128)(2,1)} %get-tuple-element.34.refs_0_), channel_id=1, source_target_pairs={{0,16},{16,0},{1,17},{17,1},{2,18},{18,2},{3,19},{19,3},{4,20},{20... | collective-permute-start | bytes 1327112 | tf_op jit(solution)/shard_map/ppermute | solution.py:283
  20.5 10.9 %collective-permute-start.6 = (bf16[576,384]{1,0:T(8,128)(2,1)}, bf16[576,384]{1,0:T(8,128)(2,1)}, u32[]{:S(2)}, u32[]{:S(2)}) collective-permute-start(bf16[576,384]{1,0:T(8,128)(2,1)} %get-tuple-element.33), channel_id=1, source_target_pairs={{2,0},{0,2},{3,1},{1,3},{6,4},{4,6},{7,5},{5,7},{10,8},{8,10},{11,... | collective-permute-start | bytes 1327112 | tf_op jit(solution)/shard_map/ppermute | solution.py:277
  22.8 16.6 %collective-permute-start.8 = (bf16[256,896]{1,0:T(8,128)(2,1)}, bf16[256,896]{1,0:T(8,128)(2,1)}, u32[]{:S(2)}, u32[]{:S(2)}) collective-permute-start(bf16[256,896]{1,0:T(8,128)(2,1)} %get-tuple-element.36.refs_4_), channel_id=1, source_target_pairs={{0,4},{4,8},{8,12},{12,0},{1,5},{5,9},{9,13},{13,1},{2,6},{6,10},{... | collective-permute-start | bytes 1376264 | tf_op jit(solution)/shard_map/ppermute | solution.py:320
  30.3 10.9 %collective-permute-start.9 = (bf16[256,896]{1,0:T(8,128)(2,1)}, bf16[256,896]{1,0:T(8,128)(2,1)S(1)}, u32[]{:S(2)}, u32[]{:S(2)}) collective-permute-start(bf16[256,896]{1,0:T(8,128)(2,1)} %get-tuple-element.36.refs_4_), channel_id=1, source_target_pairs={{0,1},{1,0},{2,3},{3,2},{4,5},{5,4},{6,7},{7,6},{8,9},{9,8},{10,11... | collective-permute-start | bytes 1376264 | tf_op jit(solution)/shard_map/ppermute | solution.py:338
  31.4 13.0 %collective-permute-start.11 = (bf16[576,384]{1,0:T(8,128)(2,1)}, bf16[576,384]{1,0:T(8,128)(2,1)S(1)}, u32[]{:S(2)}, u32[]{:S(2)}) collective-permute-start(bf16[576,384]{1,0:T(8,128)(2,1)} %get-tuple-element.38.refs_1_), channel_id=1, source_target_pairs={{0,16},{16,0},{1,17},{17,1},{2,18},{18,2},{3,19},{19,3},{4,20},{20... | collective-permute-start | bytes 1327112 | tf_op jit(solution)/shard_map/ppermute | solution.py:283
  33.2 11.2 %collective-permute-start.10 = (bf16[512,384]{1,0:T(8,128)(2,1)}, bf16[512,384]{1,0:T(8,128)(2,1)S(1)}, u32[]{:S(2)}, u32[]{:S(2)}) collective-permute-start(bf16[512,384]{1,0:T(8,128)(2,1)} %get-tuple-element.37), channel_id=1, source_target_pairs={{2,0},{0,2},{3,1},{1,3},{6,4},{4,6},{7,5},{5,7},{10,8},{8,10},{11,... | collective-permute-start | bytes 1179656 | tf_op jit(solution)/shard_map/ppermute | solution.py:277
  35.1 1.3 %collective-permute-start = (f32[32,256]{1,0:T(8,128)S(1)}, f32[32,256]{1,0:T(8,128)S(1)}, u32[]{:S(2)}, u32[]{:S(2)}) collective-permute-start(f32[32,256]{1,0:T(8,128)S(1)} %fusion.grad_mine), channel_id=1, source_target_pairs={{0,1},{1,0},{2,3},{3,2},{4,5},{5,4},{6,7},{7,6},{8,9},{9,8},{10,11... | collective-permute-start | bytes 98312 | tf_op jit(solution)/shard_map/ppermute | solution.py:252
  36.3 18.2 %collective-permute-start.12 = (bf16[256,1152]{1,0:T(8,128)(2,1)}, bf16[256,1152]{1,0:T(8,128)(2,1)S(1)}, u32[]{:S(2)}, u32[]{:S(2)}) collective-permute-start(bf16[256,1152]{1,0:T(8,128)(2,1)} %get-tuple-element.40.refs_5_), channel_id=1, source_target_pairs={{0,4},{4,8},{8,12},{12,0},{1,5},{5,9},{9,13},{13,1},{2,6},{6,10},{... | collective-permute-start | bytes 1769480 | tf_op jit(solution)/shard_map/ppermute | solution.py:320
  39.4 15.1 %collective-permute-start.13 = (bf16[256,1152]{1,0:T(8,128)(2,1)}, bf16[256,1152]{1,0:T(8,128)(2,1)S(1)}, u32[]{:S(2)}, u32[]{:S(2)}) collective-permute-start(bf16[256,1152]{1,0:T(8,128)(2,1)} %get-tuple-element.40.refs_5_), channel_id=1, source_target_pairs={{0,1},{1,0},{2,3},{3,2},{4,5},{5,4},{6,7},{7,6},{8,9},{9,8},{10,11... | collective-permute-start | bytes 1769480 | tf_op jit(solution)/shard_map/ppermute | solution.py:338
  41.3 3.1 %copy-start.9 = (bf16[256,896]{1,0:T(8,128)(2,1)}, bf16[256,896]{1,0:T(8,128)(2,1)S(1)}, u32[]{:S(2)}) copy-start(bf16[256,896]{1,0:T(8,128)(2,1)S(1)} %collective-permute-done.9.refs_2_) | copy-start | bytes 1376260
  45.3 10.5 %collective-permute-start.15 = (bf16[512,384]{1,0:T(8,128)(2,1)}, bf16[512,384]{1,0:T(8,128)(2,1)}, u32[]{:S(2)}, u32[]{:S(2)}) collective-permute-start(bf16[512,384]{1,0:T(8,128)(2,1)} %get-tuple-element.42.refs_2_), channel_id=1, source_target_pairs={{0,16},{16,0},{1,17},{17,1},{2,18},{18,2},{3,19},{19,3},{4,20},{20... | collective-permute-start | bytes 1179656 | tf_op jit(solution)/shard_map/ppermute | solution.py:283
  46.5 8.4 %collective-permute-start.14 = (bf16[384,384]{1,0:T(8,128)(2,1)}, bf16[384,384]{1,0:T(8,128)(2,1)}, u32[]{:S(2)}, u32[]{:S(2)}) collective-permute-start(bf16[384,384]{1,0:T(8,128)(2,1)} %get-tuple-element.41), channel_id=1, source_target_pairs={{2,0},{0,2},{3,1},{1,3},{6,4},{4,6},{7,5},{5,7},{10,8},{8,10},{11,... | collective-permute-start | bytes 884744 | tf_op jit(solution)/shard_map/ppermute | solution.py:277
  48.0 17.1 %collective-permute-start.16 = (bf16[256,896]{1,0:T(8,128)(2,1)}, bf16[256,896]{1,0:T(8,128)(2,1)}, u32[]{:S(2)}, u32[]{:S(2)}) collective-permute-start(bf16[256,896]{1,0:T(8,128)(2,1)} %get-tuple-element.44.refs_0_), channel_id=1, source_target_pairs={{0,4},{4,8},{8,12},{12,0},{1,5},{5,9},{9,13},{13,1},{2,6},{6,10},{... | collective-permute-start | bytes 1376264 | tf_op jit(solution)/shard_map/ppermute | solution.py:320
  54.5 1.3 %copy-start.13 = (bf16[256,1152]{1,0:T(8,128)(2,1)}, bf16[256,1152]{1,0:T(8,128)(2,1)S(1)}, u32[]{:S(2)}) copy-start(bf16[256,1152]{1,0:T(8,128)(2,1)S(1)} %collective-permute-done.12.refs_1_) | copy-start | bytes 1769476
  54.5 10.6 %collective-permute-start.17 = (bf16[256,896]{1,0:T(8,128)(2,1)}, bf16[256,896]{1,0:T(8,128)(2,1)S(1)}, u32[]{:S(2)}, u32[]{:S(2)}) collective-permute-start(bf16[256,896]{1,0:T(8,128)(2,1)} %get-tuple-element.44.refs_0_), channel_id=1, source_target_pairs={{0,1},{1,0},{2,3},{3,2},{4,5},{5,4},{6,7},{7,6},{8,9},{9,8},{10,11... | collective-permute-start | bytes 1376264 | tf_op jit(solution)/shard_map/ppermute | solution.py:338
  54.5 1.3 %copy-start.1 = (bf16[256,1152]{1,0:T(8,128)(2,1)}, bf16[256,1152]{1,0:T(8,128)(2,1)S(1)}, u32[]{:S(2)}) copy-start(bf16[256,1152]{1,0:T(8,128)(2,1)S(1)} %collective-permute-done.13.refs_2_) | copy-start | bytes 1769476
  55.8 15.1 %collective-permute-start.21 = (bf16[256,1152]{1,0:T(8,128)(2,1)}, bf16[256,1152]{1,0:T(8,128)(2,1)S(1)}, u32[]{:S(2)}, u32[]{:S(2)}) collective-permute-start(bf16[256,1152]{1,0:T(8,128)(2,1)} %get-tuple-element.54.refs_1_), channel_id=1, source_target_pairs={{0,1},{1,0},{2,3},{3,2},{4,5},{5,4},{6,7},{7,6},{8,9},{9,8},{10,11... | collective-permute-start | bytes 1769480 | tf_op jit(solution)/shard_map/ppermute | solution.py:338
  55.9 20.3 %collective-permute-start.19 = (bf16[256,1152]{1,0:T(8,128)(2,1)}, bf16[256,1152]{1,0:T(8,128)(2,1)S(1)}, u32[]{:S(2)}, u32[]{:S(2)}) collective-permute-start(bf16[256,1152]{1,0:T(8,128)(2,1)} %get-tuple-element.54.refs_1_), channel_id=1, source_target_pairs={{0,4},{4,8},{8,12},{12,0},{1,5},{5,9},{9,13},{13,1},{2,6},{6,10},{... | collective-permute-start | bytes 1769480 | tf_op jit(solution)/shard_map/ppermute | solution.py:320
  55.9 9.6 %collective-permute-start.18 = (bf16[384,384]{1,0:T(8,128)(2,1)}, bf16[384,384]{1,0:T(8,128)(2,1)S(1)}, u32[]{:S(2)}, u32[]{:S(2)}) collective-permute-start(bf16[384,384]{1,0:T(8,128)(2,1)} %get-tuple-element.45.refs_0_), channel_id=1, source_target_pairs={{0,16},{16,0},{1,17},{17,1},{2,18},{18,2},{3,19},{19,3},{4,20},{20... | collective-permute-start | bytes 884744 | tf_op jit(solution)/shard_map/ppermute | solution.py:283
  57.5 3.4 %copy-start.2 = (bf16[256,1152]{1,0:T(8,128)(2,1)S(1)}, bf16[256,1152]{1,0:T(8,128)(2,1)}, u32[]{:S(2)}) copy-start(bf16[256,1152]{1,0:T(8,128)(2,1)} %get-tuple-element.49.refs_7_) | copy-start | bytes 1769476
  57.5 3.4 %copy-start.4 = (bf16[256,1152]{1,0:T(8,128)(2,1)S(1)}, bf16[256,1152]{1,0:T(8,128)(2,1)}, u32[]{:S(2)}) copy-start(bf16[256,1152]{1,0:T(8,128)(2,1)} %get-tuple-element.40.refs_5_) | copy-start | bytes 1769476
  57.5 3.4 %copy-start.6 = (bf16[256,1152]{1,0:T(8,128)(2,1)S(1)}, bf16[256,1152]{1,0:T(8,128)(2,1)}, u32[]{:S(2)}) copy-start(bf16[256,1152]{1,0:T(8,128)(2,1)} %get-tuple-element.47.refs_3_) | copy-start | bytes 1769476
  57.5 3.4 %copy-start.8 = (bf16[256,896]{1,0:T(8,128)(2,1)S(1)}, bf16[256,896]{1,0:T(8,128)(2,1)}, u32[]{:S(2)}) copy-start(bf16[256,896]{1,0:T(8,128)(2,1)} %copy-done.7) | copy-start | bytes 1376260
  57.5 3.4 %copy-start.10 = (bf16[256,896]{1,0:T(8,128)(2,1)S(1)}, bf16[256,896]{1,0:T(8,128)(2,1)}, u32[]{:S(2)}) copy-start(bf16[256,896]{1,0:T(8,128)(2,1)} %get-tuple-element.48.refs_6_) | copy-start | bytes 1376260
  57.5 3.4 %copy-start.12 = (bf16[256,896]{1,0:T(8,128)(2,1)S(1)}, bf16[256,896]{1,0:T(8,128)(2,1)}, u32[]{:S(2)}) copy-start(bf16[256,896]{1,0:T(8,128)(2,1)} %get-tuple-element.46.refs_2_) | copy-start | bytes 1376260
  66.1 1.8 %copy-start.17 = (bf16[32,384]{1,0:T(8,128)(2,1)S(1)}, bf16[32,384]{1,0:T(8,128)(2,1)}, u32[]{:S(2)}) copy-start(bf16[32,384]{1,0:T(8,128)(2,1)} %refs_3_.1) | copy-start | bytes 73732
  68.0 2.9 %copy-start.14 = (bf16[256,1152]{1,0:T(8,128)(2,1)S(1)}, bf16[256,1152]{1,0:T(8,128)(2,1)}, u32[]{:S(2)}) copy-start(bf16[256,1152]{1,0:T(8,128)(2,1)} %get-tuple-element.54.refs_1_) | copy-start | bytes 1769476
  68.0 2.9 %copy-start.16 = (bf16[256,896]{1,0:T(8,128)(2,1)S(1)}, bf16[256,896]{1,0:T(8,128)(2,1)}, u32[]{:S(2)}) copy-start(bf16[256,896]{1,0:T(8,128)(2,1)} %get-tuple-element.56.refs_2_) | copy-start | bytes 1376260
  69.5 1.3 %collective-permute-start.20 = (f32[2,32,256]{2,1,0:T(8,128)S(1)}, f32[2,32,256]{2,1,0:T(8,128)S(1)}, u32[]{:S(2)}, u32[]{:S(2)}) collective-permute-start(f32[2,32,256]{2,1,0:T(8,128)S(1)} %shards.4), channel_id=1, source_target_pairs={{0,1},{1,0},{2,3},{3,2},{4,5},{5,4},{6,7},{7,6},{8,9},{9,8},{10,11... | collective-permute-start | bytes 196616 | tf_op jit(solution)/shard_map/ppermute | solution.py:361
  70.9 5.3 %copy-start.18 = (f32[8,128]{1,0:T(8,128)S(1)}, f32[8,128]{1,0:T(8,128)}, u32[]{:S(2)}) copy-start(f32[8,128]{1,0:T(8,128)} %get-tuple-element.53.refs_0_) | copy-start | bytes 12292
  76.2 4.8 %collective-permute-start.22 = (bf16[256,1152]{1,0:T(8,128)(2,1)S(1)}, bf16[256,1152]{1,0:T(8,128)(2,1)S(1)}, u32[]{:S(2)}, u32[]{:S(2)}) collective-permute-start(bf16[256,1152]{1,0:T(8,128)(2,1)S(1)} %get-tuple-element.57.mine), channel_id=1, source_target_pairs={{0,1},{1,0},{2,3},{3,2},{4,5},{5,4},{6,7},{7,6},{8,9},{9,8},{10,11... | collective-permute-start | bytes 1769480 | tf_op jit(solution)/shard_map/ppermute | solution.py:370
  76.2 2.7 %collective-permute-start.23 = (bf16[256,896]{1,0:T(8,128)(2,1)}, bf16[256,896]{1,0:T(8,128)(2,1)S(1)}, u32[]{:S(2)}, u32[]{:S(2)}) collective-permute-start(bf16[256,896]{1,0:T(8,128)(2,1)} %get-tuple-element.58.mine), channel_id=1, source_target_pairs={{0,1},{1,0},{2,3},{3,2},{4,5},{5,4},{6,7},{7,6},{8,9},{9,8},{10,11... | collective-permute-start | bytes 1376264 | tf_op jit(solution)/shard_map/ppermute | solution.py:370
  76.7 5.9 %collective-permute-start.27 = (f32[1,32,256]{2,1,0:T(8,128)S(1)}, f32[1,32,256]{2,1,0:T(8,128)S(1)}, u32[]{:S(2)}, u32[]{:S(2)}) collective-permute-start(f32[1,32,256]{2,1,0:T(8,128)S(1)} %shards.5), channel_id=1, source_target_pairs={{0,1},{1,0},{2,3},{3,2},{4,5},{5,4},{6,7},{7,6},{8,9},{9,8},{10,11... | collective-permute-start | bytes 98312 | tf_op jit(solution)/shard_map/ppermute | solution.py:361
  76.7 8.6 %collective-permute-start.26 = (f32[32,256]{1,0:T(8,128)S(1)}, f32[32,256]{1,0:T(8,128)S(1)}, u32[]{:S(2)}, u32[]{:S(2)}) collective-permute-start(f32[32,256]{1,0:T(8,128)S(1)} %get-tuple-element.61), channel_id=1, source_target_pairs={{0,12},{4,0},{8,4},{12,8},{1,13},{5,1},{9,5},{13,9},{2,14},{6,2},{... | collective-permute-start | bytes 98312 | tf_op jit(solution)/shard_map/ppermute | solution.py:364
  80.9 6.5 %copy-start.19 = (s32[256,2]{0,1:T(2,128)S(1)}, s32[256,2]{0,1:T(2,128)}, u32[]{:S(2)}) copy-start(s32[256,2]{0,1:T(2,128)} %param.10) | copy-start | bytes 6148
  80.9 6.5 %copy-start.20 = (s32[1,256]{1,0:T(1,128)S(1)}, s32[1,256]{1,0:T(1,128)}, u32[]{:S(2)}) copy-start(s32[1,256]{1,0:T(1,128)} %docs.3) | copy-start | bytes 3076
  82.3 1.2 %collective-permute-start.24 = (f32[32,256]{1,0:T(8,128)S(1)}, f32[32,256]{1,0:T(8,128)S(1)}, u32[]{:S(2)}, u32[]{:S(2)}) collective-permute-start(f32[32,256]{1,0:T(8,128)S(1)} %part.3), channel_id=1, source_target_pairs={{0,1},{1,0},{2,3},{3,2},{4,5},{5,4},{6,7},{7,6},{8,9},{9,8},{10,11... | collective-permute-start | bytes 98312 | tf_op jit(solution)/shard_map/ppermute | solution.py:379
  82.6 4.9 %collective-permute-start.28 = (f32[32,256]{1,0:T(8,128)S(1)}, f32[32,256]{1,0:T(8,128)S(1)}, u32[]{:S(2)}, u32[]{:S(2)}) collective-permute-start(f32[32,256]{1,0:T(8,128)S(1)} %add_bitcast_fusion), channel_id=1, source_target_pairs={{0,8},{4,12},{8,0},{12,4},{1,9},{5,13},{9,1},{13,5},{2,10},{6,14},... | collective-permute-start | bytes 98312 | tf_op jit(solution)/shard_map/ppermute | solution.py:364
  83.6 5.7 %collective-permute-start.25 = (f32[32,256]{1,0:T(8,128)S(1)}, f32[32,256]{1,0:T(8,128)S(1)}, u32[]{:S(2)}, u32[]{:S(2)}) collective-permute-start(f32[32,256]{1,0:T(8,128)S(1)} %add.10), channel_id=1, source_target_pairs={{0,4},{4,8},{8,12},{12,0},{1,5},{5,9},{9,13},{13,1},{2,6},{6,10},{... | collective-permute-start | bytes 98312 | tf_op jit(solution)/shard_map/ppermute | solution.py:380
  (8 other events, 6.9 us)

commit v7 on v6

--- a/solution.py
+++ b/solution.py
@@ -344,7 +344,7 @@
         begun.append(shards_call(low, high, [(0,)] * (high - low), 0, (), False))
     ready = exchanged.pop(0)
     turn, got = ordered(
-        turn, [mine[-1][0], *ready, *swapping], [x[0, :8, :LANES] for x in begun]
+        turn, [mine[-1][0], *ready, *swapping], [x[0, :8, :LANES] for x in begun], False
     )
     mine[-1][0] = got[0]
     flat += got[1 : 1 + len(ready)] + exchanged.pop(0)

time: 90.6 us -> 90.6 us (level)
    unnamed x54 -> x50, local copies, waits for them, and re-layouts: 2.69 us -> 2.64 us
where the time goes in v7:
time: 90.6 us; the launch traced here: 90.2 us
  waiting for transfers between devices  35.7 us (39%)
  starting transfers between devices  23.8 us (26%)
  Pallas kernels  19.2 us (21%)
  other arithmetic  6.14 us (7%)
  local copies, waits for them, and re-layouts  4.6 us (5%)
    ppermute x6, waiting for transfers between devices, on_device(): moved = [lax.ppermute(x, 'exp', ring) for x in mine[-1]]  15.3 us
    ppermute x4, waiting for transfers between devices, along_dat(): lax.ppermute(x, 'dat', [((z + k) % dats, z) for z in range(dats)])  12.7 us
    pallas_call x5, Pallas kernels, vmem_call(): pl.pallas_call(kernel, in_specs=[hbm] * far + [vmem] * (len(args) - far),...  12.4 us
    ppermute x6, starting transfers between devices, on_device(): moved = [lax.ppermute(x, 'exp', ring) for x in mine[-1]]  6.48 us
    ppermute x4, starting transfers between devices, over_grp(): return [lax.ppermute(x, 'grp', swap) for x in xs]  6.06 us
    select_n x3, other arithmetic, on_device(): jnp.where(grp == 0, gate[low:high], up[low:high])  6.04 us
    ppermute x4, starting transfers between devices, along_dat(): lax.ppermute(x, 'dat', [((z + k) % dats, z) for z in range(dats)])  5.96 us
    pallas_call x2, Pallas kernels, join(): pl.pallas_call(functools.partial(join_kernel, dats, edges), in_specs=[pl....  5.17 us
  transfers between devices with their start and end apart: 29, of which 16 were waited for; matrix products, arithmetic and copies ran while one was open for 8% of the time, Pallas kernels for 20%

profile of v7, /device:TPU:0, one launch (start us, length us, event | category | flops | bytes accessed | tf_op | source)
XLA Modules:
  0.0 90.2 jit_solution(16784350039645611192)
XLA Ops:
  0.0 1.2 %slice.47.refs_0_ = bf16[256,896]{1,0:T(8,128)(2,1)S(1)} slice(bf16[256,2048]{1,0:T(8,128)(2,1)} %param.8), slice={[0:256], [0:896]} | slice | bytes 917504 | tf_op jit(solution)/shard_map/slice | solution.py:259
  1.2 3.1 %collective-permute-start.1 = (bf16[256,896]{1,0:T(8,128)(2,1)S(1)}, bf16[256,896]{1,0:T(8,128)(2,1)}, u32[]{:S(2)}, u32[]{:S(2)}) collective-permute-start(bf16[256,896]{1,0:T(8,128)(2,1)S(1)} %slice.47.refs_0_), channel_id=1, source_target_pairs={{0,4},{4,8},{8,12},{12,0},{1,5},{5,9},{9,13},{13,1},{2,6},{6,10},{... | collective-permute-start | bytes 1376264 | tf_op jit(solution)/shard_map/ppermute | solution.py:320
  4.3 2.3 %select_bitcast_fusion = (bf16[576,384]{1,0:T(8,128)(2,1)}, bf16[576,384]{1,0:T(8,128)(2,1)S(1)}) fusion(bf16[1,2048,384]{2,1,0:T(8,128)(2,1)} %param.13, bf16[1,2048,384]{2,1,0:T(8,128)(2,1)} %param.12, pred[]{:T(512)S(6)} %eq.2), kind=kLoop, calls=%fused_computation | loop fusion | flops 442368 | bytes 2654209 | tf_op jit(solution)/shard_map/jit(_where)/select_n | solution.py:270
  6.6 1.5 %collective-permute-start.2 = (bf16[576,384]{1,0:T(8,128)(2,1)S(1)}, bf16[576,384]{1,0:T(8,128)(2,1)S(1)}, u32[]{:S(2)}, u32[]{:S(2)}) collective-permute-start(bf16[576,384]{1,0:T(8,128)(2,1)S(1)} %get-tuple-element.60), channel_id=1, source_target_pairs={{2,0},{0,2},{3,1},{1,3},{6,4},{4,6},{7,5},{5,7},{10,8},{8,10},{11,... | collective-permute-start | bytes 1327112 | tf_op jit(solution)/shard_map/ppermute | solution.py:277
  8.2 1.6 %collective-permute-start.3 = (bf16[256,1152]{1,0:T(8,128)(2,1)S(1)}, bf16[256,1152]{1,0:T(8,128)(2,1)S(1)}, u32[]{:S(2)}, u32[]{:S(2)}) collective-permute-start(bf16[256,1152]{1,0:T(8,128)(2,1)S(1)} %slice.52.refs_1_), channel_id=1, source_target_pairs={{0,4},{4,8},{8,12},{12,0},{1,5},{5,9},{9,13},{13,1},{2,6},{6,10},{... | collective-permute-start | bytes 1769480 | tf_op jit(solution)/shard_map/ppermute | solution.py:320
  10.0 8.2 %collective-permute-done.2.refs_2_ = bf16[576,384]{1,0:T(8,128)(2,1)S(1)} collective-permute-done((bf16[576,384]{1,0:T(8,128)(2,1)S(1)}, bf16[576,384]{1,0:T(8,128)(2,1)S(1)}, u32[]{:S(2)}, u32[]{:S(2)}) %collective-permute-start.2) | collective-permute-done | bytes 442400 | tf_op jit(solution)/shard_map/ppermute | solution.py:277
  18.2 0.6 broadcast_in_dim.3.refs_0_
  19.0 1.5 %collective-permute-start.7 = (bf16[576,384]{1,0:T(8,128)(2,1)}, bf16[576,384]{1,0:T(8,128)(2,1)}, u32[]{:S(2)}, u32[]{:S(2)}) collective-permute-start(bf16[576,384]{1,0:T(8,128)(2,1)} %get-tuple-element.34.refs_0_), channel_id=1, source_target_pairs={{0,16},{16,0},{1,17},{17,1},{2,18},{18,2},{3,19},{19,3},{4,20},{20... | collective-permute-start | bytes 1327112 | tf_op jit(solution)/shard_map/ppermute | solution.py:283
  20.5 1.5 %collective-permute-start.6 = (bf16[576,384]{1,0:T(8,128)(2,1)}, bf16[576,384]{1,0:T(8,128)(2,1)}, u32[]{:S(2)}, u32[]{:S(2)}) collective-permute-start(bf16[576,384]{1,0:T(8,128)(2,1)} %get-tuple-element.33), channel_id=1, source_target_pairs={{2,0},{0,2},{3,1},{1,3},{6,4},{4,6},{7,5},{5,7},{10,8},{8,10},{11,... | collective-permute-start | bytes 1327112 | tf_op jit(solution)/shard_map/ppermute | solution.py:277
  22.0 0.8 copy-done.11
  22.8 1.6 %collective-permute-start.8 = (bf16[256,896]{1,0:T(8,128)(2,1)}, bf16[256,896]{1,0:T(8,128)(2,1)}, u32[]{:S(2)}, u32[]{:S(2)}) collective-permute-start(bf16[256,896]{1,0:T(8,128)(2,1)} %get-tuple-element.36.refs_4_), channel_id=1, source_target_pairs={{0,4},{4,8},{8,12},{12,0},{1,5},{5,9},{9,13},{13,1},{2,6},{6,10},{... | collective-permute-start | bytes 1376264 | tf_op jit(solution)/shard_map/ppermute | solution.py:320
  24.3 1.9 %select_bitcast_fusion.2.refs_6_ = bf16[512,384]{1,0:T(8,128)(2,1)} fusion(bf16[1,2048,384]{2,1,0:T(8,128)(2,1)} %param.13, bf16[1,2048,384]{2,1,0:T(8,128)(2,1)} %param.12, pred[]{:T(512)S(6)} %eq.2), kind=kLoop, calls=%fused_computation.2 | loop fusion | flops 196608 | bytes 1179649 | tf_op jit(solution)/shard_map/jit(_where)/select_n | solution.py:270
  26.3 4.0 %collective-permute-done.3.refs_1_ = bf16[256,1152]{1,0:T(8,128)(2,1)S(1)} collective-permute-done((bf16[256,1152]{1,0:T(8,128)(2,1)S(1)}, bf16[256,1152]{1,0:T(8,128)(2,1)S(1)}, u32[]{:S(2)}, u32[]{:S(2)}) %collective-permute-start.3) | collective-permute-done | bytes 589856 | tf_op jit(solution)/shard_map/ppermute | solution.py:320
  30.3 1.0 %collective-permute-done.6.refs_4_ = bf16[576,384]{1,0:T(8,128)(2,1)} collective-permute-done((bf16[576,384]{1,0:T(8,128)(2,1)}, bf16[576,384]{1,0:T(8,128)(2,1)}, u32[]{:S(2)}, u32[]{:S(2)}) %collective-permute-start.6) | collective-permute-done | bytes 442400 | tf_op jit(solution)/shard_map/ppermute | solution.py:277
  31.4 1.8 %collective-permute-start.11 = (bf16[576,384]{1,0:T(8,128)(2,1)}, bf16[576,384]{1,0:T(8,128)(2,1)S(1)}, u32[]{:S(2)}, u32[]{:S(2)}) collective-permute-start(bf16[576,384]{1,0:T(8,128)(2,1)} %get-tuple-element.38.refs_1_), channel_id=1, source_target_pairs={{0,16},{16,0},{1,17},{17,1},{2,18},{18,2},{3,19},{19,3},{4,20},{20... | collective-permute-start | bytes 1327112 | tf_op jit(solution)/shard_map/ppermute | solution.py:283
  33.1 1.5 %collective-permute-start.10 = (bf16[512,384]{1,0:T(8,128)(2,1)}, bf16[512,384]{1,0:T(8,128)(2,1)S(1)}, u32[]{:S(2)}, u32[]{:S(2)}) collective-permute-start(bf16[512,384]{1,0:T(8,128)(2,1)} %get-tuple-element.37), channel_id=1, source_target_pairs={{2,0},{0,2},{3,1},{1,3},{6,4},{4,6},{7,5},{5,7},{10,8},{8,10},{11,... | collective-permute-start | bytes 1179656 | tf_op jit(solution)/shard_map/ppermute | solution.py:277
  34.6 0.4 fusion.grad_mine
  35.1 1.2 %collective-permute-done.refs_6_.grad_other = f32[32,256]{1,0:T(8,128)S(1)} collective-permute-done((f32[32,256]{1,0:T(8,128)S(1)}, f32[32,256]{1,0:T(8,128)S(1)}, u32[]{:S(2)}, u32[]{:S(2)}) %collective-permute-start) | collective-permute-done | bytes 32800 | tf_op jit(solution)/shard_map/ppermute | solution.py:252
  36.5 2.9 %collective-permute-done.8.refs_1_ = bf16[256,896]{1,0:T(8,128)(2,1)} collective-permute-done((bf16[256,896]{1,0:T(8,128)(2,1)}, bf16[256,896]{1,0:T(8,128)(2,1)}, u32[]{:S(2)}, u32[]{:S(2)}) %collective-permute-start.8) | collective-permute-done | bytes 458784 | tf_op jit(solution)/shard_map/ppermute | solution.py:320
  39.4 1.8 %select_bitcast_fusion.3.refs_5_ = bf16[384,384]{1,0:T(8,128)(2,1)} fusion(bf16[1,2048,384]{2,1,0:T(8,128)(2,1)} %param.13, bf16[1,2048,384]{2,1,0:T(8,128)(2,1)} %param.12, pred[]{:T(512)S(6)} %eq.2), kind=kLoop, calls=%fused_computation.3 | loop fusion | flops 147456 | bytes 884737 | tf_op jit(solution)/shard_map/jit(_where)/select_n | solution.py:270
  41.3 3.1 %collective-permute-done.10.refs_3_ = bf16[512,384]{1,0:T(8,128)(2,1)S(1)} collective-permute-done((bf16[512,384]{1,0:T(8,128)(2,1)}, bf16[512,384]{1,0:T(8,128)(2,1)S(1)}, u32[]{:S(2)}, u32[]{:S(2)}) %collective-permute-start.10) | collective-permute-done | bytes 393248 | tf_op jit(solution)/shard_map/ppermute | solution.py:277
  44.4 0.8 copy-done.22
  45.3 1.2 %collective-permute-start.15 = (bf16[512,384]{1,0:T(8,128)(2,1)}, bf16[512,384]{1,0:T(8,128)(2,1)}, u32[]{:S(2)}, u32[]{:S(2)}) collective-permute-start(bf16[512,384]{1,0:T(8,128)(2,1)} %get-tuple-element.42.refs_2_), channel_id=1, source_target_pairs={{0,16},{16,0},{1,17},{17,1},{2,18},{18,2},{3,19},{19,3},{4,20},{20... | collective-permute-start | bytes 1179656 | tf_op jit(solution)/shard_map/ppermute | solution.py:283
  46.5 1.5 %collective-permute-start.14 = (bf16[384,384]{1,0:T(8,128)(2,1)}, bf16[384,384]{1,0:T(8,128)(2,1)}, u32[]{:S(2)}, u32[]{:S(2)}) collective-permute-start(bf16[384,384]{1,0:T(8,128)(2,1)} %get-tuple-element.41), channel_id=1, source_target_pairs={{2,0},{0,2},{3,1},{1,3},{6,4},{4,6},{7,5},{5,7},{10,8},{8,10},{11,... | collective-permute-start | bytes 884744 | tf_op jit(solution)/shard_map/ppermute | solution.py:277
  48.0 6.5 %collective-permute-done.12.refs_1_ = bf16[256,1152]{1,0:T(8,128)(2,1)S(1)} collective-permute-done((bf16[256,1152]{1,0:T(8,128)(2,1)}, bf16[256,1152]{1,0:T(8,128)(2,1)S(1)}, u32[]{:S(2)}, u32[]{:S(2)}) %collective-permute-start.12) | collective-permute-done | bytes 589856 | tf_op jit(solution)/shard_map/ppermute | solution.py:320
  54.5 0.4 collective-permute-done.14.refs_3_
  54.9 0.9 collective-permute-done.15.refs_4_
  55.8 1.6 %collective-permute-start.18 = (bf16[384,384]{1,0:T(8,128)(2,1)}, bf16[384,384]{1,0:T(8,128)(2,1)S(1)}, u32[]{:S(2)}, u32[]{:S(2)}) collective-permute-start(bf16[384,384]{1,0:T(8,128)(2,1)} %get-tuple-element.45.refs_0_), channel_id=1, source_target_pairs={{0,16},{16,0},{1,17},{17,1},{2,18},{18,2},{3,19},{19,3},{4,20},{20... | collective-permute-start | bytes 884744 | tf_op jit(solution)/shard_map/ppermute | solution.py:283
  57.5 3.4 %join.2.refs_8_.refs_4_.refs_0_ = bf16[2,1664,768]{2,1,0:T(8,128)(2,1)S(1)} custom-call(s32[3]{0:T(128)S(1)} %pad_add_fusion.where, bf16[2048,384]{1,0:T(8,128)(2,1)} %bitcast.34, bf16[2048,384]{1,0:T(8,128)(2,1)} %bitcast.32, bf16[576,384]{1,0:T(8,128)(2,1)} %get-tuple-element.34.refs_0_, bf16[576,384]{1,0:T(8,128)(2,1)} %get-tuple-element.38.refs_1_, ...), custom_call_target="tpu_custom_call" | custom-call | flops 1 | bytes 1 | tf_op jit(solution)/shard_map/join/pallas_call | solution.py:74
  61.0 4.1 %shards.3.refs_9_ = f32[2,256,768]{2,1,0:T(8,128)S(1)} custom-call(bf16[256,896]{1,0:T(8,128)(2,1)S(1)} %copy-done.8, bf16[256,1152]{1,0:T(8,128)(2,1)S(1)} %slice.52.refs_1_, bf16[256,896]{1,0:T(8,128)(2,1)S(1)} %copy-done.12, bf16[256,1152]{1,0:T(8,128)(2,1)S(1)} %copy-done.6, bf16[256,896]{1,0:T(8,128)(2,1)} %get-tuple-element.36.refs_4_, ...), custom_call_target="tpu_custom_call" | custom-call | flops 1 | bytes 1 | tf_op jit(solution)/shard_map/shards/pallas_call | solution.py:171
  65.1 0.3 collective-permute-done.18.refs_3_
  65.4 0.7 copy-done.15
  66.1 1.8 %join.3.refs_8_.refs_5_.refs_1_ = bf16[2,384,768]{2,1,0:T(8,128)(2,1)S(1)} custom-call(s32[3]{0:T(128)S(1)} %pad_add_fusion.where, bf16[2048,384]{1,0:T(8,128)(2,1)} %bitcast.35, bf16[2048,384]{1,0:T(8,128)(2,1)} %bitcast.33, bf16[384,384]{1,0:T(8,128)(2,1)} %get-tuple-element.45.refs_0_, bf16[384,384]{1,0:T(8,128)(2,1)} %copy-done.15), custom_call_target="tpu_custom_call" | custom-call | flops 1 | bytes 1 | tf_op jit(solution)/shard_map/join/pallas_call | solution.py:74
  68.0 1.5 %shards.4 = f32[2,32,256]{2,1,0:T(8,128)S(1)} custom-call(bf16[256,896]{1,0:T(8,128)(2,1)S(1)} %copy-done.8, bf16[256,1152]{1,0:T(8,128)(2,1)S(1)} %slice.52.refs_1_, bf16[256,896]{1,0:T(8,128)(2,1)S(1)} %copy-done.12, bf16[256,1152]{1,0:T(8,128)(2,1)S(1)} %copy-done.6, bf16[256,896]{1,0:T(8,128)(2,1)} %get-tuple-element.36.refs_4_, ...), custom_call_target="tpu_custom_call" | custom-call | flops 1 | bytes 1 | tf_op jit(solution)/shard_map/shards/pallas_call | solution.py:171
  69.5 1.2 %collective-permute-done.20 = f32[2,32,256]{2,1,0:T(8,128)S(1)} collective-permute-done((f32[2,32,256]{2,1,0:T(8,128)S(1)}, f32[2,32,256]{2,1,0:T(8,128)S(1)}, u32[]{:S(2)}, u32[]{:S(2)}) %collective-permute-start.20) | collective-permute-done | bytes 65568 | tf_op jit(solution)/shard_map/ppermute | solution.py:361
  70.8 3.5 %shards.5 = f32[1,32,256]{2,1,0:T(8,128)S(1)} custom-call(bf16[256,896]{1,0:T(8,128)(2,1)} %get-tuple-element.44.refs_0_, bf16[256,1152]{1,0:T(8,128)(2,1)S(1)} %copy-done.14, bf16[256,896]{1,0:T(8,128)(2,1)S(1)} %get-tuple-element.56.refs_2_, bf16[256,1152]{1,0:T(8,128)(2,1)S(1)} %collective-permute-done.21.refs_3_, ...), custom_call_target="tpu_custom_call" | custom-call | flops 1 | bytes 1 | tf_op jit(solution)/shard_map/shards/pallas_call | solution.py:171
  74.3 1.8 %collective-permute-done.19.refs_1_ = bf16[256,1152]{1,0:T(8,128)(2,1)S(1)} collective-permute-done((bf16[256,1152]{1,0:T(8,128)(2,1)}, bf16[256,1152]{1,0:T(8,128)(2,1)S(1)}, u32[]{:S(2)}, u32[]{:S(2)}) %collective-permute-start.19) | collective-permute-done | bytes 589856 | tf_op jit(solution)/shard_map/ppermute | solution.py:320
  76.2 0.5 collective-permute-start.23
  76.7 2.0 %collective-permute-start.26 = (f32[32,256]{1,0:T(8,128)S(1)}, f32[32,256]{1,0:T(8,128)S(1)}, u32[]{:S(2)}, u32[]{:S(2)}) collective-permute-start(f32[32,256]{1,0:T(8,128)S(1)} %get-tuple-element.61), channel_id=1, source_target_pairs={{0,12},{4,0},{8,4},{12,8},{1,13},{5,1},{9,5},{13,9},{2,14},{6,2},{... | collective-permute-start | bytes 98312 | tf_op jit(solution)/shard_map/ppermute | solution.py:364
  78.9 2.0 %part.2.refs_2_ = f32[256,768]{1,0:T(8,128)S(1)} custom-call(bf16[256,896]{1,0:T(8,128)(2,1)} %get-tuple-element.58.mine, bf16[256,896]{1,0:T(8,128)(2,1)S(1)} %collective-permute-done.23.other, bf16[2,1664,768]{2,1,0:T(8,128)(2,1)S(1)} %join.2.refs_8_.refs_4_.refs_0_, bf16[2,384,768]{2,1,0:T(8,128)(2,1)S(1)} %join.3.refs_8_.refs_5_.refs_1_), custom_call_target="tpu_custom_call" | custom-call | flops 1 | bytes 1 | tf_op jit(solution)/shard_map/part/pallas_call | solution.py:171
  80.9 1.4 %part.3 = f32[32,256]{1,0:T(8,128)S(1)} custom-call(bf16[256,1152]{1,0:T(8,128)(2,1)S(1)} %get-tuple-element.57.mine, bf16[256,1152]{1,0:T(8,128)(2,1)S(1)} %collective-permute-done.22.other, bf16[2,1664,768]{2,1,0:T(8,128)(2,1)S(1)} %join.2.refs_8_.refs_4_.refs_0_, bf16[2,384,768]{2,1,0:T(8,128)(2,1)S(1)} %join.3.refs_8_.refs_5_.refs_1_, ...), custom_call_target="tpu_custom_call" | custom-call | flops 1 | bytes 1 | tf_op jit(solution)/shard_map/part/pallas_call | solution.py:171
  82.6 0.6 collective-permute-start.28
  83.1 0.4 collective-permute-done.24
  83.6 1.6 %collective-permute-start.25 = (f32[32,256]{1,0:T(8,128)S(1)}, f32[32,256]{1,0:T(8,128)S(1)}, u32[]{:S(2)}, u32[]{:S(2)}) collective-permute-start(f32[32,256]{1,0:T(8,128)S(1)} %add.10), channel_id=1, source_target_pairs={{0,4},{4,8},{8,12},{12,0},{1,5},{5,9},{9,13},{13,1},{2,6},{6,10},{... | collective-permute-start | bytes 98312 | tf_op jit(solution)/shard_map/ppermute | solution.py:380
  85.2 2.2 %collective-permute-done.28.refs_2_ = f32[32,256]{1,0:T(8,128)S(1)} collective-permute-done((f32[32,256]{1,0:T(8,128)S(1)}, f32[32,256]{1,0:T(8,128)S(1)}, u32[]{:S(2)}, u32[]{:S(2)}) %collective-permute-start.28) | collective-permute-done | bytes 32800 | tf_op jit(solution)/shard_map/ppermute | solution.py:364
  87.4 0.7 doc_grads.2.refs_1_
  88.1 1.2 %collective-permute-done.25.refs_0_ = f32[32,256]{1,0:T(8,128)S(1)} collective-permute-done((f32[32,256]{1,0:T(8,128)S(1)}, f32[32,256]{1,0:T(8,128)S(1)}, u32[]{:S(2)}, u32[]{:S(2)}) %collective-permute-start.25) | collective-permute-done | bytes 32800 | tf_op jit(solution)/shard_map/ppermute | solution.py:380
  89.3 1.0 %doc_grads.3 = f32[4,4,1024]{2,1,0:T(4,128)} custom-call(s32[1]{0:T(128)} %bitcast.where, f32[32,256]{1,0:T(8,128)S(1)} %fusion.grad_mine, f32[32,256]{1,0:T(8,128)S(1)} %collective-permute-done.refs_6_.grad_other, s32[1,256]{1,0:T(1,128)S(1)} %copy-done.19, s32[2,256]{1,0:T(2,128)S(1)} %bitcast.31, f32[32,256]{1,0:T(8,128)S(1)} %collective-permute-done.25.refs_0_, ...), custom_call_target="tpu_custom_call" | custom-call | flops 1 | bytes 1 | tf_op jit(solution)/shard_map/doc_grads/pallas_call | solution.py:385
  (89 shorter events, 1.7 us)
Async XLA Ops:
  0.0 34.6 %copy-start = (bf16[256,2048]{1,0:T(8,128)(2,1)S(1)}, bf16[256,2048]{1,0:T(8,128)(2,1)}, u32[]{:S(2)}) copy-start(bf16[256,2048]{1,0:T(8,128)(2,1)} %param.9) | copy-start | bytes 3145732
  0.0 8.1 %copy-start.23 = (bf16[256,2048]{1,0:T(8,128)(2,1)S(1)}, bf16[256,2048]{1,0:T(8,128)(2,1)}, u32[]{:S(2)}) copy-start(bf16[256,2048]{1,0:T(8,128)(2,1)} %param.8) | copy-start | bytes 3145732
  1.2 6.9 %copy-start.7 = (bf16[256,896]{1,0:T(8,128)(2,1)}, bf16[256,896]{1,0:T(8,128)(2,1)S(1)}, u32[]{:S(2)}) copy-start(bf16[256,896]{1,0:T(8,128)(2,1)S(1)} %slice.47.refs_0_) | copy-start | bytes 1376260
  1.2 17.0 %collective-permute-start.1 = (bf16[256,896]{1,0:T(8,128)(2,1)S(1)}, bf16[256,896]{1,0:T(8,128)(2,1)}, u32[]{:S(2)}, u32[]{:S(2)}) collective-permute-start(bf16[256,896]{1,0:T(8,128)(2,1)S(1)} %slice.47.refs_0_), channel_id=1, source_target_pairs={{0,4},{4,8},{8,12},{12,0},{1,5},{5,9},{9,13},{13,1},{2,6},{6,10},{... | collective-permute-start | bytes 1376264 | tf_op jit(solution)/shard_map/ppermute | solution.py:320
  6.6 19.7 %copy-start.24 = (bf16[32,2048]{1,0:T(8,128)(2,1)S(1)}, bf16[32,2048]{1,0:T(8,128)(2,1)}, u32[]{:S(2)}) copy-start(bf16[32,2048]{1,0:T(8,128)(2,1)} %param.15) | copy-start | bytes 393220
  6.6 11.6 %collective-permute-start.2 = (bf16[576,384]{1,0:T(8,128)(2,1)S(1)}, bf16[576,384]{1,0:T(8,128)(2,1)S(1)}, u32[]{:S(2)}, u32[]{:S(2)}) collective-permute-start(bf16[576,384]{1,0:T(8,128)(2,1)S(1)} %get-tuple-element.60), channel_id=1, source_target_pairs={{2,0},{0,2},{3,1},{1,3},{6,4},{4,6},{7,5},{5,7},{10,8},{8,10},{11,... | collective-permute-start | bytes 1327112 | tf_op jit(solution)/shard_map/ppermute | solution.py:277
  8.1 13.9 %collective-permute-start.4 = (bf16[256,896]{1,0:T(8,128)(2,1)S(1)}, bf16[256,896]{1,0:T(8,128)(2,1)S(1)}, u32[]{:S(2)}, u32[]{:S(2)}) collective-permute-start(bf16[256,896]{1,0:T(8,128)(2,1)S(1)} %slice.47.refs_0_), channel_id=1, source_target_pairs={{0,1},{1,0},{2,3},{3,2},{4,5},{5,4},{6,7},{7,6},{8,9},{9,8},{10,11... | collective-permute-start | bytes 1376264 | tf_op jit(solution)/shard_map/ppermute | solution.py:260
  8.2 22.2 %collective-permute-start.3 = (bf16[256,1152]{1,0:T(8,128)(2,1)S(1)}, bf16[256,1152]{1,0:T(8,128)(2,1)S(1)}, u32[]{:S(2)}, u32[]{:S(2)}) collective-permute-start(bf16[256,1152]{1,0:T(8,128)(2,1)S(1)} %slice.52.refs_1_), channel_id=1, source_target_pairs={{0,4},{4,8},{8,12},{12,0},{1,5},{5,9},{9,13},{13,1},{2,6},{6,10},{... | collective-permute-start | bytes 1769480 | tf_op jit(solution)/shard_map/ppermute | solution.py:320
  9.8 20.5 %collective-permute-start.5 = (bf16[256,1152]{1,0:T(8,128)(2,1)S(1)}, bf16[256,1152]{1,0:T(8,128)(2,1)S(1)}, u32[]{:S(2)}, u32[]{:S(2)}) collective-permute-start(bf16[256,1152]{1,0:T(8,128)(2,1)S(1)} %slice.52.refs_1_), channel_id=1, source_target_pairs={{0,1},{1,0},{2,3},{3,2},{4,5},{5,4},{6,7},{7,6},{8,9},{9,8},{10,11... | collective-permute-start | bytes 1769480 | tf_op jit(solution)/shard_map/ppermute | solution.py:260
  19.0 11.4 %collective-permute-start.7 = (bf16[576,384]{1,0:T(8,128)(2,1)}, bf16[576,384]{1,0:T(8,128)(2,1)}, u32[]{:S(2)}, u32[]{:S(2)}) collective-permute-start(bf16[576,384]{1,0:T(8,128)(2,1)} %get-tuple-element.34.refs_0_), channel_id=1, source_target_pairs={{0,16},{16,0},{1,17},{17,1},{2,18},{18,2},{3,19},{19,3},{4,20},{20... | collective-permute-start | bytes 1327112 | tf_op jit(solution)/shard_map/ppermute | solution.py:283
  20.5 10.9 %collective-permute-start.6 = (bf16[576,384]{1,0:T(8,128)(2,1)}, bf16[576,384]{1,0:T(8,128)(2,1)}, u32[]{:S(2)}, u32[]{:S(2)}) collective-permute-start(bf16[576,384]{1,0:T(8,128)(2,1)} %get-tuple-element.33), channel_id=1, source_target_pairs={{2,0},{0,2},{3,1},{1,3},{6,4},{4,6},{7,5},{5,7},{10,8},{8,10},{11,... | collective-permute-start | bytes 1327112 | tf_op jit(solution)/shard_map/ppermute | solution.py:277
  22.8 16.6 %collective-permute-start.8 = (bf16[256,896]{1,0:T(8,128)(2,1)}, bf16[256,896]{1,0:T(8,128)(2,1)}, u32[]{:S(2)}, u32[]{:S(2)}) collective-permute-start(bf16[256,896]{1,0:T(8,128)(2,1)} %get-tuple-element.36.refs_4_), channel_id=1, source_target_pairs={{0,4},{4,8},{8,12},{12,0},{1,5},{5,9},{9,13},{13,1},{2,6},{6,10},{... | collective-permute-start | bytes 1376264 | tf_op jit(solution)/shard_map/ppermute | solution.py:320
  30.3 10.9 %collective-permute-start.9 = (bf16[256,896]{1,0:T(8,128)(2,1)}, bf16[256,896]{1,0:T(8,128)(2,1)S(1)}, u32[]{:S(2)}, u32[]{:S(2)}) collective-permute-start(bf16[256,896]{1,0:T(8,128)(2,1)} %get-tuple-element.36.refs_4_), channel_id=1, source_target_pairs={{0,1},{1,0},{2,3},{3,2},{4,5},{5,4},{6,7},{7,6},{8,9},{9,8},{10,11... | collective-permute-start | bytes 1376264 | tf_op jit(solution)/shard_map/ppermute | solution.py:338
  30.3 1.1 %copy-start.5 = (bf16[256,1152]{1,0:T(8,128)(2,1)}, bf16[256,1152]{1,0:T(8,128)(2,1)S(1)}, u32[]{:S(2)}) copy-start(bf16[256,1152]{1,0:T(8,128)(2,1)S(1)} %collective-permute-done.5.refs_3_) | copy-start | bytes 1769476
  31.4 13.0 %collective-permute-start.11 = (bf16[576,384]{1,0:T(8,128)(2,1)}, bf16[576,384]{1,0:T(8,128)(2,1)S(1)}, u32[]{:S(2)}, u32[]{:S(2)}) collective-permute-start(bf16[576,384]{1,0:T(8,128)(2,1)} %get-tuple-element.38.refs_1_), channel_id=1, source_target_pairs={{0,16},{16,0},{1,17},{17,1},{2,18},{18,2},{3,19},{19,3},{4,20},{20... | collective-permute-start | bytes 1327112 | tf_op jit(solution)/shard_map/ppermute | solution.py:283
  33.1 11.2 %collective-permute-start.10 = (bf16[512,384]{1,0:T(8,128)(2,1)}, bf16[512,384]{1,0:T(8,128)(2,1)S(1)}, u32[]{:S(2)}, u32[]{:S(2)}) collective-permute-start(bf16[512,384]{1,0:T(8,128)(2,1)} %get-tuple-element.37), channel_id=1, source_target_pairs={{2,0},{0,2},{3,1},{1,3},{6,4},{4,6},{7,5},{5,7},{10,8},{8,10},{11,... | collective-permute-start | bytes 1179656 | tf_op jit(solution)/shard_map/ppermute | solution.py:277
  35.0 1.3 %collective-permute-start = (f32[32,256]{1,0:T(8,128)S(1)}, f32[32,256]{1,0:T(8,128)S(1)}, u32[]{:S(2)}, u32[]{:S(2)}) collective-permute-start(f32[32,256]{1,0:T(8,128)S(1)} %fusion.grad_mine), channel_id=1, source_target_pairs={{0,1},{1,0},{2,3},{3,2},{4,5},{5,4},{6,7},{7,6},{8,9},{9,8},{10,11... | collective-permute-start | bytes 98312 | tf_op jit(solution)/shard_map/ppermute | solution.py:252
  36.3 18.2 %collective-permute-start.12 = (bf16[256,1152]{1,0:T(8,128)(2,1)}, bf16[256,1152]{1,0:T(8,128)(2,1)S(1)}, u32[]{:S(2)}, u32[]{:S(2)}) collective-permute-start(bf16[256,1152]{1,0:T(8,128)(2,1)} %get-tuple-element.40.refs_5_), channel_id=1, source_target_pairs={{0,4},{4,8},{8,12},{12,0},{1,5},{5,9},{9,13},{13,1},{2,6},{6,10},{... | collective-permute-start | bytes 1769480 | tf_op jit(solution)/shard_map/ppermute | solution.py:320
  39.4 15.1 %collective-permute-start.13 = (bf16[256,1152]{1,0:T(8,128)(2,1)}, bf16[256,1152]{1,0:T(8,128)(2,1)S(1)}, u32[]{:S(2)}, u32[]{:S(2)}) collective-permute-start(bf16[256,1152]{1,0:T(8,128)(2,1)} %get-tuple-element.40.refs_5_), channel_id=1, source_target_pairs={{0,1},{1,0},{2,3},{3,2},{4,5},{5,4},{6,7},{7,6},{8,9},{9,8},{10,11... | collective-permute-start | bytes 1769480 | tf_op jit(solution)/shard_map/ppermute | solution.py:338
  41.3 3.1 %copy-start.9 = (bf16[256,896]{1,0:T(8,128)(2,1)}, bf16[256,896]{1,0:T(8,128)(2,1)S(1)}, u32[]{:S(2)}) copy-start(bf16[256,896]{1,0:T(8,128)(2,1)S(1)} %collective-permute-done.9.refs_2_) | copy-start | bytes 1376260
  45.3 10.5 %collective-permute-start.15 = (bf16[512,384]{1,0:T(8,128)(2,1)}, bf16[512,384]{1,0:T(8,128)(2,1)}, u32[]{:S(2)}, u32[]{:S(2)}) collective-permute-start(bf16[512,384]{1,0:T(8,128)(2,1)} %get-tuple-element.42.refs_2_), channel_id=1, source_target_pairs={{0,16},{16,0},{1,17},{17,1},{2,18},{18,2},{3,19},{19,3},{4,20},{20... | collective-permute-start | bytes 1179656 | tf_op jit(solution)/shard_map/ppermute | solution.py:283
  46.5 8.4 %collective-permute-start.14 = (bf16[384,384]{1,0:T(8,128)(2,1)}, bf16[384,384]{1,0:T(8,128)(2,1)}, u32[]{:S(2)}, u32[]{:S(2)}) collective-permute-start(bf16[384,384]{1,0:T(8,128)(2,1)} %get-tuple-element.41), channel_id=1, source_target_pairs={{2,0},{0,2},{3,1},{1,3},{6,4},{4,6},{7,5},{5,7},{10,8},{8,10},{11,... | collective-permute-start | bytes 884744 | tf_op jit(solution)/shard_map/ppermute | solution.py:277
  48.0 17.1 %collective-permute-start.16 = (bf16[256,896]{1,0:T(8,128)(2,1)}, bf16[256,896]{1,0:T(8,128)(2,1)}, u32[]{:S(2)}, u32[]{:S(2)}) collective-permute-start(bf16[256,896]{1,0:T(8,128)(2,1)} %get-tuple-element.44.refs_0_), channel_id=1, source_target_pairs={{0,4},{4,8},{8,12},{12,0},{1,5},{5,9},{9,13},{13,1},{2,6},{6,10},{... | collective-permute-start | bytes 1376264 | tf_op jit(solution)/shard_map/ppermute | solution.py:320
  54.5 1.3 %copy-start.13 = (bf16[256,1152]{1,0:T(8,128)(2,1)}, bf16[256,1152]{1,0:T(8,128)(2,1)S(1)}, u32[]{:S(2)}) copy-start(bf16[256,1152]{1,0:T(8,128)(2,1)S(1)} %collective-permute-done.12.refs_1_) | copy-start | bytes 1769476
  54.5 10.6 %collective-permute-start.17 = (bf16[256,896]{1,0:T(8,128)(2,1)}, bf16[256,896]{1,0:T(8,128)(2,1)S(1)}, u32[]{:S(2)}, u32[]{:S(2)}) collective-permute-start(bf16[256,896]{1,0:T(8,128)(2,1)} %get-tuple-element.44.refs_0_), channel_id=1, source_target_pairs={{0,1},{1,0},{2,3},{3,2},{4,5},{5,4},{6,7},{7,6},{8,9},{9,8},{10,11... | collective-permute-start | bytes 1376264 | tf_op jit(solution)/shard_map/ppermute | solution.py:338
  54.5 1.3 %copy-start.1 = (bf16[256,1152]{1,0:T(8,128)(2,1)}, bf16[256,1152]{1,0:T(8,128)(2,1)S(1)}, u32[]{:S(2)}) copy-start(bf16[256,1152]{1,0:T(8,128)(2,1)S(1)} %collective-permute-done.13.refs_2_) | copy-start | bytes 1769476
  55.8 15.0 %collective-permute-start.21 = (bf16[256,1152]{1,0:T(8,128)(2,1)}, bf16[256,1152]{1,0:T(8,128)(2,1)S(1)}, u32[]{:S(2)}, u32[]{:S(2)}) collective-permute-start(bf16[256,1152]{1,0:T(8,128)(2,1)} %get-tuple-element.54.refs_1_), channel_id=1, source_target_pairs={{0,1},{1,0},{2,3},{3,2},{4,5},{5,4},{6,7},{7,6},{8,9},{9,8},{10,11... | collective-permute-start | bytes 1769480 | tf_op jit(solution)/shard_map/ppermute | solution.py:338
  55.8 20.3 %collective-permute-start.19 = (bf16[256,1152]{1,0:T(8,128)(2,1)}, bf16[256,1152]{1,0:T(8,128)(2,1)S(1)}, u32[]{:S(2)}, u32[]{:S(2)}) collective-permute-start(bf16[256,1152]{1,0:T(8,128)(2,1)} %get-tuple-element.54.refs_1_), channel_id=1, source_target_pairs={{0,4},{4,8},{8,12},{12,0},{1,5},{5,9},{9,13},{13,1},{2,6},{6,10},{... | collective-permute-start | bytes 1769480 | tf_op jit(solution)/shard_map/ppermute | solution.py:320
  55.8 9.6 %collective-permute-start.18 = (bf16[384,384]{1,0:T(8,128)(2,1)}, bf16[384,384]{1,0:T(8,128)(2,1)S(1)}, u32[]{:S(2)}, u32[]{:S(2)}) collective-permute-start(bf16[384,384]{1,0:T(8,128)(2,1)} %get-tuple-element.45.refs_0_), channel_id=1, source_target_pairs={{0,16},{16,0},{1,17},{17,1},{2,18},{18,2},{3,19},{19,3},{4,20},{20... | collective-permute-start | bytes 884744 | tf_op jit(solution)/shard_map/ppermute | solution.py:283
  57.5 3.4 %copy-start.2 = (bf16[256,1152]{1,0:T(8,128)(2,1)S(1)}, bf16[256,1152]{1,0:T(8,128)(2,1)}, u32[]{:S(2)}) copy-start(bf16[256,1152]{1,0:T(8,128)(2,1)} %get-tuple-element.49.refs_7_) | copy-start | bytes 1769476
  57.5 3.4 %copy-start.4 = (bf16[256,1152]{1,0:T(8,128)(2,1)S(1)}, bf16[256,1152]{1,0:T(8,128)(2,1)}, u32[]{:S(2)}) copy-start(bf16[256,1152]{1,0:T(8,128)(2,1)} %get-tuple-element.40.refs_5_) | copy-start | bytes 1769476
  57.5 3.4 %copy-start.6 = (bf16[256,1152]{1,0:T(8,128)(2,1)S(1)}, bf16[256,1152]{1,0:T(8,128)(2,1)}, u32[]{:S(2)}) copy-start(bf16[256,1152]{1,0:T(8,128)(2,1)} %get-tuple-element.47.refs_3_) | copy-start | bytes 1769476
  57.5 3.4 %copy-start.8 = (bf16[256,896]{1,0:T(8,128)(2,1)S(1)}, bf16[256,896]{1,0:T(8,128)(2,1)}, u32[]{:S(2)}) copy-start(bf16[256,896]{1,0:T(8,128)(2,1)} %copy-done.7) | copy-start | bytes 1376260
  57.5 3.4 %copy-start.10 = (bf16[256,896]{1,0:T(8,128)(2,1)S(1)}, bf16[256,896]{1,0:T(8,128)(2,1)}, u32[]{:S(2)}) copy-start(bf16[256,896]{1,0:T(8,128)(2,1)} %get-tuple-element.48.refs_6_) | copy-start | bytes 1376260
  57.5 3.4 %copy-start.12 = (bf16[256,896]{1,0:T(8,128)(2,1)S(1)}, bf16[256,896]{1,0:T(8,128)(2,1)}, u32[]{:S(2)}) copy-start(bf16[256,896]{1,0:T(8,128)(2,1)} %get-tuple-element.46.refs_2_) | copy-start | bytes 1376260
  61.0 4.4 %copy-start.17 = (f32[8,128]{1,0:T(8,128)S(1)}, f32[8,128]{1,0:T(8,128)}, u32[]{:S(2)}) copy-start(f32[8,128]{1,0:T(8,128)} %get-tuple-element.43.refs_0_) | copy-start | bytes 12292
  66.1 1.8 %copy-start.16 = (bf16[32,384]{1,0:T(8,128)(2,1)S(1)}, bf16[32,384]{1,0:T(8,128)(2,1)}, u32[]{:S(2)}) copy-start(bf16[32,384]{1,0:T(8,128)(2,1)} %refs_3_.1) | copy-start | bytes 73732
  68.0 2.9 %copy-start.14 = (bf16[256,1152]{1,0:T(8,128)(2,1)S(1)}, bf16[256,1152]{1,0:T(8,128)(2,1)}, u32[]{:S(2)}) copy-start(bf16[256,1152]{1,0:T(8,128)(2,1)} %get-tuple-element.54.refs_1_) | copy-start | bytes 1769476
  69.5 1.3 %collective-permute-start.20 = (f32[2,32,256]{2,1,0:T(8,128)S(1)}, f32[2,32,256]{2,1,0:T(8,128)S(1)}, u32[]{:S(2)}, u32[]{:S(2)}) collective-permute-start(f32[2,32,256]{2,1,0:T(8,128)S(1)} %shards.4), channel_id=1, source_target_pairs={{0,1},{1,0},{2,3},{3,2},{4,5},{5,4},{6,7},{7,6},{8,9},{9,8},{10,11... | collective-permute-start | bytes 196616 | tf_op jit(solution)/shard_map/ppermute | solution.py:361
  76.2 4.8 %collective-permute-start.22 = (bf16[256,1152]{1,0:T(8,128)(2,1)S(1)}, bf16[256,1152]{1,0:T(8,128)(2,1)S(1)}, u32[]{:S(2)}, u32[]{:S(2)}) collective-permute-start(bf16[256,1152]{1,0:T(8,128)(2,1)S(1)} %get-tuple-element.57.mine), channel_id=1, source_target_pairs={{0,1},{1,0},{2,3},{3,2},{4,5},{5,4},{6,7},{7,6},{8,9},{9,8},{10,11... | collective-permute-start | bytes 1769480 | tf_op jit(solution)/shard_map/ppermute | solution.py:370
  76.2 2.7 %collective-permute-start.23 = (bf16[256,896]{1,0:T(8,128)(2,1)}, bf16[256,896]{1,0:T(8,128)(2,1)S(1)}, u32[]{:S(2)}, u32[]{:S(2)}) collective-permute-start(bf16[256,896]{1,0:T(8,128)(2,1)} %get-tuple-element.58.mine), channel_id=1, source_target_pairs={{0,1},{1,0},{2,3},{3,2},{4,5},{5,4},{6,7},{7,6},{8,9},{9,8},{10,11... | collective-permute-start | bytes 1376264 | tf_op jit(solution)/shard_map/ppermute | solution.py:370
  76.7 5.9 %collective-permute-start.27 = (f32[1,32,256]{2,1,0:T(8,128)S(1)}, f32[1,32,256]{2,1,0:T(8,128)S(1)}, u32[]{:S(2)}, u32[]{:S(2)}) collective-permute-start(f32[1,32,256]{2,1,0:T(8,128)S(1)} %shards.5), channel_id=1, source_target_pairs={{0,1},{1,0},{2,3},{3,2},{4,5},{5,4},{6,7},{7,6},{8,9},{9,8},{10,11... | collective-permute-start | bytes 98312 | tf_op jit(solution)/shard_map/ppermute | solution.py:361
  76.7 8.5 %collective-permute-start.26 = (f32[32,256]{1,0:T(8,128)S(1)}, f32[32,256]{1,0:T(8,128)S(1)}, u32[]{:S(2)}, u32[]{:S(2)}) collective-permute-start(f32[32,256]{1,0:T(8,128)S(1)} %get-tuple-element.61), channel_id=1, source_target_pairs={{0,12},{4,0},{8,4},{12,8},{1,13},{5,1},{9,5},{13,9},{2,14},{6,2},{... | collective-permute-start | bytes 98312 | tf_op jit(solution)/shard_map/ppermute | solution.py:364
  80.9 6.5 %copy-start.18 = (s32[256,2]{0,1:T(2,128)S(1)}, s32[256,2]{0,1:T(2,128)}, u32[]{:S(2)}) copy-start(s32[256,2]{0,1:T(2,128)} %param.10) | copy-start | bytes 6148
  80.9 6.5 %copy-start.19 = (s32[1,256]{1,0:T(1,128)S(1)}, s32[1,256]{1,0:T(1,128)}, u32[]{:S(2)}) copy-start(s32[1,256]{1,0:T(1,128)} %docs.3) | copy-start | bytes 3076
  82.3 1.2 %collective-permute-start.24 = (f32[32,256]{1,0:T(8,128)S(1)}, f32[32,256]{1,0:T(8,128)S(1)}, u32[]{:S(2)}, u32[]{:S(2)}) collective-permute-start(f32[32,256]{1,0:T(8,128)S(1)} %part.3), channel_id=1, source_target_pairs={{0,1},{1,0},{2,3},{3,2},{4,5},{5,4},{6,7},{7,6},{8,9},{9,8},{10,11... | collective-permute-start | bytes 98312 | tf_op jit(solution)/shard_map/ppermute | solution.py:379
  82.6 4.9 %collective-permute-start.28 = (f32[32,256]{1,0:T(8,128)S(1)}, f32[32,256]{1,0:T(8,128)S(1)}, u32[]{:S(2)}, u32[]{:S(2)}) collective-permute-start(f32[32,256]{1,0:T(8,128)S(1)} %add_bitcast_fusion), channel_id=1, source_target_pairs={{0,8},{4,12},{8,0},{12,4},{1,9},{5,13},{9,1},{13,5},{2,10},{6,14},... | collective-permute-start | bytes 98312 | tf_op jit(solution)/shard_map/ppermute | solution.py:364
  83.6 5.7 %collective-permute-start.25 = (f32[32,256]{1,0:T(8,128)S(1)}, f32[32,256]{1,0:T(8,128)S(1)}, u32[]{:S(2)}, u32[]{:S(2)}) collective-permute-start(f32[32,256]{1,0:T(8,128)S(1)} %add.10), channel_id=1, source_target_pairs={{0,4},{4,8},{8,12},{12,0},{1,5},{5,9},{9,13},{13,1},{2,6},{6,10},{... | collective-permute-start | bytes 98312 | tf_op jit(solution)/shard_map/ppermute | solution.py:380
  (6 other events, 5.0 us)
